TPU v7x, 32 devices: a whole 2x2x4 slice. The times are simulated.
32 devices in a mesh: stretch: 2 (over x), cp: 4 (over z), tp: 4 (over y, core).
Axes of the slice: x: 2, y: 2, z: 4, core: 2. Of those that a mesh axis runs over, the one named last changes fastest.
Arguments:
- query_rows: bfloat16 [4, 512, 6144], P('stretch', 'cp', 'tp'), may hold values from -56 to 56
- key_rows: bfloat16 [4, 512, 6144], P('stretch', 'cp', 'tp'), may hold values from -4 to 4
- value_rows: bfloat16 [4, 512, 6144], P('stretch', 'cp', 'tp'), may hold values from -208 to 208
- gate_table: bfloat16 [16, 6144], P(None, 'tp'), may hold values from 0.5 to 2
- levels: int32 [4], replicated, may hold values from 0 to 15, as said below
- kv_ranges: int32 [2, 4, 4, 4], replicated, may hold values from 0 to 4, as said below
Outputs:
- attention_out: bfloat16 [4, 512, 6144], P('stretch', 'cp', 'tp')
Inputs may be any that keep to these rules, and one draw needn't show every extreme that they name: levels[c] lies in [c * 4, (c + 1) * 4), so later stretches are noisier. Write q for a query block, p = 1 and w = [max(0, (q // p - 2) * p), (q // p + 1) * p). Every range has kv_ranges[0] <= kv_ranges[1]. For key stretch c2 > c the range is empty (both 0). For c2 == c it contains block q and lies within w. For c2 < c it is empty (both 0) or lies within w; for c2 == c - 1 it is never empty.
All inputs are finite; a program needn't handle non-finite values.
Results may differ from a plain program's by a relative error of at most 0.0039.
Values may be sent and summed in bfloat16 or wider, within the bound.
No kernel may reach another device: no remote copies, remote signals or barrier semaphores. Data moves between devices by JAX's collectives and lax.ppermute only.
A program may use at most 64 MiB of HBM per device.

v0:
```python
import functools
import math

import jax
import jax.numpy as jnp
from jax import lax
from jax.experimental import pallas as pl
from jax.experimental.pallas import tpu as pltpu
from jax.sharding import PartitionSpec as P

HEADS = 48
HEAD_DIM = 128
BLOCK = 128
REACH = 2
CHUNKS = (3, 3, 3, 3)
STAT_ROWS = 16
HIDDEN = -1e30
EXPONENT_SCALE = math.log2(math.e) / math.sqrt(HEAD_DIM)


def moved(block, axis, distance):
    devices = range(lax.axis_size(axis))
    route = [(i - distance, i) for i in devices if i - distance in devices]
    return lax.ppermute(block, axis, route)


def head_columns(head):
    return slice(head * HEAD_DIM, (head + 1) * HEAD_DIM)


def stretch_rows(slot):
    return slice(slot * BLOCK, (slot + 1) * BLOCK)


def as_rows(columns):
    return jnp.transpose(columns)[:STAT_ROWS]


def as_columns(rows):
    fill = jnp.zeros((BLOCK - rows.shape[0], BLOCK), jnp.float32)
    return jnp.transpose(jnp.concatenate([rows, fill], axis=0))


def put_stats(payload_ref, stats, token_rows):
    high = stats.astype(jnp.bfloat16)
    rest = stats - high.astype(jnp.float32)
    middle = rest.astype(jnp.bfloat16)
    low = (rest - middle.astype(jnp.float32)).astype(jnp.bfloat16)
    rows = slice(token_rows, token_rows + STAT_ROWS)
    for index, piece in enumerate((high, middle, low)):
        payload_ref[rows, head_columns(index)] = piece


def get_stats(payload_ref, token_rows):
    rows = slice(token_rows, token_rows + STAT_ROWS)
    pieces = [
        payload_ref[rows, head_columns(index)].astype(jnp.float32) for index in range(3)
    ]
    return (pieces[0] + pieces[1]) + pieces[2]


def attend_kernel(
    head_count,
    place_ref,
    ranges_ref,
    own_q,
    near_q,
    far_q,
    own_kv,
    prior_kv,
    own_out,
    own_stats,
    near_out,
    near_stats,
    far_payload,
):
    group, position, stretch_count, block_count = (place_ref[i] for i in range(4))
    pair_count = own_q.shape[0] // BLOCK
    token_rows = pair_count * BLOCK
    value_base = head_count * HEAD_DIM
    high_base = stretch_count * block_count * stretch_count

    def hidden_bias(query_stretch, query_block, key_stretch):
        valid = (key_stretch >= 0) & (query_block < block_count)
        entry = (
            query_stretch * block_count + jnp.minimum(query_block, block_count - 1)
        ) * stretch_count + jnp.maximum(key_stretch, 0)
        visible = (
            valid
            & (ranges_ref[entry] <= position)
            & (position < ranges_ref[high_base + entry])
        )
        return jnp.where(visible, 0.0, HIDDEN)

    lane = lax.broadcasted_iota(jnp.int32, (BLOCK, BLOCK), 1)
    stats = [jnp.zeros((BLOCK, BLOCK), jnp.float32) for _ in range(REACH + 1)]
    biases = {
        (distance, slot): [
            hidden_bias(
                group * pair_count + slot,
                position + distance,
                (group - 1) * pair_count + key_slot,
            )
            for key_slot in range(2 * pair_count)
        ]
        for distance in range(REACH + 1)
        for slot in range(pair_count)
    }
    for head in range(head_count):
        columns = head_columns(head)
        value_columns = slice(value_base + columns.start, value_base + columns.stop)
        keys = jnp.concatenate([prior_kv[:, columns], own_kv[:, columns]], axis=0)
        values = jnp.concatenate(
            [prior_kv[:, value_columns], own_kv[:, value_columns]], axis=0
        )
        for distance, query_ref in ((2, far_q), (1, near_q), (0, own_q)):
            for slot in range(pair_count):
                rows = stretch_rows(slot)
                scores = lax.dot_general(
                    query_ref[rows, columns],
                    keys,
                    (((1,), (1,)), ((), ())),
                    preferred_element_type=jnp.float32,
                )
                scores = jnp.concatenate(
                    [
                        scores[:, stretch_rows(key_slot)] + bias
                        for key_slot, bias in enumerate(biases[distance, slot])
                    ],
                    axis=1,
                )
                peak = jnp.max(scores, axis=1, keepdims=True)
                weight = jnp.exp2((scores - peak) * EXPONENT_SCALE)
                total = jnp.sum(weight, axis=1, keepdims=True)
                summed = jnp.dot(
                    weight.astype(jnp.bfloat16), values, preferred_element_type=jnp.float32
                )
                attended = summed * (1.0 / total)
                log_total = peak * EXPONENT_SCALE + jnp.log2(total)
                stats[distance] = jnp.where(
                    lane == slot * head_count + head, log_total, stats[distance]
                )
                if distance == 0:
                    own_out[rows, columns] = attended
                elif distance == 1:
                    near_out[rows, columns] = attended
                else:
                    far_payload[rows, columns] = attended.astype(jnp.bfloat16)
    own_stats[...] = as_rows(stats[0])
    near_stats[...] = as_rows(stats[1])
    put_stats(far_payload, as_rows(stats[2]), token_rows)


def joined(place_ref, local_out, local_stats, payload_ref, head_count):
    token_rows = local_out.shape[0]
    local_log = local_stats[...]
    remote_log = jnp.where(place_ref[1] > 0, get_stats(payload_ref, token_rows), HIDDEN)
    top = jnp.maximum(local_log, remote_log)
    local_weight = jnp.exp2(local_log - top)
    remote_weight = jnp.exp2(remote_log - top)
    both = local_weight + remote_weight
    scale = 1.0 / both
    columns_of = as_columns(
        jnp.concatenate([local_weight * scale, remote_weight * scale], axis=0)
    )
    parts = {}
    for slot in range(token_rows // BLOCK):
        for head in range(head_count):
            index = slot * head_count + head
            rows, columns = stretch_rows(slot), head_columns(head)
            parts[slot, head] = local_out[rows, columns] * columns_of[
                :, index : index + 1
            ] + payload_ref[rows, columns].astype(jnp.float32) * columns_of[
                :, STAT_ROWS + index : STAT_ROWS + index + 1
            ]
    return parts, top + jnp.log2(both)


def relay_kernel(head_count, place_ref, local_out, local_stats, payload_in, payload_out):
    parts, log_total = joined(place_ref, local_out, local_stats, payload_in, head_count)
    for (slot, head), part in parts.items():
        payload_out[stretch_rows(slot), head_columns(head)] = part.astype(jnp.bfloat16)
    put_stats(payload_out, log_total, local_out.shape[0])


def finish_kernel(
    head_count, place_ref, local_out, local_stats, payload_in, squares_in, out, squares_out
):
    parts, _ = joined(place_ref, local_out, local_stats, payload_in, head_count)
    lane = lax.broadcasted_iota(jnp.int32, (BLOCK, BLOCK), 1)
    squares = jnp.zeros((BLOCK, BLOCK), jnp.float32)
    for slot in range(local_out.shape[0] // BLOCK):
        total = jnp.zeros((BLOCK, HEAD_DIM), jnp.float32)
        for head in range(head_count):
            part = parts[slot, head]
            out[stretch_rows(slot), head_columns(head)] = part
            total = total + part * part
        total = jnp.sum(total, axis=1, keepdims=True)
        squares = jnp.where(lane == slot, total, squares)
    squares_out[...] = squares_in[...] + jnp.transpose(squares)[: squares_out.shape[0]]


def scale_kernel(head_counts, feature_count, place_ref, levels_ref, squares, gate_table, *refs):
    parts, out = refs[:-1], refs[-1]
    factors = as_columns(lax.rsqrt(squares[...] / feature_count + 1e-06))
    pair_count = out.shape[0] // BLOCK
    gates = gate_table[...].astype(jnp.float32)
    level_ids = lax.broadcasted_iota(jnp.int32, gates.shape, 0)
    for slot in range(pair_count):
        level = levels_ref[place_ref[0] * pair_count + slot]
        gate_row = jnp.sum(jnp.where(level_ids == level, gates, 0.0), axis=0, keepdims=True)
        rows = stretch_rows(slot)
        factor = factors[:, slot : slot + 1]
        base = 0
        for part, head_count in zip(parts, head_counts):
            for head in range(head_count):
                columns = head_columns(base + head)
                out[rows, columns] = (
                    part[rows, head_columns(head)] * factor * gate_row[:, columns]
                ).astype(jnp.bfloat16)
            base += head_count


SMEM = pl.BlockSpec(memory_space=pltpu.SMEM)
VMEM = pl.BlockSpec(memory_space=pltpu.VMEM)
PARAMS = pltpu.CompilerParams(vmem_limit_bytes=32 * 1024 * 1024)


def on_device(query_rows, key_rows, value_rows, gate_table, levels, kv_ranges):
    pair_count, row_count, width_dev = query_rows.shape
    assert row_count == BLOCK
    token_rows = pair_count * row_count
    head_total = width_dev // HEAD_DIM
    group = lax.axis_index("stretch")
    position = lax.axis_index("cp")
    place = jnp.stack(
        [group, position, jnp.int32(kv_ranges.shape[1]), jnp.int32(kv_ranges.shape[2])]
    ).astype(jnp.int32)
    ranges = kv_ranges.reshape(-1)
    queries, keys, values = (
        array.reshape(token_rows, width_dev) for array in (query_rows, key_rows, value_rows)
    )
    head_counts = CHUNKS
    assert sum(head_counts) == head_total
    starts = [sum(head_counts[:i]) * HEAD_DIM for i in range(len(head_counts))]
    widths = [count * HEAD_DIM for count in head_counts]
    chunks = range(len(head_counts))

    def cut(array, chunk):
        return lax.slice_in_dim(array, starts[chunk], starts[chunk] + widths[chunk], axis=1)

    own_q = [cut(queries, i) for i in chunks]
    own_kv = [jnp.concatenate([cut(keys, i), cut(values, i)], axis=1) for i in chunks]
    near_q = [moved(own_q[i], "cp", -1) for i in chunks]
    prior_kv = [moved(own_kv[i], "stretch", 1) for i in chunks]
    far_q = [moved(near_q[i], "cp", -1) for i in chunks]

    def stats_shape():
        return jax.ShapeDtypeStruct((STAT_ROWS, BLOCK), jnp.float32)

    squares = jnp.zeros((8, BLOCK), jnp.float32)
    finished = []
    for i in chunks:
        head_count, width = head_counts[i], widths[i]
        float_shape = jax.ShapeDtypeStruct((token_rows, width), jnp.float32)
        payload_shape = jax.ShapeDtypeStruct((token_rows + STAT_ROWS, width), jnp.bfloat16)
        own_out, own_stats, near_out, near_stats, far_payload = pl.pallas_call(
            functools.partial(attend_kernel, head_count),
            out_shape=(float_shape, stats_shape(), float_shape, stats_shape(), payload_shape),
            in_specs=[SMEM, SMEM] + [VMEM] * 5,
            out_specs=(VMEM,) * 5,
            compiler_params=PARAMS,
        )(place, ranges, own_q[i], near_q[i], far_q[i], own_kv[i], prior_kv[i])
        arrived = moved(far_payload, "cp", 1)
        relayed = pl.pallas_call(
            functools.partial(relay_kernel, head_count),
            out_shape=payload_shape,
            in_specs=[SMEM] + [VMEM] * 3,
            out_specs=VMEM,
            compiler_params=PARAMS,
        )(place, near_out, near_stats, arrived)
        arrived = moved(relayed, "cp", 1)
        part, squares = pl.pallas_call(
            functools.partial(finish_kernel, head_count),
            out_shape=(float_shape, jax.ShapeDtypeStruct(squares.shape, jnp.float32)),
            in_specs=[SMEM] + [VMEM] * 4,
            out_specs=(VMEM, VMEM),
            compiler_params=PARAMS,
        )(place, own_out, own_stats, arrived, squares)
        finished.append(part)
    squares = lax.psum(squares, "tp")
    out = pl.pallas_call(
        functools.partial(scale_kernel, head_counts, float(HEADS * HEAD_DIM)),
        out_shape=jax.ShapeDtypeStruct((token_rows, width_dev), jnp.bfloat16),
        in_specs=[SMEM, SMEM] + [VMEM] * (2 + len(finished)),
        out_specs=VMEM,
        compiler_params=PARAMS,
    )(place, levels, squares, gate_table, *finished)
    return out.reshape(query_rows.shape)


def solution(mesh):
    in_specs = (
        P("stretch", "cp", "tp"),
        P("stretch", "cp", "tp"),
        P("stretch", "cp", "tp"),
        P(None, "tp"),
        P(),
        P(),
    )
    out_specs = P("stretch", "cp", "tp")
    return jax.shard_map(
        on_device, mesh=mesh, in_specs=in_specs, out_specs=out_specs, check_vma=False
    )
```

profile of v0, /device:TPU:0, one launch (start us, length us, event | category | flops | bytes accessed | tf_op | source)
XLA Modules:
  0.0 106.7 jit_solution(5727149463636684668)
XLA Ops:
  0.0 1.4 %fusion.2 = (bf16[256,384]{1,0:T(8,128)(2,1)S(1)}, bf16[256,384]{1,0:T(8,128)(2,1)S(1)}, bf16[256,384]{1,0:T(8,128)(2,1)S(1)}, bf16[256,384]{1,0:T(8,128)(2,1)S(1)}) fusion(bf16[256,1536]{1,0:T(8,128)(2,1)} %bitcast.6), kind=kLoop, calls=%fused_computation.7 | loop fusion | bytes 1572864 | tf_op jit(solution)/shard_map/slice | solution.py:250
  1.4 1.3 %collective-permute-start.15 = (bf16[256,384]{1,0:T(8,128)(2,1)S(1)}, bf16[256,384]{1,0:T(8,128)(2,1)S(1)}, u32[]{:S(2)}, u32[]{:S(2)}) collective-permute-start(bf16[256,384]{1,0:T(8,128)(2,1)S(1)} %get-tuple-element.69.own_q), channel_id=1, source_target_pairs={{4,0},{8,4},{12,8},{5,1},{9,5},{13,9},{6,2},{10,6},{14,10},{7,3},{... | collective-permute-start | bytes 589832 | tf_op jit(solution)/shard_map/ppermute | solution.py:24
  2.7 0.2 fusion
  3.0 4.9 %collective-permute-start.17 = (bf16[256,768]{1,0:T(8,128)(2,1)S(1)}, bf16[256,768]{1,0:T(8,128)(2,1)S(1)}, u32[]{:S(2)}, u32[]{:S(2)}) collective-permute-start(bf16[256,768]{1,0:T(8,128)(2,1)S(1)} %pad_maximum_fusion.3.own_kv), channel_id=1, source_target_pairs={{0,16},{1,17},{2,18},{3,19},{4,20},{5,21},{6,22},{7,23},{8,24},{9,... | collective-permute-start | bytes 1179656 | tf_op jit(solution)/shard_map/ppermute | solution.py:24
  7.8 1.3 %collective-permute-start.10 = (bf16[256,384]{1,0:T(8,128)(2,1)S(1)}, bf16[256,384]{1,0:T(8,128)(2,1)}, u32[]{:S(2)}, u32[]{:S(2)}) collective-permute-start(bf16[256,384]{1,0:T(8,128)(2,1)S(1)} %get-tuple-element.70.own_q), channel_id=1, source_target_pairs={{4,0},{8,4},{12,8},{5,1},{9,5},{13,9},{6,2},{10,6},{14,10},{7,3},{... | collective-permute-start | bytes 589832 | tf_op jit(solution)/shard_map/ppermute | solution.py:24
  9.1 1.3 %collective-permute-start.5 = (bf16[256,384]{1,0:T(8,128)(2,1)S(1)}, bf16[256,384]{1,0:T(8,128)(2,1)}, u32[]{:S(2)}, u32[]{:S(2)}) collective-permute-start(bf16[256,384]{1,0:T(8,128)(2,1)S(1)} %get-tuple-element.71.own_q), channel_id=1, source_target_pairs={{4,0},{8,4},{12,8},{5,1},{9,5},{13,9},{6,2},{10,6},{14,10},{7,3},{... | collective-permute-start | bytes 589832 | tf_op jit(solution)/shard_map/ppermute | solution.py:24
  10.5 1.3 %collective-permute-start.12 = (bf16[256,768]{1,0:T(8,128)(2,1)S(1)}, bf16[256,768]{1,0:T(8,128)(2,1)S(1)}, u32[]{:S(2)}, u32[]{:S(2)}) collective-permute-start(bf16[256,768]{1,0:T(8,128)(2,1)S(1)} %pad_maximum_fusion.2.own_kv), channel_id=1, source_target_pairs={{0,16},{1,17},{2,18},{3,19},{4,20},{5,21},{6,22},{7,23},{8,24},{9,... | collective-permute-start | bytes 1179656 | tf_op jit(solution)/shard_map/ppermute | solution.py:24
  11.8 0.0 collective-permute-done.15.near_q
  11.8 1.3 %collective-permute-start = (bf16[256,384]{1,0:T(8,128)(2,1)S(1)}, bf16[256,384]{1,0:T(8,128)(2,1)}, u32[]{:S(2)}, u32[]{:S(2)}) collective-permute-start(bf16[256,384]{1,0:T(8,128)(2,1)S(1)} %get-tuple-element.72.own_q), channel_id=1, source_target_pairs={{4,0},{8,4},{12,8},{5,1},{9,5},{13,9},{6,2},{10,6},{14,10},{7,3},{... | collective-permute-start | bytes 589832 | tf_op jit(solution)/shard_map/ppermute | solution.py:24
  13.2 5.1 %collective-permute-done.10.near_q = bf16[256,384]{1,0:T(8,128)(2,1)} collective-permute-done((bf16[256,384]{1,0:T(8,128)(2,1)S(1)}, bf16[256,384]{1,0:T(8,128)(2,1)}, u32[]{:S(2)}, u32[]{:S(2)}) %collective-permute-start.10) | collective-permute-done | bytes 196640 | tf_op jit(solution)/shard_map/ppermute | solution.py:24
  18.3 1.5 %collective-permute-start.7 = (bf16[256,768]{1,0:T(8,128)(2,1)S(1)}, bf16[256,768]{1,0:T(8,128)(2,1)S(1)}, u32[]{:S(2)}, u32[]{:S(2)}) collective-permute-start(bf16[256,768]{1,0:T(8,128)(2,1)S(1)} %pad_maximum_fusion.1.own_kv), channel_id=1, source_target_pairs={{0,16},{1,17},{2,18},{3,19},{4,20},{5,21},{6,22},{7,23},{8,24},{9,... | collective-permute-start | bytes 1179656 | tf_op jit(solution)/shard_map/ppermute | solution.py:24
  19.8 2.7 %collective-permute-done.5.near_q = bf16[256,384]{1,0:T(8,128)(2,1)} collective-permute-done((bf16[256,384]{1,0:T(8,128)(2,1)S(1)}, bf16[256,384]{1,0:T(8,128)(2,1)}, u32[]{:S(2)}, u32[]{:S(2)}) %collective-permute-start.5) | collective-permute-done | bytes 196640 | tf_op jit(solution)/shard_map/ppermute | solution.py:24
  22.5 1.3 %collective-permute-start.16 = (bf16[256,384]{1,0:T(8,128)(2,1)S(1)}, bf16[256,384]{1,0:T(8,128)(2,1)S(1)}, u32[]{:S(2)}, u32[]{:S(2)}) collective-permute-start(bf16[256,384]{1,0:T(8,128)(2,1)S(1)} %collective-permute-done.15.near_q), channel_id=1, source_target_pairs={{4,0},{8,4},{12,8},{5,1},{9,5},{13,9},{6,2},{10,6},{14,10},{7,3},{... | collective-permute-start | bytes 589832 | tf_op jit(solution)/shard_map/ppermute | solution.py:24
  23.8 2.3 %collective-permute-done.near_q = bf16[256,384]{1,0:T(8,128)(2,1)} collective-permute-done((bf16[256,384]{1,0:T(8,128)(2,1)S(1)}, bf16[256,384]{1,0:T(8,128)(2,1)}, u32[]{:S(2)}, u32[]{:S(2)}) %collective-permute-start) | collective-permute-done | bytes 196640 | tf_op jit(solution)/shard_map/ppermute | solution.py:24
  26.2 1.5 %collective-permute-start.2 = (bf16[256,768]{1,0:T(8,128)(2,1)S(1)}, bf16[256,768]{1,0:T(8,128)(2,1)S(1)}, u32[]{:S(2)}, u32[]{:S(2)}) collective-permute-start(bf16[256,768]{1,0:T(8,128)(2,1)S(1)} %pad_maximum_fusion.own_kv), channel_id=1, source_target_pairs={{0,16},{1,17},{2,18},{3,19},{4,20},{5,21},{6,22},{7,23},{8,24},{9,... | collective-permute-start | bytes 1179656 | tf_op jit(solution)/shard_map/ppermute | solution.py:24
  27.7 0.0 collective-permute-done.17.prior_kv
  27.7 0.0 copy-start
  27.7 0.7 copy-done
  28.4 1.3 %collective-permute-start.11 = (bf16[256,384]{1,0:T(8,128)(2,1)}, bf16[256,384]{1,0:T(8,128)(2,1)}, u32[]{:S(2)}, u32[]{:S(2)}) collective-permute-start(bf16[256,384]{1,0:T(8,128)(2,1)} %collective-permute-done.10.near_q), channel_id=1, source_target_pairs={{4,0},{8,4},{12,8},{5,1},{9,5},{13,9},{6,2},{10,6},{14,10},{7,3},{... | collective-permute-start | bytes 589832 | tf_op jit(solution)/shard_map/ppermute | solution.py:24
  29.7 0.3 collective-permute-done.16.far_q
  30.1 0.7 copy-done.4
  30.8 1.3 %collective-permute-start.6 = (bf16[256,384]{1,0:T(8,128)(2,1)}, bf16[256,384]{1,0:T(8,128)(2,1)}, u32[]{:S(2)}, u32[]{:S(2)}) collective-permute-start(bf16[256,384]{1,0:T(8,128)(2,1)} %collective-permute-done.5.near_q), channel_id=1, source_target_pairs={{4,0},{8,4},{12,8},{5,1},{9,5},{13,9},{6,2},{10,6},{14,10},{7,3},{... | collective-permute-start | bytes 589832 | tf_op jit(solution)/shard_map/ppermute | solution.py:24
  32.0 0.0 collective-permute-done.12.prior_kv
  32.1 1.3 %collective-permute-start.1 = (bf16[256,384]{1,0:T(8,128)(2,1)}, bf16[256,384]{1,0:T(8,128)(2,1)}, u32[]{:S(2)}, u32[]{:S(2)}) collective-permute-start(bf16[256,384]{1,0:T(8,128)(2,1)} %collective-permute-done.near_q), channel_id=1, source_target_pairs={{4,0},{8,4},{12,8},{5,1},{9,5},{13,9},{6,2},{10,6},{14,10},{7,3},{... | collective-permute-start | bytes 589832 | tf_op jit(solution)/shard_map/ppermute | solution.py:24
  33.4 0.8 reshape.15.ranges_ref
  34.2 0.1 pad_add_fusion.place_ref
  34.3 1.0 copy-done.1
  35.3 0.9 copy-done.3
  36.2 0.9 copy-done.5
  37.1 5.5 %shard_map.70 = (f32[256,384]{1,0:T(8,128)S(1)}, f32[16,128]{1,0:T(8,128)S(1)}, f32[256,384]{1,0:T(8,128)S(1)}, f32[16,128]{1,0:T(8,128)S(1)}, bf16[272,384]{1,0:T(8,128)(2,1)S(1)}) custom-call(s32[4]{0:T(128)S(1)} %pad_add_fusion.place_ref, s32[128]{0:T(128)S(1)} %reshape.15.ranges_ref, bf16[256,384]{1,0:T(8,128)(2,1)S(1)} %get-tuple-element.69.own_q, ...), custom_call_target="tpu_custom_call" | custom-call | tf_op jit(solution)/shard_map/pallas_call | solution.py:267
  42.6 0.0 collective-permute-done.11.far_q
  42.6 5.5 %collective-permute-start.18 = (bf16[272,384]{1,0:T(8,128)(2,1)S(1)}, bf16[272,384]{1,0:T(8,128)(2,1)S(1)}, u32[]{:S(2)}, u32[]{:S(2)}) collective-permute-start(bf16[272,384]{1,0:T(8,128)(2,1)S(1)} %get-tuple-element.52), channel_id=1, source_target_pairs={{0,4},{4,8},{8,12},{1,5},{5,9},{9,13},{2,6},{6,10},{10,14},{3,7},{... | collective-permute-start | bytes 626696 | tf_op jit(solution)/shard_map/ppermute | solution.py:24
  48.1 6.0 %shard_map.68 = (f32[256,384]{1,0:T(8,128)S(1)}, f32[16,128]{1,0:T(8,128)S(1)}, f32[256,384]{1,0:T(8,128)S(1)}, f32[16,128]{1,0:T(8,128)S(1)}, bf16[272,384]{1,0:T(8,128)(2,1)S(1)}) custom-call(s32[4]{0:T(128)S(1)} %pad_add_fusion.place_ref, s32[128]{0:T(128)S(1)} %reshape.15.ranges_ref, bf16[256,384]{1,0:T(8,128)(2,1)S(1)} %get-tuple-element.70.own_q, ...), custom_call_target="tpu_custom_call" | custom-call | tf_op jit(solution)/shard_map/pallas_call | solution.py:267
  54.1 0.0 collective-permute-done.7.prior_kv
  54.1 3.9 %collective-permute-start.13 = (bf16[272,384]{1,0:T(8,128)(2,1)S(1)}, bf16[272,384]{1,0:T(8,128)(2,1)S(1)}, u32[]{:S(2)}, u32[]{:S(2)}) collective-permute-start(bf16[272,384]{1,0:T(8,128)(2,1)S(1)} %get-tuple-element.47), channel_id=1, source_target_pairs={{0,4},{4,8},{8,12},{1,5},{5,9},{9,13},{2,6},{6,10},{10,14},{3,7},{... | collective-permute-start | bytes 626696 | tf_op jit(solution)/shard_map/ppermute | solution.py:24
  58.1 0.0 collective-permute-done.6.far_q
  58.1 6.0 %shard_map.66 = (f32[256,384]{1,0:T(8,128)S(1)}, f32[16,128]{1,0:T(8,128)S(1)}, f32[256,384]{1,0:T(8,128)S(1)}, f32[16,128]{1,0:T(8,128)S(1)}, bf16[272,384]{1,0:T(8,128)(2,1)S(1)}) custom-call(s32[4]{0:T(128)S(1)} %pad_add_fusion.place_ref, s32[128]{0:T(128)S(1)} %reshape.15.ranges_ref, bf16[256,384]{1,0:T(8,128)(2,1)S(1)} %get-tuple-element.71.own_q, ...), custom_call_target="tpu_custom_call" | custom-call | tf_op jit(solution)/shard_map/pallas_call | solution.py:267
  64.1 4.7 %collective-permute-start.8 = (bf16[272,384]{1,0:T(8,128)(2,1)S(1)}, bf16[272,384]{1,0:T(8,128)(2,1)S(1)}, u32[]{:S(2)}, u32[]{:S(2)}) collective-permute-start(bf16[272,384]{1,0:T(8,128)(2,1)S(1)} %get-tuple-element.42), channel_id=1, source_target_pairs={{0,4},{4,8},{8,12},{1,5},{5,9},{9,13},{2,6},{6,10},{10,14},{3,7},{... | collective-permute-start | bytes 626696 | tf_op jit(solution)/shard_map/ppermute | solution.py:24
  68.8 0.0 collective-permute-done.2.prior_kv
  68.8 0.0 collective-permute-done.1.far_q
  68.8 6.0 %shard_map.64 = (f32[256,384]{1,0:T(8,128)S(1)}, f32[16,128]{1,0:T(8,128)S(1)}, f32[256,384]{1,0:T(8,128)S(1)}, f32[16,128]{1,0:T(8,128)S(1)}, bf16[272,384]{1,0:T(8,128)(2,1)S(1)}) custom-call(s32[4]{0:T(128)S(1)} %pad_add_fusion.place_ref, s32[128]{0:T(128)S(1)} %reshape.15.ranges_ref, bf16[256,384]{1,0:T(8,128)(2,1)S(1)} %get-tuple-element.72.own_q, ...), custom_call_target="tpu_custom_call" | custom-call | tf_op jit(solution)/shard_map/pallas_call | solution.py:267
  74.8 1.9 %collective-permute-start.3 = (bf16[272,384]{1,0:T(8,128)(2,1)S(1)}, bf16[272,384]{1,0:T(8,128)(2,1)S(1)}, u32[]{:S(2)}, u32[]{:S(2)}) collective-permute-start(bf16[272,384]{1,0:T(8,128)(2,1)S(1)} %get-tuple-element.37), channel_id=1, source_target_pairs={{0,4},{4,8},{8,12},{1,5},{5,9},{9,13},{2,6},{6,10},{10,14},{3,7},{... | collective-permute-start | bytes 626696 | tf_op jit(solution)/shard_map/ppermute | solution.py:24
  76.8 0.0 collective-permute-done.18.payload_in
  76.8 1.0 shard_map.71
  77.8 1.9 %collective-permute-start.19 = (bf16[272,384]{1,0:T(8,128)(2,1)S(1)}, bf16[272,384]{1,0:T(8,128)(2,1)S(1)}, u32[]{:S(2)}, u32[]{:S(2)}) collective-permute-start(bf16[272,384]{1,0:T(8,128)(2,1)S(1)} %shard_map.71), channel_id=1, source_target_pairs={{0,4},{4,8},{8,12},{1,5},{5,9},{9,13},{2,6},{6,10},{10,14},{3,7},{... | collective-permute-start | bytes 626696 | tf_op jit(solution)/shard_map/ppermute | solution.py:24
  79.7 0.0 collective-permute-done.13.payload_in
  79.7 1.0 shard_map.69
  80.7 1.9 %collective-permute-start.14 = (bf16[272,384]{1,0:T(8,128)(2,1)S(1)}, bf16[272,384]{1,0:T(8,128)(2,1)S(1)}, u32[]{:S(2)}, u32[]{:S(2)}) collective-permute-start(bf16[272,384]{1,0:T(8,128)(2,1)S(1)} %shard_map.69), channel_id=1, source_target_pairs={{0,4},{4,8},{8,12},{1,5},{5,9},{9,13},{2,6},{6,10},{10,14},{3,7},{... | collective-permute-start | bytes 626696 | tf_op jit(solution)/shard_map/ppermute | solution.py:24
  82.6 0.0 collective-permute-done.8.payload_in
  82.6 1.0 shard_map.67
  83.6 1.9 %collective-permute-start.9 = (bf16[272,384]{1,0:T(8,128)(2,1)S(1)}, bf16[272,384]{1,0:T(8,128)(2,1)S(1)}, u32[]{:S(2)}, u32[]{:S(2)}) collective-permute-start(bf16[272,384]{1,0:T(8,128)(2,1)S(1)} %shard_map.67), channel_id=1, source_target_pairs={{0,4},{4,8},{8,12},{1,5},{5,9},{9,13},{2,6},{6,10},{10,14},{3,7},{... | collective-permute-start | bytes 626696 | tf_op jit(solution)/shard_map/ppermute | solution.py:24
  85.5 0.0 collective-permute-done.3.payload_in
  85.5 1.0 shard_map.65
  86.5 1.9 %collective-permute-start.4 = (bf16[272,384]{1,0:T(8,128)(2,1)S(1)}, bf16[272,384]{1,0:T(8,128)(2,1)S(1)}, u32[]{:S(2)}, u32[]{:S(2)}) collective-permute-start(bf16[272,384]{1,0:T(8,128)(2,1)S(1)} %shard_map.65), channel_id=1, source_target_pairs={{0,4},{4,8},{8,12},{1,5},{5,9},{9,13},{2,6},{6,10},{10,14},{3,7},{... | collective-permute-start | bytes 626696 | tf_op jit(solution)/shard_map/ppermute | solution.py:24
  88.4 1.1 %shard_map.72 = (f32[256,384]{1,0:T(8,128)S(1)}, f32[8,128]{1,0:T(8,128)S(1)}) custom-call(s32[4]{0:T(128)S(1)} %pad_add_fusion.place_ref, f32[256,384]{1,0:T(8,128)S(1)} %get-tuple-element.48.local_out, f32[16,128]{1,0:T(8,128)S(1)} %get-tuple-element.49.local_stats, bf16[272,384]{1,0:T(8,128)(2,1)S(1)} %collective-permute-done.19.payload_in, ...), custom_call_target="tpu_custom_call" | custom-call | tf_op jit(solution)/shard_map/pallas_call | solution.py:283
  89.5 1.6 %collective-permute-done.14.payload_in = bf16[272,384]{1,0:T(8,128)(2,1)S(1)} collective-permute-done((bf16[272,384]{1,0:T(8,128)(2,1)S(1)}, bf16[272,384]{1,0:T(8,128)(2,1)S(1)}, u32[]{:S(2)}, u32[]{:S(2)}) %collective-permute-start.14) | collective-permute-done | bytes 208928 | tf_op jit(solution)/shard_map/ppermute | solution.py:24
  91.2 1.1 %shard_map.73 = (f32[256,384]{1,0:T(8,128)S(1)}, f32[8,128]{1,0:T(8,128)S(1)}) custom-call(s32[4]{0:T(128)S(1)} %pad_add_fusion.place_ref, f32[256,384]{1,0:T(8,128)S(1)} %get-tuple-element.43.local_out, f32[16,128]{1,0:T(8,128)S(1)} %get-tuple-element.44.local_stats, bf16[272,384]{1,0:T(8,128)(2,1)S(1)} %collective-permute-done.14.payload_in, ...), custom_call_target="tpu_custom_call" | custom-call | tf_op jit(solution)/shard_map/pallas_call | solution.py:283
  92.3 3.1 %collective-permute-done.9.payload_in = bf16[272,384]{1,0:T(8,128)(2,1)S(1)} collective-permute-done((bf16[272,384]{1,0:T(8,128)(2,1)S(1)}, bf16[272,384]{1,0:T(8,128)(2,1)S(1)}, u32[]{:S(2)}, u32[]{:S(2)}) %collective-permute-start.9) | collective-permute-done | bytes 208928 | tf_op jit(solution)/shard_map/ppermute | solution.py:24
  95.3 1.1 %shard_map.74 = (f32[256,384]{1,0:T(8,128)S(1)}, f32[8,128]{1,0:T(8,128)S(1)}) custom-call(s32[4]{0:T(128)S(1)} %pad_add_fusion.place_ref, f32[256,384]{1,0:T(8,128)S(1)} %get-tuple-element.38.local_out, f32[16,128]{1,0:T(8,128)S(1)} %get-tuple-element.39.local_stats, bf16[272,384]{1,0:T(8,128)(2,1)S(1)} %collective-permute-done.9.payload_in, ...), custom_call_target="tpu_custom_call" | custom-call | tf_op jit(solution)/shard_map/pallas_call | solution.py:283
  96.4 1.2 %collective-permute-done.4.payload_in = bf16[272,384]{1,0:T(8,128)(2,1)S(1)} collective-permute-done((bf16[272,384]{1,0:T(8,128)(2,1)S(1)}, bf16[272,384]{1,0:T(8,128)(2,1)S(1)}, u32[]{:S(2)}, u32[]{:S(2)}) %collective-permute-start.4) | collective-permute-done | bytes 208928 | tf_op jit(solution)/shard_map/ppermute | solution.py:24
  97.6 1.1 %shard_map.75 = (f32[256,384]{1,0:T(8,128)S(1)}, f32[8,128]{1,0:T(8,128)S(1)}) custom-call(s32[4]{0:T(128)S(1)} %pad_add_fusion.place_ref, f32[256,384]{1,0:T(8,128)S(1)} %get-tuple-element.33.local_out, f32[16,128]{1,0:T(8,128)S(1)} %get-tuple-element.34.local_stats, bf16[272,384]{1,0:T(8,128)(2,1)S(1)} %collective-permute-done.4.payload_in, ...), custom_call_target="tpu_custom_call" | custom-call | tf_op jit(solution)/shard_map/pallas_call | solution.py:283
  98.6 5.6 %psum.7.squares = f32[8,128]{1,0:T(8,128)S(1)} all-reduce(f32[8,128]{1,0:T(8,128)S(1)} %get-tuple-element.56), channel_id=1, replica_groups=mesh['stretch'=2,'cp'=4,'tp'=4] {'tp'}, use_global_device_ids=true, to_apply=%region_0.0 | all-reduce | flops 1024 | bytes 8192 | tf_op jit(solution)/shard_map/psum | solution.py:291
  104.3 0.6 copy-done.7
  104.9 1.8 %shard_map.76 = bf16[256,1536]{1,0:T(8,128)(2,1)} custom-call(s32[4]{0:T(128)S(1)} %pad_add_fusion.place_ref, s32[4]{0:T(128)S(1)} %copy-done.7, f32[8,128]{1,0:T(8,128)S(1)} %psum.7.squares, bf16[16,1536]{1,0:T(8,128)(2,1)S(1)} %copy-done.6, f32[256,384]{1,0:T(8,128)S(1)} %get-tuple-element.57.refs_0_, f32[256,384]{1,0:T(8,128)S(1)} %get-tuple-element.58.refs_1_, ...), custom_call_target="tpu_custom_call" | custom-call | tf_op jit(solution)/shard_map/pallas_call | solution.py:292
  (20 shorter events, 0.2 us)
Async XLA Ops:
  0.0 2.7 %copy-start.8 = (bf16[2,128,1536]{2,1,0:T(8,128)(2,1)S(1)}, bf16[2,128,1536]{2,1,0:T(8,128)(2,1)}, u32[]{:S(2)}) copy-start(bf16[2,128,1536]{2,1,0:T(8,128)(2,1)} %param.7) | copy-start | bytes 2359300
  0.0 2.7 %copy-start.9 = (bf16[2,128,1536]{2,1,0:T(8,128)(2,1)S(1)}, bf16[2,128,1536]{2,1,0:T(8,128)(2,1)}, u32[]{:S(2)}) copy-start(bf16[2,128,1536]{2,1,0:T(8,128)(2,1)} %param.8) | copy-start | bytes 2359300
  1.4 10.4 %collective-permute-start.15 = (bf16[256,384]{1,0:T(8,128)(2,1)S(1)}, bf16[256,384]{1,0:T(8,128)(2,1)S(1)}, u32[]{:S(2)}, u32[]{:S(2)}) collective-permute-start(bf16[256,384]{1,0:T(8,128)(2,1)S(1)} %get-tuple-element.69.own_q), channel_id=1, source_target_pairs={{4,0},{8,4},{12,8},{5,1},{9,5},{13,9},{6,2},{10,6},{14,10},{7,3},{... | collective-permute-start | bytes 589832 | tf_op jit(solution)/shard_map/ppermute | solution.py:24
  3.0 24.7 %collective-permute-start.17 = (bf16[256,768]{1,0:T(8,128)(2,1)S(1)}, bf16[256,768]{1,0:T(8,128)(2,1)S(1)}, u32[]{:S(2)}, u32[]{:S(2)}) collective-permute-start(bf16[256,768]{1,0:T(8,128)(2,1)S(1)} %pad_maximum_fusion.3.own_kv), channel_id=1, source_target_pairs={{0,16},{1,17},{2,18},{3,19},{4,20},{5,21},{6,22},{7,23},{8,24},{9,... | collective-permute-start | bytes 1179656 | tf_op jit(solution)/shard_map/ppermute | solution.py:24
  7.8 10.5 %collective-permute-start.10 = (bf16[256,384]{1,0:T(8,128)(2,1)S(1)}, bf16[256,384]{1,0:T(8,128)(2,1)}, u32[]{:S(2)}, u32[]{:S(2)}) collective-permute-start(bf16[256,384]{1,0:T(8,128)(2,1)S(1)} %get-tuple-element.70.own_q), channel_id=1, source_target_pairs={{4,0},{8,4},{12,8},{5,1},{9,5},{13,9},{6,2},{10,6},{14,10},{7,3},{... | collective-permute-start | bytes 589832 | tf_op jit(solution)/shard_map/ppermute | solution.py:24
  9.1 13.4 %collective-permute-start.5 = (bf16[256,384]{1,0:T(8,128)(2,1)S(1)}, bf16[256,384]{1,0:T(8,128)(2,1)}, u32[]{:S(2)}, u32[]{:S(2)}) collective-permute-start(bf16[256,384]{1,0:T(8,128)(2,1)S(1)} %get-tuple-element.71.own_q), channel_id=1, source_target_pairs={{4,0},{8,4},{12,8},{5,1},{9,5},{13,9},{6,2},{10,6},{14,10},{7,3},{... | collective-permute-start | bytes 589832 | tf_op jit(solution)/shard_map/ppermute | solution.py:24
  10.5 21.6 %collective-permute-start.12 = (bf16[256,768]{1,0:T(8,128)(2,1)S(1)}, bf16[256,768]{1,0:T(8,128)(2,1)S(1)}, u32[]{:S(2)}, u32[]{:S(2)}) collective-permute-start(bf16[256,768]{1,0:T(8,128)(2,1)S(1)} %pad_maximum_fusion.2.own_kv), channel_id=1, source_target_pairs={{0,16},{1,17},{2,18},{3,19},{4,20},{5,21},{6,22},{7,23},{8,24},{9,... | collective-permute-start | bytes 1179656 | tf_op jit(solution)/shard_map/ppermute | solution.py:24
  11.8 10.7 %copy-start.2 = (bf16[256,384]{1,0:T(8,128)(2,1)}, bf16[256,384]{1,0:T(8,128)(2,1)S(1)}, u32[]{:S(2)}) copy-start(bf16[256,384]{1,0:T(8,128)(2,1)S(1)} %collective-permute-done.15.near_q) | copy-start | bytes 589828
  11.8 14.3 %collective-permute-start = (bf16[256,384]{1,0:T(8,128)(2,1)S(1)}, bf16[256,384]{1,0:T(8,128)(2,1)}, u32[]{:S(2)}, u32[]{:S(2)}) collective-permute-start(bf16[256,384]{1,0:T(8,128)(2,1)S(1)} %get-tuple-element.72.own_q), channel_id=1, source_target_pairs={{4,0},{8,4},{12,8},{5,1},{9,5},{13,9},{6,2},{10,6},{14,10},{7,3},{... | collective-permute-start | bytes 589832 | tf_op jit(solution)/shard_map/ppermute | solution.py:24
  18.3 35.8 %collective-permute-start.7 = (bf16[256,768]{1,0:T(8,128)(2,1)S(1)}, bf16[256,768]{1,0:T(8,128)(2,1)S(1)}, u32[]{:S(2)}, u32[]{:S(2)}) collective-permute-start(bf16[256,768]{1,0:T(8,128)(2,1)S(1)} %pad_maximum_fusion.1.own_kv), channel_id=1, source_target_pairs={{0,16},{1,17},{2,18},{3,19},{4,20},{5,21},{6,22},{7,23},{8,24},{9,... | collective-permute-start | bytes 1179656 | tf_op jit(solution)/shard_map/ppermute | solution.py:24
  22.5 7.6 %collective-permute-start.16 = (bf16[256,384]{1,0:T(8,128)(2,1)S(1)}, bf16[256,384]{1,0:T(8,128)(2,1)S(1)}, u32[]{:S(2)}, u32[]{:S(2)}) collective-permute-start(bf16[256,384]{1,0:T(8,128)(2,1)S(1)} %collective-permute-done.15.near_q), channel_id=1, source_target_pairs={{4,0},{8,4},{12,8},{5,1},{9,5},{13,9},{6,2},{10,6},{14,10},{7,3},{... | collective-permute-start | bytes 589832 | tf_op jit(solution)/shard_map/ppermute | solution.py:24
  26.2 42.7 %collective-permute-start.2 = (bf16[256,768]{1,0:T(8,128)(2,1)S(1)}, bf16[256,768]{1,0:T(8,128)(2,1)S(1)}, u32[]{:S(2)}, u32[]{:S(2)}) collective-permute-start(bf16[256,768]{1,0:T(8,128)(2,1)S(1)} %pad_maximum_fusion.own_kv), channel_id=1, source_target_pairs={{0,16},{1,17},{2,18},{3,19},{4,20},{5,21},{6,22},{7,23},{8,24},{9,... | collective-permute-start | bytes 1179656 | tf_op jit(solution)/shard_map/ppermute | solution.py:24
  27.7 0.7 copy-start
  28.4 14.2 %collective-permute-start.11 = (bf16[256,384]{1,0:T(8,128)(2,1)}, bf16[256,384]{1,0:T(8,128)(2,1)}, u32[]{:S(2)}, u32[]{:S(2)}) collective-permute-start(bf16[256,384]{1,0:T(8,128)(2,1)} %collective-permute-done.10.near_q), channel_id=1, source_target_pairs={{4,0},{8,4},{12,8},{5,1},{9,5},{13,9},{6,2},{10,6},{14,10},{7,3},{... | collective-permute-start | bytes 589832 | tf_op jit(solution)/shard_map/ppermute | solution.py:24
  30.1 0.7 copy-start.4
  30.8 27.3 %collective-permute-start.6 = (bf16[256,384]{1,0:T(8,128)(2,1)}, bf16[256,384]{1,0:T(8,128)(2,1)}, u32[]{:S(2)}, u32[]{:S(2)}) collective-permute-start(bf16[256,384]{1,0:T(8,128)(2,1)} %collective-permute-done.5.near_q), channel_id=1, source_target_pairs={{4,0},{8,4},{12,8},{5,1},{9,5},{13,9},{6,2},{10,6},{14,10},{7,3},{... | collective-permute-start | bytes 589832 | tf_op jit(solution)/shard_map/ppermute | solution.py:24
  32.1 36.8 %collective-permute-start.1 = (bf16[256,384]{1,0:T(8,128)(2,1)}, bf16[256,384]{1,0:T(8,128)(2,1)}, u32[]{:S(2)}, u32[]{:S(2)}) collective-permute-start(bf16[256,384]{1,0:T(8,128)(2,1)} %collective-permute-done.near_q), channel_id=1, source_target_pairs={{4,0},{8,4},{12,8},{5,1},{9,5},{13,9},{6,2},{10,6},{14,10},{7,3},{... | collective-permute-start | bytes 589832 | tf_op jit(solution)/shard_map/ppermute | solution.py:24
  34.3 1.0 copy-start.1
  35.3 0.9 copy-start.3
  36.2 0.9 copy-start.5
  42.6 34.2 %collective-permute-start.18 = (bf16[272,384]{1,0:T(8,128)(2,1)S(1)}, bf16[272,384]{1,0:T(8,128)(2,1)S(1)}, u32[]{:S(2)}, u32[]{:S(2)}) collective-permute-start(bf16[272,384]{1,0:T(8,128)(2,1)S(1)} %get-tuple-element.52), channel_id=1, source_target_pairs={{0,4},{4,8},{8,12},{1,5},{5,9},{9,13},{2,6},{6,10},{10,14},{3,7},{... | collective-permute-start | bytes 626696 | tf_op jit(solution)/shard_map/ppermute | solution.py:24
  54.1 25.6 %collective-permute-start.13 = (bf16[272,384]{1,0:T(8,128)(2,1)S(1)}, bf16[272,384]{1,0:T(8,128)(2,1)S(1)}, u32[]{:S(2)}, u32[]{:S(2)}) collective-permute-start(bf16[272,384]{1,0:T(8,128)(2,1)S(1)} %get-tuple-element.47), channel_id=1, source_target_pairs={{0,4},{4,8},{8,12},{1,5},{5,9},{9,13},{2,6},{6,10},{10,14},{3,7},{... | collective-permute-start | bytes 626696 | tf_op jit(solution)/shard_map/ppermute | solution.py:24
  64.1 18.5 %collective-permute-start.8 = (bf16[272,384]{1,0:T(8,128)(2,1)S(1)}, bf16[272,384]{1,0:T(8,128)(2,1)S(1)}, u32[]{:S(2)}, u32[]{:S(2)}) collective-permute-start(bf16[272,384]{1,0:T(8,128)(2,1)S(1)} %get-tuple-element.42), channel_id=1, source_target_pairs={{0,4},{4,8},{8,12},{1,5},{5,9},{9,13},{2,6},{6,10},{10,14},{3,7},{... | collective-permute-start | bytes 626696 | tf_op jit(solution)/shard_map/ppermute | solution.py:24
  74.8 10.7 %collective-permute-start.3 = (bf16[272,384]{1,0:T(8,128)(2,1)S(1)}, bf16[272,384]{1,0:T(8,128)(2,1)S(1)}, u32[]{:S(2)}, u32[]{:S(2)}) collective-permute-start(bf16[272,384]{1,0:T(8,128)(2,1)S(1)} %get-tuple-element.37), channel_id=1, source_target_pairs={{0,4},{4,8},{8,12},{1,5},{5,9},{9,13},{2,6},{6,10},{10,14},{3,7},{... | collective-permute-start | bytes 626696 | tf_op jit(solution)/shard_map/ppermute | solution.py:24
  77.8 10.7 %collective-permute-start.19 = (bf16[272,384]{1,0:T(8,128)(2,1)S(1)}, bf16[272,384]{1,0:T(8,128)(2,1)S(1)}, u32[]{:S(2)}, u32[]{:S(2)}) collective-permute-start(bf16[272,384]{1,0:T(8,128)(2,1)S(1)} %shard_map.71), channel_id=1, source_target_pairs={{0,4},{4,8},{8,12},{1,5},{5,9},{9,13},{2,6},{6,10},{10,14},{3,7},{... | collective-permute-start | bytes 626696 | tf_op jit(solution)/shard_map/ppermute | solution.py:24
  80.7 10.5 %collective-permute-start.14 = (bf16[272,384]{1,0:T(8,128)(2,1)S(1)}, bf16[272,384]{1,0:T(8,128)(2,1)S(1)}, u32[]{:S(2)}, u32[]{:S(2)}) collective-permute-start(bf16[272,384]{1,0:T(8,128)(2,1)S(1)} %shard_map.69), channel_id=1, source_target_pairs={{0,4},{4,8},{8,12},{1,5},{5,9},{9,13},{2,6},{6,10},{10,14},{3,7},{... | collective-permute-start | bytes 626696 | tf_op jit(solution)/shard_map/ppermute | solution.py:24
  83.6 11.7 %collective-permute-start.9 = (bf16[272,384]{1,0:T(8,128)(2,1)S(1)}, bf16[272,384]{1,0:T(8,128)(2,1)S(1)}, u32[]{:S(2)}, u32[]{:S(2)}) collective-permute-start(bf16[272,384]{1,0:T(8,128)(2,1)S(1)} %shard_map.67), channel_id=1, source_target_pairs={{0,4},{4,8},{8,12},{1,5},{5,9},{9,13},{2,6},{6,10},{10,14},{3,7},{... | collective-permute-start | bytes 626696 | tf_op jit(solution)/shard_map/ppermute | solution.py:24
  86.5 11.1 %collective-permute-start.4 = (bf16[272,384]{1,0:T(8,128)(2,1)S(1)}, bf16[272,384]{1,0:T(8,128)(2,1)S(1)}, u32[]{:S(2)}, u32[]{:S(2)}) collective-permute-start(bf16[272,384]{1,0:T(8,128)(2,1)S(1)} %shard_map.65), channel_id=1, source_target_pairs={{0,4},{4,8},{8,12},{1,5},{5,9},{9,13},{2,6},{6,10},{10,14},{3,7},{... | collective-permute-start | bytes 626696 | tf_op jit(solution)/shard_map/ppermute | solution.py:24
  97.6 6.7 %copy-start.6 = (bf16[16,1536]{1,0:T(8,128)(2,1)S(1)}, bf16[16,1536]{1,0:T(8,128)(2,1)}, u32[]{:S(2)}) copy-start(bf16[16,1536]{1,0:T(8,128)(2,1)} %gate_table.1) | copy-start | bytes 147460
  104.3 0.7 copy-start.7
where the time goes:
time: 108 us; the launch traced here: 107 us
  starting transfers between devices  43.3 us (40%)
  Pallas kernels  33.4 us (31%)
  waiting for transfers between devices  16.4 us (15%)
  local copies, waits for them, and re-layouts  7.34 us (7%)
  blocking collectives  5.64 us (5%)
    ppermute x20, starting transfers between devices, moved(): return lax.ppermute(block, axis, route)  43.3 us
    pallas_call x4, Pallas kernels, on_device(): pl.pallas_call(functools.partial(attend_kernel, head_count), out_shape=(f...  23.5 us
    ppermute x20, waiting for transfers between devices, moved(): return lax.ppermute(block, axis, route)  16.4 us
    psum x1, blocking collectives, on_device(): squares = lax.psum(squares, 'tp')  5.64 us
    unnamed x20, local copies, waits for them, and re-layouts  4.93 us
    pallas_call x4, Pallas kernels, on_device(): pl.pallas_call(functools.partial(finish_kernel, head_count), out_shape=(f...  4.34 us
    pallas_call x4, Pallas kernels, on_device(): pl.pallas_call(functools.partial(relay_kernel, head_count), out_shape=pay...  3.86 us
  transfers between devices with their start and end apart: 20, of which 7 were waited for; matrix products, arithmetic and copies ran while one was open for 1% of the time, Pallas kernels for 29%

commit v1 on v0

v1 whole, which is shorter than its diff:
```python
import functools
import math

import jax
import jax.numpy as jnp
from jax import lax
from jax.experimental import pallas as pl
from jax.experimental.pallas import tpu as pltpu
from jax.sharding import PartitionSpec as P

HEADS = 48
HEAD_DIM = 128
BLOCK = 128
REACH = 2
CHUNKS = (4, 4)
KEYS_MOVED = 4
FINISH_ORDER = (2, 0, 1)
STAT_ROWS = 16
HIDDEN = -1e30
EXPONENT_SCALE = math.log2(math.e) / math.sqrt(HEAD_DIM)


def moved(block, axis, distance):
    devices = range(lax.axis_size(axis))
    route = [(i - distance, i) for i in devices if i - distance in devices]
    return lax.ppermute(block, axis, route)


def head_columns(head):
    return slice(head * HEAD_DIM, (head + 1) * HEAD_DIM)


def stretch_rows(slot):
    return slice(slot * BLOCK, (slot + 1) * BLOCK)


def as_columns(rows):
    fill = jnp.zeros((BLOCK - rows.shape[0], BLOCK), jnp.float32)
    return jnp.transpose(jnp.concatenate([rows, fill], axis=0))


def put_stats(payload_ref, stats, token_rows):
    high = stats.astype(jnp.bfloat16)
    rest = stats - high.astype(jnp.float32)
    middle = rest.astype(jnp.bfloat16)
    low = (rest - middle.astype(jnp.float32)).astype(jnp.bfloat16)
    rows = slice(token_rows, token_rows + STAT_ROWS)
    for index, piece in enumerate((high, middle, low)):
        payload_ref[rows, head_columns(index)] = piece


def get_stats(payload_ref, token_rows):
    rows = slice(token_rows, token_rows + STAT_ROWS)
    pieces = [
        payload_ref[rows, head_columns(index)].astype(jnp.float32) for index in range(3)
    ]
    return (pieces[0] + pieces[1]) + pieces[2]


def shown(place_ref, ranges_ref, query_stretch, query_block, key_stretch, key_block):
    stretch_count, block_count = place_ref[2], place_ref[3]
    low, high = (
        ranges_ref[
            end,
            jnp.minimum(query_stretch, stretch_count - 1),
            jnp.minimum(query_block, block_count - 1),
            jnp.maximum(key_stretch, 0),
        ]
        for end in range(2)
    )
    exists = (
        (query_stretch < stretch_count)
        & (query_block < block_count)
        & (key_stretch >= 0)
        & (key_block >= 0)
    )
    return exists & (low <= key_block) & (key_block < high)


def attend(query, keys, values, seen):
    scores = lax.dot_general(
        keys, query, (((1,), (1,)), ((), ())), preferred_element_type=jnp.float32
    )
    blocks = [scores[stretch_rows(j)] for j in range(len(seen))]
    peak = jnp.full((1, BLOCK), HIDDEN, jnp.float32)
    for block, flag in zip(blocks, seen):
        block_peak = jnp.max(block, axis=0, keepdims=True)
        peak = jnp.maximum(peak, jnp.where(flag, block_peak, HIDDEN))
    shift = peak * EXPONENT_SCALE
    weights = [
        jnp.exp2(block * EXPONENT_SCALE - jnp.where(flag, shift, -HIDDEN))
        for block, flag in zip(blocks, seen)
    ]
    total = sum(jnp.sum(weight, axis=0, keepdims=True) for weight in weights)
    weights = jnp.concatenate([weight.astype(jnp.bfloat16) for weight in weights], axis=0)
    summed = jnp.dot(values, weights, preferred_element_type=jnp.float32)
    total = jnp.maximum(total, 1e-30)
    return summed * (1.0 / total), jnp.maximum(shift + jnp.log2(total), HIDDEN)


def keys_and_values(refs, head, head_count):
    columns = head_columns(head)
    value_columns = head_columns(head_count + head)
    keys = jnp.concatenate([ref[:, columns] for ref in refs], axis=0)
    values = jnp.concatenate([ref[:, value_columns] for ref in refs], axis=0)
    return keys, jnp.transpose(values)


def queries_moved_kernel(
    head_count,
    place_ref,
    ranges_ref,
    own_q,
    near_q,
    far_q,
    own_kv,
    prior_kv,
    *rest,
    pair_count,
):
    own_out, own_stats, near_out, near_stats, far_payload = rest[-5:]
    group, position = place_ref[0], place_ref[1]
    token_rows = pair_count * BLOCK
    seen = {
        (distance, slot): [
            shown(
                place_ref,
                ranges_ref,
                group * pair_count + slot,
                position + distance,
                (group - 1) * pair_count + key_slot,
                position,
            )
            for key_slot in range(2 * pair_count)
        ]
        for distance in range(REACH + 1)
        for slot in range(pair_count)
    }
    own_stats[...] = jnp.zeros_like(own_stats)
    near_stats[...] = jnp.zeros_like(near_stats)
    far_stats = [jnp.zeros((1, BLOCK), jnp.float32)] * STAT_ROWS
    for head in range(head_count):
        columns = head_columns(head)
        keys, values = keys_and_values((prior_kv, own_kv), head, head_count)
        for distance, query_ref in ((2, far_q), (1, near_q), (0, own_q)):
            for slot in range(pair_count):
                rows = stretch_rows(slot)
                attended, log_total = attend(
                    query_ref[rows, columns], keys, values, seen[distance, slot]
                )
                index = slot * head_count + head
                if distance == 0:
                    own_out[rows, columns] = attended
                    own_stats[index : index + 1, :] = log_total
                elif distance == 1:
                    near_out[rows, columns] = attended
                    near_stats[index : index + 1, :] = log_total
                else:
                    far_payload[rows, columns] = attended.astype(jnp.bfloat16)
                    far_stats[index] = log_total
    put_stats(far_payload, jnp.concatenate(far_stats, axis=0), token_rows)


def keys_moved_kernel(
    head_count,
    place_ref,
    ranges_ref,
    own_q,
    next_q,
    own_kv,
    near_kv,
    far_kv,
    *rest,
    pair_count,
):
    own_out, own_stats, next_payload = rest[-3:]
    group, position = place_ref[0], place_ref[1]
    token_rows = pair_count * BLOCK
    seen = {
        (ahead, slot): [
            shown(
                place_ref,
                ranges_ref,
                (group + ahead) * pair_count + slot,
                position,
                group * pair_count + key_slot,
                position - distance,
            )
            for distance in range(REACH + 1)
            for key_slot in range(pair_count)
        ]
        for ahead in range(2)
        for slot in range(pair_count)
    }
    own_stats[...] = jnp.zeros_like(own_stats)
    next_stats = [jnp.zeros((1, BLOCK), jnp.float32)] * STAT_ROWS
    for head in range(head_count):
        columns = head_columns(head)
        keys, values = keys_and_values((own_kv, near_kv, far_kv), head, head_count)
        for ahead, query_ref in ((1, next_q), (0, own_q)):
            for slot in range(pair_count):
                rows = stretch_rows(slot)
                attended, log_total = attend(
                    query_ref[rows, columns], keys, values, seen[ahead, slot]
                )
                index = slot * head_count + head
                if ahead:
                    next_payload[rows, columns] = attended.astype(jnp.bfloat16)
                    next_stats[index] = log_total
                else:
                    own_out[rows, columns] = attended
                    own_stats[index : index + 1, :] = log_total
    put_stats(next_payload, jnp.concatenate(next_stats, axis=0), token_rows)


def joined(sender_index, local_out, local_stats, payload_ref, head_count):
    token_rows = local_out.shape[0]
    local_log = local_stats[...]
    remote_log = jnp.where(sender_index > 0, get_stats(payload_ref, token_rows), HIDDEN)
    top = jnp.maximum(local_log, remote_log)
    local_weight = jnp.exp2(local_log - top)
    remote_weight = jnp.exp2(remote_log - top)
    both = local_weight + remote_weight
    scale = 1.0 / both
    local_weight = local_weight * scale
    remote_weight = remote_weight * scale
    parts = {}
    for slot in range(token_rows // BLOCK):
        for head in range(head_count):
            index = slot * head_count + head
            rows, columns = stretch_rows(slot), head_columns(head)
            parts[slot, head] = (
                local_out[rows, columns] * local_weight[index : index + 1]
                + payload_ref[rows, columns].astype(jnp.float32)
                * remote_weight[index : index + 1]
            )
    return parts, top + jnp.log2(both)


def relay_kernel(
    head_count, place_ref, local_out, local_stats, payload_in, *rest, axis
):
    payload_out = rest[-1]
    parts, log_total = joined(place_ref[axis], local_out, local_stats, payload_in, head_count)
    for (slot, head), part in parts.items():
        payload_out[stretch_rows(slot), head_columns(head)] = part.astype(jnp.bfloat16)
    put_stats(payload_out, log_total, local_out.shape[0])


def finish_kernel(
    head_count, place_ref, local_out, local_stats, payload_in, squares_in, *rest, axis
):
    out, squares_out = rest[-2:]
    parts, _ = joined(place_ref[axis], local_out, local_stats, payload_in, head_count)
    squares_out[...] = squares_in[...]
    for slot in range(local_out.shape[0] // BLOCK):
        total = jnp.zeros((1, BLOCK), jnp.float32)
        for head in range(head_count):
            part = parts[slot, head]
            total = total + jnp.sum(part * part, axis=0, keepdims=True)
            out[stretch_rows(slot), head_columns(head)] = jnp.transpose(part)
        squares_out[slot : slot + 1, :] += total


def scale_kernel(head_counts, feature_count, place_ref, levels_ref, squares, gate_table, *refs):
    parts, out = refs[:-1], refs[-1]
    factors = as_columns(lax.rsqrt(squares[...] / feature_count + 1e-06))
    pair_count = out.shape[0] // BLOCK
    gates = gate_table[...].astype(jnp.float32)
    level_ids = lax.broadcasted_iota(jnp.int32, gates.shape, 0)
    for slot in range(pair_count):
        level = levels_ref[place_ref[0] * pair_count + slot]
        gate_row = jnp.sum(jnp.where(level_ids == level, gates, 0.0), axis=0, keepdims=True)
        rows = stretch_rows(slot)
        factor = factors[:, slot : slot + 1]
        base = 0
        for part, head_count in zip(parts, head_counts):
            for head in range(head_count):
                columns = head_columns(base + head)
                out[rows, columns] = (
                    part[rows, head_columns(head)] * factor * gate_row[:, columns]
                ).astype(jnp.bfloat16)
            base += head_count


def cost(microseconds):
    return pl.CostEstimate(
        flops=int(microseconds * 1e9), bytes_accessed=int(microseconds * 1e6), transcendentals=0
    )


SMEM = pl.BlockSpec(memory_space=pltpu.SMEM)
VMEM = pl.BlockSpec(memory_space=pltpu.VMEM)
PARAMS = pltpu.CompilerParams(vmem_limit_bytes=32 * 1024 * 1024)


def on_device(query_rows, key_rows, value_rows, gate_table, levels, kv_ranges):
    pair_count, row_count, width_dev = query_rows.shape
    assert row_count == BLOCK
    token_rows = pair_count * row_count
    head_total = width_dev // HEAD_DIM
    place = jnp.stack(
        [
            lax.axis_index("stretch"),
            lax.axis_index("cp"),
            jnp.int32(kv_ranges.shape[1]),
            jnp.int32(kv_ranges.shape[2]),
        ]
    ).astype(jnp.int32)
    queries, keys, values = (
        array.reshape(token_rows, width_dev) for array in (query_rows, key_rows, value_rows)
    )
    head_counts = CHUNKS + (KEYS_MOVED,)
    assert sum(head_counts) == head_total
    starts = [sum(head_counts[:i]) * HEAD_DIM for i in range(len(head_counts))]
    widths = [count * HEAD_DIM for count in head_counts]
    chunks = range(len(CHUNKS))
    last = len(CHUNKS)

    def cut(array, chunk):
        return lax.slice_in_dim(array, starts[chunk], starts[chunk] + widths[chunk], axis=1)

    def cut_kv(chunk):
        return jnp.concatenate([cut(keys, chunk), cut(values, chunk)], axis=1)

    def float_shape(chunk):
        return jax.ShapeDtypeStruct((token_rows, widths[chunk]), jnp.float32)

    def payload_shape(chunk):
        return jax.ShapeDtypeStruct((token_rows + STAT_ROWS, widths[chunk]), jnp.bfloat16)

    stats_shape = jax.ShapeDtypeStruct((STAT_ROWS, BLOCK), jnp.float32)
    squares_shape = jax.ShapeDtypeStruct((8, BLOCK), jnp.float32)

    def run(kernel, chunk, microseconds, out_shape, smem, vmem, after=()):
        return pl.pallas_call(
            functools.partial(kernel, head_counts[chunk]),
            out_shape=out_shape,
            in_specs=[SMEM] * len(smem)
            + [VMEM] * len(vmem)
            + [pl.BlockSpec(memory_space=pl.ANY)] * len(after),
            out_specs=(VMEM,) * len(out_shape),
            compiler_params=PARAMS,
            cost_estimate=cost(microseconds),
        )(*smem, *vmem, *after)

    own_q = [cut(queries, i) for i in chunks]
    own_kv = [cut_kv(i) for i in chunks]
    near_q = [moved(own_q[i], "cp", -1) for i in chunks]
    first_q = cut(queries, last)
    first_kv = cut_kv(last)
    near_kv = moved(first_kv, "cp", 1)
    next_q = moved(first_q, "stretch", -1)
    prior_kv = [moved(own_kv[i], "stretch", 1) for i in chunks]
    far_q = [moved(near_q[i], "cp", -1) for i in chunks]
    far_kv = moved(near_kv, "cp", 1)

    own_parts, near_parts, arrived = [], [], []
    for i in chunks:
        own_out, own_stats, near_out, near_stats, far_payload = run(
            functools.partial(queries_moved_kernel, pair_count=pair_count),
            i,
            1.0 * head_counts[i],
            (float_shape(i), stats_shape, float_shape(i), stats_shape, payload_shape(i)),
            (place, kv_ranges),
            (own_q[i], near_q[i], far_q[i], own_kv[i], prior_kv[i]),
        )
        own_parts.append((own_out, own_stats))
        near_parts.append((near_out, near_stats))
        arrived.append(moved(far_payload, "cp", 1))
    own_out, own_stats, next_payload = run(
        functools.partial(keys_moved_kernel, pair_count=pair_count),
        last,
        1.0 * head_counts[last],
        (float_shape(last), stats_shape, payload_shape(last)),
        (place, kv_ranges),
        (first_q, next_q, first_kv, near_kv, far_kv),
    )
    own_parts.append((own_out, own_stats))
    prior_payload = moved(next_payload, "stretch", 1)
    for i in chunks:
        (relayed,) = run(
            functools.partial(relay_kernel, axis=1),
            i,
            0.7,
            (payload_shape(i),),
            (place,),
            (*near_parts[i], arrived[i]),
        )
        arrived[i] = moved(relayed, "cp", 1)
    arrived.append(prior_payload)
    squares = jnp.zeros(squares_shape.shape, jnp.float32)
    finished = [None] * len(head_counts)
    for i in FINISH_ORDER:
        finished[i], squares = run(
            functools.partial(finish_kernel, axis=0 if i == last else 1),
            i,
            0.8,
            (float_shape(i), squares_shape),
            (place,),
            (*own_parts[i], arrived[i], squares),
        )
    squares = lax.psum(squares, "tp")
    out = pl.pallas_call(
        functools.partial(scale_kernel, head_counts, float(HEADS * HEAD_DIM)),
        out_shape=jax.ShapeDtypeStruct((token_rows, width_dev), jnp.bfloat16),
        in_specs=[SMEM, SMEM] + [VMEM] * (2 + len(finished)),
        out_specs=VMEM,
        compiler_params=PARAMS,
    )(place, levels, squares, gate_table, *finished)
    return out.reshape(query_rows.shape)


def solution(mesh):
    in_specs = (
        P("stretch", "cp", "tp"),
        P("stretch", "cp", "tp"),
        P("stretch", "cp", "tp"),
        P(None, "tp"),
        P(),
        P(),
    )
    out_specs = P("stretch", "cp", "tp")
    return jax.shard_map(
        on_device, mesh=mesh, in_specs=in_specs, out_specs=out_specs, check_vma=False
    )
```

time: 108 us -> 74.4 us (0.69)
  Pallas kernels: 33.4 us -> 16.2 us
  waiting for transfers between devices: 16.4 us -> 7.42 us
  local copies, waits for them, and re-layouts: 7.34 us -> 2.19 us
  starting transfers between devices: 43.3 us -> 41.8 us
    pallas_call x12 -> x8, Pallas kernels: 31.7 us -> 14.5 us  [run(): pl.pallas_call(functools.partial(kernel, head_counts[chunk]), out_shape=o...]
    ppermute x20 -> x14, waiting for transfers between devices: 16.4 us -> 7.42 us  [moved(): return lax.ppermute(block, axis, route)]
    unnamed x20 -> x8, local copies, waits for them, and re-layouts: 4.93 us -> 0.66 us
    ppermute x20 -> x14, starting transfers between devices: 43.3 us -> 41.8 us  [moved(): return lax.ppermute(block, axis, route)]
  transfers between devices with their start and end apart: 20 -> 14, of which waited for: 7 -> 4; matrix products, arithmetic and copies ran while one was open for 1% -> 0% of each run, Pallas kernels for 29% -> 19%
where the time goes in v1:
time: 74.4 us; the launch traced here: 73.9 us
  starting transfers between devices  41.8 us (56%)
  Pallas kernels  16.2 us (22%)
  waiting for transfers between devices  7.42 us (10%)
  blocking collectives  5.67 us (8%)
  local copies, waits for them, and re-layouts  2.19 us (3%)
    ppermute x14, starting transfers between devices, moved(): return lax.ppermute(block, axis, route)  41.8 us
    pallas_call x8, Pallas kernels, run(): pl.pallas_call(functools.partial(kernel, head_counts[chunk]), out_shape=o...  14.5 us
    ppermute x14, waiting for transfers between devices, moved(): return lax.ppermute(block, axis, route)  7.42 us
    psum x1, blocking collectives, on_device(): squares = lax.psum(squares, 'tp')  5.67 us
    pallas_call x1, Pallas kernels, on_device(): pl.pallas_call(functools.partial(scale_kernel, head_counts, float(HEADS *...  1.74 us
    slice x2, local copies, waits for them, and re-layouts, cut(): lax.slice_in_dim(array, starts[chunk], starts[chunk] + widths[chunk], axi...  1.52 us
  transfers between devices with their start and end apart: 14, of which 4 were waited for; matrix products, arithmetic and copies ran while one was open for 0% of the time, Pallas kernels for 19%

profile of v1, /device:TPU:0, one launch (start us, length us, event | category | flops | bytes accessed | tf_op | source)
XLA Modules:
  0.0 73.9 jit_solution(5037145717843709592)
XLA Ops:
  0.0 1.5 %fusion = (bf16[256,512]{1,0:T(8,128)(2,1)S(1)}, bf16[256,512]{1,0:T(8,128)(2,1)S(1)}, bf16[256,512]{1,0:T(8,128)(2,1)S(1)}, bf16[256,512]{1,0:T(8,128)(2,1)S(1)...) fusion(bf16[256,1536]{1,0:T(8,128)(2,1)} %bitcast.7, bf16[256,1536]{1,0:T(8,128)(2,1)} %bitcast.8), kind=kLoop, calls=%fused_computation.4 | loop fusion | bytes 3145728 | tf_op jit(solution)/shard_map/slice | solution.py:321
  1.5 0.0 copy-start.3
  1.5 0.1 pad_maximum_fusion.2.own_kv
  1.5 5.1 %collective-permute-start.11 = (bf16[256,1024]{1,0:T(8,128)(2,1)S(1)}, bf16[256,1024]{1,0:T(8,128)(2,1)S(1)}, u32[]{:S(2)}, u32[]{:S(2)}) collective-permute-start(bf16[256,1024]{1,0:T(8,128)(2,1)S(1)} %pad_maximum_fusion.2.own_kv), channel_id=1, source_target_pairs={{0,4},{4,8},{8,12},{1,5},{5,9},{9,13},{2,6},{6,10},{10,14},{3,7},{... | collective-permute-start | bytes 1572872 | tf_op jit(solution)/shard_map/ppermute | solution.py:26
  6.6 0.0 copy-done.3
  6.6 0.1 fusion.2
  6.7 1.3 %collective-permute-start.5 = (bf16[256,512]{1,0:T(8,128)(2,1)S(1)}, bf16[256,512]{1,0:T(8,128)(2,1)}, u32[]{:S(2)}, u32[]{:S(2)}) collective-permute-start(bf16[256,512]{1,0:T(8,128)(2,1)S(1)} %get-tuple-element.50.own_q), channel_id=1, source_target_pairs={{4,0},{8,4},{12,8},{5,1},{9,5},{13,9},{6,2},{10,6},{14,10},{7,3},{... | collective-permute-start | bytes 786440 | tf_op jit(solution)/shard_map/ppermute | solution.py:26
  8.0 0.1 pad_maximum_fusion.1.own_kv
  8.1 4.2 %collective-permute-start.7 = (bf16[256,1024]{1,0:T(8,128)(2,1)S(1)}, bf16[256,1024]{1,0:T(8,128)(2,1)}, u32[]{:S(2)}, u32[]{:S(2)}) collective-permute-start(bf16[256,1024]{1,0:T(8,128)(2,1)S(1)} %pad_maximum_fusion.1.own_kv), channel_id=1, source_target_pairs={{0,16},{1,17},{2,18},{3,19},{4,20},{5,21},{6,22},{7,23},{8,24},{9,... | collective-permute-start | bytes 1572872 | tf_op jit(solution)/shard_map/ppermute | solution.py:26
  12.3 1.3 %collective-permute-start = (bf16[256,512]{1,0:T(8,128)(2,1)S(1)}, bf16[256,512]{1,0:T(8,128)(2,1)}, u32[]{:S(2)}, u32[]{:S(2)}) collective-permute-start(bf16[256,512]{1,0:T(8,128)(2,1)S(1)} %get-tuple-element.51.own_q), channel_id=1, source_target_pairs={{4,0},{8,4},{12,8},{5,1},{9,5},{13,9},{6,2},{10,6},{14,10},{7,3},{... | collective-permute-start | bytes 786440 | tf_op jit(solution)/shard_map/ppermute | solution.py:26
  13.6 2.9 %collective-permute-done.5.near_q = bf16[256,512]{1,0:T(8,128)(2,1)} collective-permute-done((bf16[256,512]{1,0:T(8,128)(2,1)S(1)}, bf16[256,512]{1,0:T(8,128)(2,1)}, u32[]{:S(2)}, u32[]{:S(2)}) %collective-permute-start.5) | collective-permute-done | bytes 262176 | tf_op jit(solution)/shard_map/ppermute | solution.py:26
  16.5 1.3 %collective-permute-start.6 = (bf16[256,512]{1,0:T(8,128)(2,1)}, bf16[256,512]{1,0:T(8,128)(2,1)}, u32[]{:S(2)}, u32[]{:S(2)}) collective-permute-start(bf16[256,512]{1,0:T(8,128)(2,1)} %collective-permute-done.5.near_q), channel_id=1, source_target_pairs={{4,0},{8,4},{12,8},{5,1},{9,5},{13,9},{6,2},{10,6},{14,10},{7,3},{... | collective-permute-start | bytes 786440 | tf_op jit(solution)/shard_map/ppermute | solution.py:26
  17.8 0.1 pad_maximum_fusion.own_kv
  17.8 0.0 copy-start.2
  17.8 4.9 %collective-permute-start.2 = (bf16[256,1024]{1,0:T(8,128)(2,1)S(1)}, bf16[256,1024]{1,0:T(8,128)(2,1)S(1)}, u32[]{:S(2)}, u32[]{:S(2)}) collective-permute-start(bf16[256,1024]{1,0:T(8,128)(2,1)S(1)} %pad_maximum_fusion.own_kv), channel_id=1, source_target_pairs={{0,16},{1,17},{2,18},{3,19},{4,20},{5,21},{6,22},{7,23},{8,24},{9,... | collective-permute-start | bytes 1572872 | tf_op jit(solution)/shard_map/ppermute | solution.py:26
  22.8 0.1 pad_add_fusion.place_ref
  22.8 1.3 %collective-permute-done.near_q = bf16[256,512]{1,0:T(8,128)(2,1)} collective-permute-done((bf16[256,512]{1,0:T(8,128)(2,1)S(1)}, bf16[256,512]{1,0:T(8,128)(2,1)}, u32[]{:S(2)}, u32[]{:S(2)}) %collective-permute-start) | collective-permute-done | bytes 262176 | tf_op jit(solution)/shard_map/ppermute | solution.py:26
  24.2 1.3 %collective-permute-start.10 = (bf16[256,512]{1,0:T(8,128)(2,1)S(1)}, bf16[256,512]{1,0:T(8,128)(2,1)S(1)}, u32[]{:S(2)}, u32[]{:S(2)}) collective-permute-start(bf16[256,512]{1,0:T(8,128)(2,1)S(1)} %get-tuple-element.49.own_q), channel_id=1, source_target_pairs={{16,0},{17,1},{18,2},{19,3},{20,4},{21,5},{22,6},{23,7},{24,8},{25... | collective-permute-start | bytes 786440 | tf_op jit(solution)/shard_map/ppermute | solution.py:26
  25.4 0.0 collective-permute-done.11.near_kv
  25.5 1.3 %collective-permute-start.1 = (bf16[256,512]{1,0:T(8,128)(2,1)}, bf16[256,512]{1,0:T(8,128)(2,1)S(1)}, u32[]{:S(2)}, u32[]{:S(2)}) collective-permute-start(bf16[256,512]{1,0:T(8,128)(2,1)} %collective-permute-done.near_q), channel_id=1, source_target_pairs={{4,0},{8,4},{12,8},{5,1},{9,5},{13,9},{6,2},{10,6},{14,10},{7,3},{... | collective-permute-start | bytes 786440 | tf_op jit(solution)/shard_map/ppermute | solution.py:26
  26.8 0.0 collective-permute-done.7.prior_kv
  26.8 4.6 %collective-permute-start.12 = (bf16[256,1024]{1,0:T(8,128)(2,1)S(1)}, bf16[256,1024]{1,0:T(8,128)(2,1)S(1)}, u32[]{:S(2)}, u32[]{:S(2)}) collective-permute-start(bf16[256,1024]{1,0:T(8,128)(2,1)S(1)} %collective-permute-done.11.near_kv), channel_id=1, source_target_pairs={{0,4},{4,8},{8,12},{1,5},{5,9},{9,13},{2,6},{6,10},{10,14},{3,7},{... | collective-permute-start | bytes 1572872 | tf_op jit(solution)/shard_map/ppermute | solution.py:26
  31.3 0.0 collective-permute-done.6.far_q
  31.4 0.0 copy-done.2
  31.4 3.7 %shard_map.66 = (f32[256,512]{1,0:T(8,128)S(1)}, f32[16,128]{1,0:T(8,128)S(1)}, f32[256,512]{1,0:T(8,128)S(1)}, f32[16,128]{1,0:T(8,128)S(1)}, bf16[272,512]{1,0:T(8,128)(2,1)S(1)}) custom-call(s32[4]{0:T(128)S(1)} %pad_add_fusion.place_ref, s32[2,4,4,4]{3,2,1,0:T(4,128)S(1)} %copy-done.2, bf16[256,512]{1,0:T(8,128)(2,1)S(1)} %get-tuple-element.50.own_q, ...), custom_call_target="tpu_custom_call" | custom-call | flops 4000000000 | bytes 4000000 | tf_op jit(solution)/shard_map/pallas_call | solution.py:336
  35.1 3.9 %collective-permute-start.8 = (bf16[272,512]{1,0:T(8,128)(2,1)S(1)}, bf16[272,512]{1,0:T(8,128)(2,1)S(1)}, u32[]{:S(2)}, u32[]{:S(2)}) collective-permute-start(bf16[272,512]{1,0:T(8,128)(2,1)S(1)} %get-tuple-element.33), channel_id=1, source_target_pairs={{0,4},{4,8},{8,12},{1,5},{5,9},{9,13},{2,6},{6,10},{10,14},{3,7},{... | collective-permute-start | bytes 835592 | tf_op jit(solution)/shard_map/ppermute | solution.py:26
  39.0 0.0 collective-permute-done.2.prior_kv
  39.0 0.0 collective-permute-done.1.far_q
  39.0 3.5 %shard_map.64 = (f32[256,512]{1,0:T(8,128)S(1)}, f32[16,128]{1,0:T(8,128)S(1)}, f32[256,512]{1,0:T(8,128)S(1)}, f32[16,128]{1,0:T(8,128)S(1)}, bf16[272,512]{1,0:T(8,128)(2,1)S(1)}) custom-call(s32[4]{0:T(128)S(1)} %pad_add_fusion.place_ref, s32[2,4,4,4]{3,2,1,0:T(4,128)S(1)} %copy-done.2, bf16[256,512]{1,0:T(8,128)(2,1)S(1)} %get-tuple-element.51.own_q, ...), custom_call_target="tpu_custom_call" | custom-call | flops 4000000000 | bytes 4000000 | tf_op jit(solution)/shard_map/pallas_call | solution.py:336
  42.5 3.5 %collective-permute-start.3 = (bf16[272,512]{1,0:T(8,128)(2,1)S(1)}, bf16[272,512]{1,0:T(8,128)(2,1)S(1)}, u32[]{:S(2)}, u32[]{:S(2)}) collective-permute-start(bf16[272,512]{1,0:T(8,128)(2,1)S(1)} %get-tuple-element.28), channel_id=1, source_target_pairs={{0,4},{4,8},{8,12},{1,5},{5,9},{9,13},{2,6},{6,10},{10,14},{3,7},{... | collective-permute-start | bytes 835592 | tf_op jit(solution)/shard_map/ppermute | solution.py:26
  46.0 0.0 collective-permute-done.10.next_q
  46.0 0.0 collective-permute-done.12.far_kv
  46.0 3.6 %shard_map.68 = (f32[256,512]{1,0:T(8,128)S(1)}, f32[16,128]{1,0:T(8,128)S(1)}, bf16[272,512]{1,0:T(8,128)(2,1)S(1)}) custom-call(s32[4]{0:T(128)S(1)} %pad_add_fusion.place_ref, s32[2,4,4,4]{3,2,1,0:T(4,128)S(1)} %copy-done.2, bf16[256,512]{1,0:T(8,128)(2,1)S(1)} %get-tuple-element.49.own_q, bf16[256,512]{1,0:T(8,128)(2,1)S(1)} %collective-permute-done.10.next_q, ...), custom_call_target="tpu_custom_call" | custom-call | flops 4000000000 | bytes 4000000 | tf_op jit(solution)/shard_map/pallas_call | solution.py:336
  49.6 4.6 %collective-permute-start.13 = (bf16[272,512]{1,0:T(8,128)(2,1)S(1)}, bf16[272,512]{1,0:T(8,128)(2,1)S(1)}, u32[]{:S(2)}, u32[]{:S(2)}) collective-permute-start(bf16[272,512]{1,0:T(8,128)(2,1)S(1)} %get-tuple-element.36), channel_id=1, source_target_pairs={{0,16},{1,17},{2,18},{3,19},{4,20},{5,21},{6,22},{7,23},{8,24},{9,... | collective-permute-start | bytes 835592 | tf_op jit(solution)/shard_map/ppermute | solution.py:26
  54.2 0.0 collective-permute-done.8.payload_in
  54.2 0.7 shard_map.67
  54.9 1.9 %collective-permute-start.9 = (bf16[272,512]{1,0:T(8,128)(2,1)S(1)}, bf16[272,512]{1,0:T(8,128)(2,1)S(1)}, u32[]{:S(2)}, u32[]{:S(2)}) collective-permute-start(bf16[272,512]{1,0:T(8,128)(2,1)S(1)} %shard_map.67), channel_id=1, source_target_pairs={{0,4},{4,8},{8,12},{1,5},{5,9},{9,13},{2,6},{6,10},{10,14},{3,7},{... | collective-permute-start | bytes 835592 | tf_op jit(solution)/shard_map/ppermute | solution.py:26
  56.8 0.0 collective-permute-done.3.payload_in
  56.9 0.7 shard_map.65
  57.5 2.7 %collective-permute-start.4 = (bf16[272,512]{1,0:T(8,128)(2,1)S(1)}, bf16[272,512]{1,0:T(8,128)(2,1)S(1)}, u32[]{:S(2)}, u32[]{:S(2)}) collective-permute-start(bf16[272,512]{1,0:T(8,128)(2,1)S(1)} %shard_map.65), channel_id=1, source_target_pairs={{0,4},{4,8},{8,12},{1,5},{5,9},{9,13},{2,6},{6,10},{10,14},{3,7},{... | collective-permute-start | bytes 835592 | tf_op jit(solution)/shard_map/ppermute | solution.py:26
  60.3 0.0 collective-permute-done.13.payload_in
  60.3 0.8 %shard_map.69 = (f32[256,512]{1,0:T(8,128)S(1)}, f32[8,128]{1,0:T(8,128)S(1)}) custom-call(s32[4]{0:T(128)S(1)} %pad_add_fusion.place_ref, f32[256,512]{1,0:T(8,128)S(1)} %get-tuple-element.34.local_out, f32[16,128]{1,0:T(8,128)S(1)} %get-tuple-element.35.local_stats, bf16[272,512]{1,0:T(8,128)(2,1)S(1)} %collective-permute-done.13.payload_in, ...), custom_call_target="tpu_custom_call" | custom-call | flops 800000000 | bytes 800000 | tf_op jit(solution)/shard_map/pallas_call | solution.py:336
  61.1 1.0 %collective-permute-done.9.payload_in = bf16[272,512]{1,0:T(8,128)(2,1)S(1)} collective-permute-done((bf16[272,512]{1,0:T(8,128)(2,1)S(1)}, bf16[272,512]{1,0:T(8,128)(2,1)S(1)}, u32[]{:S(2)}, u32[]{:S(2)}) %collective-permute-start.9) | collective-permute-done | bytes 278560 | tf_op jit(solution)/shard_map/ppermute | solution.py:26
  62.0 0.8 %shard_map.70 = (f32[256,512]{1,0:T(8,128)S(1)}, f32[8,128]{1,0:T(8,128)S(1)}) custom-call(s32[4]{0:T(128)S(1)} %pad_add_fusion.place_ref, f32[256,512]{1,0:T(8,128)S(1)} %get-tuple-element.29.local_out, f32[16,128]{1,0:T(8,128)S(1)} %get-tuple-element.30.local_stats, bf16[272,512]{1,0:T(8,128)(2,1)S(1)} %collective-permute-done.9.payload_in, ...), custom_call_target="tpu_custom_call" | custom-call | flops 800000000 | bytes 800000 | tf_op jit(solution)/shard_map/pallas_call | solution.py:336
  62.8 2.2 %collective-permute-done.4.payload_in = bf16[272,512]{1,0:T(8,128)(2,1)S(1)} collective-permute-done((bf16[272,512]{1,0:T(8,128)(2,1)S(1)}, bf16[272,512]{1,0:T(8,128)(2,1)S(1)}, u32[]{:S(2)}, u32[]{:S(2)}) %collective-permute-start.4) | collective-permute-done | bytes 278560 | tf_op jit(solution)/shard_map/ppermute | solution.py:26
  65.0 0.0 copy-start
  65.0 0.8 %shard_map.71 = (f32[256,512]{1,0:T(8,128)S(1)}, f32[8,128]{1,0:T(8,128)S(1)}) custom-call(s32[4]{0:T(128)S(1)} %pad_add_fusion.place_ref, f32[256,512]{1,0:T(8,128)S(1)} %get-tuple-element.24.local_out, f32[16,128]{1,0:T(8,128)S(1)} %get-tuple-element.25.local_stats, bf16[272,512]{1,0:T(8,128)(2,1)S(1)} %collective-permute-done.4.payload_in, ...), custom_call_target="tpu_custom_call" | custom-call | flops 800000000 | bytes 800000 | tf_op jit(solution)/shard_map/pallas_call | solution.py:336
  65.8 5.7 %psum.7.squares = f32[8,128]{1,0:T(8,128)S(1)} all-reduce(f32[8,128]{1,0:T(8,128)S(1)} %get-tuple-element.39), channel_id=1, replica_groups=mesh['stretch'=2,'cp'=4,'tp'=4] {'tp'}, use_global_device_ids=true, to_apply=%region_0.0 | all-reduce | flops 1024 | bytes 8192 | tf_op jit(solution)/shard_map/psum | solution.py:403
  71.5 0.0 copy-start.1
  71.5 0.0 copy-done
  71.5 0.6 copy-done.1
  72.1 1.7 %shard_map.72 = bf16[256,1536]{1,0:T(8,128)(2,1)} custom-call(s32[4]{0:T(128)S(1)} %pad_add_fusion.place_ref, s32[4]{0:T(128)S(1)} %copy-done.1, f32[8,128]{1,0:T(8,128)S(1)} %psum.7.squares, bf16[16,1536]{1,0:T(8,128)(2,1)S(1)} %copy-done, f32[256,512]{1,0:T(8,128)S(1)} %get-tuple-element.40.refs_0_, f32[256,512]{1,0:T(8,128)S(1)} %get-tuple-element.41.refs_1_, ...), custom_call_target="tpu_custom_call" | custom-call | tf_op jit(solution)/shard_map/pallas_call | solution.py:404
  (2 shorter events, 0.0 us)
Async XLA Ops:
  1.5 5.2 %copy-start.3 = (bf16[2,128,1536]{2,1,0:T(8,128)(2,1)S(1)}, bf16[2,128,1536]{2,1,0:T(8,128)(2,1)}, u32[]{:S(2)}) copy-start(bf16[2,128,1536]{2,1,0:T(8,128)(2,1)} %param.6) | copy-start | bytes 2359300
  1.5 23.9 %collective-permute-start.11 = (bf16[256,1024]{1,0:T(8,128)(2,1)S(1)}, bf16[256,1024]{1,0:T(8,128)(2,1)S(1)}, u32[]{:S(2)}, u32[]{:S(2)}) collective-permute-start(bf16[256,1024]{1,0:T(8,128)(2,1)S(1)} %pad_maximum_fusion.2.own_kv), channel_id=1, source_target_pairs={{0,4},{4,8},{8,12},{1,5},{5,9},{9,13},{2,6},{6,10},{10,14},{3,7},{... | collective-permute-start | bytes 1572872 | tf_op jit(solution)/shard_map/ppermute | solution.py:26
  6.7 9.8 %collective-permute-start.5 = (bf16[256,512]{1,0:T(8,128)(2,1)S(1)}, bf16[256,512]{1,0:T(8,128)(2,1)}, u32[]{:S(2)}, u32[]{:S(2)}) collective-permute-start(bf16[256,512]{1,0:T(8,128)(2,1)S(1)} %get-tuple-element.50.own_q), channel_id=1, source_target_pairs={{4,0},{8,4},{12,8},{5,1},{9,5},{13,9},{6,2},{10,6},{14,10},{7,3},{... | collective-permute-start | bytes 786440 | tf_op jit(solution)/shard_map/ppermute | solution.py:26
  8.1 18.7 %collective-permute-start.7 = (bf16[256,1024]{1,0:T(8,128)(2,1)S(1)}, bf16[256,1024]{1,0:T(8,128)(2,1)}, u32[]{:S(2)}, u32[]{:S(2)}) collective-permute-start(bf16[256,1024]{1,0:T(8,128)(2,1)S(1)} %pad_maximum_fusion.1.own_kv), channel_id=1, source_target_pairs={{0,16},{1,17},{2,18},{3,19},{4,20},{5,21},{6,22},{7,23},{8,24},{9,... | collective-permute-start | bytes 1572872 | tf_op jit(solution)/shard_map/ppermute | solution.py:26
  12.3 11.9 %collective-permute-start = (bf16[256,512]{1,0:T(8,128)(2,1)S(1)}, bf16[256,512]{1,0:T(8,128)(2,1)}, u32[]{:S(2)}, u32[]{:S(2)}) collective-permute-start(bf16[256,512]{1,0:T(8,128)(2,1)S(1)} %get-tuple-element.51.own_q), channel_id=1, source_target_pairs={{4,0},{8,4},{12,8},{5,1},{9,5},{13,9},{6,2},{10,6},{14,10},{7,3},{... | collective-permute-start | bytes 786440 | tf_op jit(solution)/shard_map/ppermute | solution.py:26
  16.5 14.9 %collective-permute-start.6 = (bf16[256,512]{1,0:T(8,128)(2,1)}, bf16[256,512]{1,0:T(8,128)(2,1)}, u32[]{:S(2)}, u32[]{:S(2)}) collective-permute-start(bf16[256,512]{1,0:T(8,128)(2,1)} %collective-permute-done.5.near_q), channel_id=1, source_target_pairs={{4,0},{8,4},{12,8},{5,1},{9,5},{13,9},{6,2},{10,6},{14,10},{7,3},{... | collective-permute-start | bytes 786440 | tf_op jit(solution)/shard_map/ppermute | solution.py:26
  17.8 13.5 %copy-start.2 = (s32[2,4,4,4]{3,2,1,0:T(4,128)S(1)}, s32[2,4,4,4]{3,2,1,0:T(4,128)}, u32[]{:S(2)}) copy-start(s32[2,4,4,4]{3,2,1,0:T(4,128)} %ranges_ref.5) | copy-start | bytes 1540
  17.8 21.2 %collective-permute-start.2 = (bf16[256,1024]{1,0:T(8,128)(2,1)S(1)}, bf16[256,1024]{1,0:T(8,128)(2,1)S(1)}, u32[]{:S(2)}, u32[]{:S(2)}) collective-permute-start(bf16[256,1024]{1,0:T(8,128)(2,1)S(1)} %pad_maximum_fusion.own_kv), channel_id=1, source_target_pairs={{0,16},{1,17},{2,18},{3,19},{4,20},{5,21},{6,22},{7,23},{8,24},{9,... | collective-permute-start | bytes 1572872 | tf_op jit(solution)/shard_map/ppermute | solution.py:26
  24.2 21.9 %collective-permute-start.10 = (bf16[256,512]{1,0:T(8,128)(2,1)S(1)}, bf16[256,512]{1,0:T(8,128)(2,1)S(1)}, u32[]{:S(2)}, u32[]{:S(2)}) collective-permute-start(bf16[256,512]{1,0:T(8,128)(2,1)S(1)} %get-tuple-element.49.own_q), channel_id=1, source_target_pairs={{16,0},{17,1},{18,2},{19,3},{20,4},{21,5},{22,6},{23,7},{24,8},{25... | collective-permute-start | bytes 786440 | tf_op jit(solution)/shard_map/ppermute | solution.py:26
  25.5 13.6 %collective-permute-start.1 = (bf16[256,512]{1,0:T(8,128)(2,1)}, bf16[256,512]{1,0:T(8,128)(2,1)S(1)}, u32[]{:S(2)}, u32[]{:S(2)}) collective-permute-start(bf16[256,512]{1,0:T(8,128)(2,1)} %collective-permute-done.near_q), channel_id=1, source_target_pairs={{4,0},{8,4},{12,8},{5,1},{9,5},{13,9},{6,2},{10,6},{14,10},{7,3},{... | collective-permute-start | bytes 786440 | tf_op jit(solution)/shard_map/ppermute | solution.py:26
  26.8 19.3 %collective-permute-start.12 = (bf16[256,1024]{1,0:T(8,128)(2,1)S(1)}, bf16[256,1024]{1,0:T(8,128)(2,1)S(1)}, u32[]{:S(2)}, u32[]{:S(2)}) collective-permute-start(bf16[256,1024]{1,0:T(8,128)(2,1)S(1)} %collective-permute-done.11.near_kv), channel_id=1, source_target_pairs={{0,4},{4,8},{8,12},{1,5},{5,9},{9,13},{2,6},{6,10},{10,14},{3,7},{... | collective-permute-start | bytes 1572872 | tf_op jit(solution)/shard_map/ppermute | solution.py:26
  35.1 19.1 %collective-permute-start.8 = (bf16[272,512]{1,0:T(8,128)(2,1)S(1)}, bf16[272,512]{1,0:T(8,128)(2,1)S(1)}, u32[]{:S(2)}, u32[]{:S(2)}) collective-permute-start(bf16[272,512]{1,0:T(8,128)(2,1)S(1)} %get-tuple-element.33), channel_id=1, source_target_pairs={{0,4},{4,8},{8,12},{1,5},{5,9},{9,13},{2,6},{6,10},{10,14},{3,7},{... | collective-permute-start | bytes 835592 | tf_op jit(solution)/shard_map/ppermute | solution.py:26
  42.5 14.3 %collective-permute-start.3 = (bf16[272,512]{1,0:T(8,128)(2,1)S(1)}, bf16[272,512]{1,0:T(8,128)(2,1)S(1)}, u32[]{:S(2)}, u32[]{:S(2)}) collective-permute-start(bf16[272,512]{1,0:T(8,128)(2,1)S(1)} %get-tuple-element.28), channel_id=1, source_target_pairs={{0,4},{4,8},{8,12},{1,5},{5,9},{9,13},{2,6},{6,10},{10,14},{3,7},{... | collective-permute-start | bytes 835592 | tf_op jit(solution)/shard_map/ppermute | solution.py:26
  49.6 10.6 %collective-permute-start.13 = (bf16[272,512]{1,0:T(8,128)(2,1)S(1)}, bf16[272,512]{1,0:T(8,128)(2,1)S(1)}, u32[]{:S(2)}, u32[]{:S(2)}) collective-permute-start(bf16[272,512]{1,0:T(8,128)(2,1)S(1)} %get-tuple-element.36), channel_id=1, source_target_pairs={{0,16},{1,17},{2,18},{3,19},{4,20},{5,21},{6,22},{7,23},{8,24},{9,... | collective-permute-start | bytes 835592 | tf_op jit(solution)/shard_map/ppermute | solution.py:26
  54.9 7.1 %collective-permute-start.9 = (bf16[272,512]{1,0:T(8,128)(2,1)S(1)}, bf16[272,512]{1,0:T(8,128)(2,1)S(1)}, u32[]{:S(2)}, u32[]{:S(2)}) collective-permute-start(bf16[272,512]{1,0:T(8,128)(2,1)S(1)} %shard_map.67), channel_id=1, source_target_pairs={{0,4},{4,8},{8,12},{1,5},{5,9},{9,13},{2,6},{6,10},{10,14},{3,7},{... | collective-permute-start | bytes 835592 | tf_op jit(solution)/shard_map/ppermute | solution.py:26
  57.5 7.5 %collective-permute-start.4 = (bf16[272,512]{1,0:T(8,128)(2,1)S(1)}, bf16[272,512]{1,0:T(8,128)(2,1)S(1)}, u32[]{:S(2)}, u32[]{:S(2)}) collective-permute-start(bf16[272,512]{1,0:T(8,128)(2,1)S(1)} %shard_map.65), channel_id=1, source_target_pairs={{0,4},{4,8},{8,12},{1,5},{5,9},{9,13},{2,6},{6,10},{10,14},{3,7},{... | collective-permute-start | bytes 835592 | tf_op jit(solution)/shard_map/ppermute | solution.py:26
  65.0 6.5 %copy-start = (bf16[16,1536]{1,0:T(8,128)(2,1)S(1)}, bf16[16,1536]{1,0:T(8,128)(2,1)}, u32[]{:S(2)}) copy-start(bf16[16,1536]{1,0:T(8,128)(2,1)} %gate_table.1) | copy-start | bytes 147460
  71.5 0.7 copy-start.1

commit v2 on v1

--- a/solution.py
+++ b/solution.py
@@ -12,18 +12,43 @@
 HEAD_DIM = 128
 BLOCK = 128
 REACH = 2
-CHUNKS = (4, 4)
+CHUNKS = (5, 3)
 KEYS_MOVED = 4
 FINISH_ORDER = (2, 0, 1)
+WRAP = True
+NEAR_COST = (3.0, 1.8)
+FAR_COST = (1.5, 0.9)
+KEYS_COST = 2.0
+PACK_LIMIT = 49 * 1024 * 1024
 STAT_ROWS = 16
 HIDDEN = -1e30
 EXPONENT_SCALE = math.log2(math.e) / math.sqrt(HEAD_DIM)
 
 
-def moved(block, axis, distance):
-    devices = range(lax.axis_size(axis))
-    route = [(i - distance, i) for i in devices if i - distance in devices]
-    return lax.ppermute(block, axis, route)
+def exchanged(block):
+    return lax.ppermute(block, "stretch", [(0, 1), (1, 0)])
+
+
+def goes_up():
+    return lax.axis_index("tp") < lax.axis_size("tp") // 2
+
+
+def round_trip(block, forward):
+    count, half = lax.axis_size("cp"), lax.axis_size("tp") // 2
+    route = []
+    for lane in range(half):
+        cycle = [i * 2 * half + lane for i in range(count)]
+        cycle += [i * 2 * half + half + lane for i in reversed(range(count))]
+        route += zip(cycle, cycle[1:] + cycle[:1])
+    if not forward:
+        route = [(target, source) for source, target in route]
+    return lax.ppermute(block, ("cp", "tp"), route)
+
+
+def passed_up(block):
+    count = lax.axis_size("cp")
+    route = [(i, (i + 1) % count) for i in range(count if WRAP else count - 1)]
+    return lax.ppermute(block, "cp", route)
 
 
 def head_columns(head):
@@ -98,84 +123,153 @@
     return summed * (1.0 / total), jnp.maximum(shift + jnp.log2(total), HIDDEN)
 
 
-def keys_and_values(refs, head, head_count):
-    columns = head_columns(head)
-    value_columns = head_columns(head_count + head)
-    keys = jnp.concatenate([ref[:, columns] for ref in refs], axis=0)
-    values = jnp.concatenate([ref[:, value_columns] for ref in refs], axis=0)
+def pick(up, refs, *index):
+    return jnp.where(up, refs[0][index], refs[1][index])
+
+
+def pack_kernel(counts, keys_moved, place_ref, q_hbm, k_hbm, v_hbm, *refs):
+    base = sum(counts)
+    q_ref, k_ref, v_ref = refs[:3]
+    outs, semaphores = refs[3:-1], refs[-1]
+    copies = [
+        pltpu.make_async_copy(source, target, semaphores.at[index])
+        for index, (source, target) in enumerate(
+            ((q_hbm, q_ref), (k_hbm, k_ref), (v_hbm, v_ref))
+        )
+    ]
+    for copy in copies:
+        copy.start()
+    for copy in copies:
+        copy.wait()
+    columns = [head_columns(head) for head in range(base + keys_moved)]
+    moving = [(ref, part) for ref in (k_ref, v_ref) for part in columns[base:]]
+    start = 0
+    up = place_ref[4] == 1
+
+    def fill(out, parts):
+        for index, (ref, part) in enumerate(parts):
+            out[:, head_columns(index)] = ref[:, part]
+
+    for i, count in enumerate(counts):
+        cross_out, forward_out, backward_out = outs[3 * i : 3 * i + 3]
+        own = columns[start : start + count]
+        queries = [(q_ref, part) for part in own]
+        keys = moving[start : start + count]
+        crossing = [(ref, part) for ref in (k_ref, v_ref) for part in own]
+
+        @pl.when(up)
+        def _():
+            fill(forward_out, keys)
+            fill(backward_out, queries)
+
+        @pl.when(jnp.logical_not(up))
+        def _():
+            fill(forward_out, queries)
+            fill(backward_out, keys)
+
+        fill(cross_out, crossing)
+        if i == 0:
+
+            @pl.when(place_ref[0] > 0)
+            def _():
+                fill(cross_out, [(q_ref, part) for part in columns[base:]])
+
+        start += count
+
+
+def crossing_keys(own_k, own_v, prior_kv, base, head, head_count):
+    own_columns = head_columns(base + head)
+    keys = jnp.concatenate([own_k[:, own_columns], prior_kv[:, head_columns(head)]], axis=0)
+    values = jnp.concatenate(
+        [own_v[:, own_columns], prior_kv[:, head_columns(head_count + head)]], axis=0
+    )
     return keys, jnp.transpose(values)
 
 
-def queries_moved_kernel(
-    head_count,
-    place_ref,
-    ranges_ref,
-    own_q,
-    near_q,
-    far_q,
-    own_kv,
-    prior_kv,
-    *rest,
-    pair_count,
+def crossing_flags(place_ref, ranges_ref, distance, slot, pair_count):
+    group, position = place_ref[0], place_ref[1]
+    return [
+        shown(
+            place_ref,
+            ranges_ref,
+            group * pair_count + slot,
+            position + distance,
+            (group - behind) * pair_count + key_slot,
+            position,
+        )
+        for behind in range(2)
+        for key_slot in range(pair_count)
+    ]
+
+
+def far_kernel(
+    head_count, place_ref, ranges_ref, own_k, own_v, forward_q, backward_q, prior_kv, *rest,
+    base, pair_count,
 ):
-    own_out, own_stats, near_out, near_stats, far_payload = rest[-5:]
-    group, position = place_ref[0], place_ref[1]
-    token_rows = pair_count * BLOCK
+    far_payload, far_stats = rest[-2:]
+    up = place_ref[4] == 1
+    seen = [crossing_flags(place_ref, ranges_ref, 2, slot, pair_count) for slot in range(pair_count)]
+    stats = [jnp.zeros((1, BLOCK), jnp.float32)] * STAT_ROWS
+    for head in range(head_count):
+        columns = head_columns(head)
+        keys, values = crossing_keys(own_k, own_v, prior_kv, base, head, head_count)
+        for slot in range(pair_count):
+            rows = stretch_rows(slot)
+            query = pick(up, (backward_q, forward_q), rows, columns)
+            attended, stats[slot * head_count + head] = attend(query, keys, values, seen[slot])
+            far_payload[rows, columns] = attended.astype(jnp.bfloat16)
+    far_stats[...] = jnp.concatenate(stats, axis=0)
+    put_stats(far_payload, far_stats[...], pair_count * BLOCK)
+
+
+def near_kernel(
+    head_count, place_ref, ranges_ref, own_q, own_k, own_v, forward_q, backward_q, prior_kv,
+    *rest, base, pair_count,
+):
+    own_out, own_stats, near_out, near_stats = rest[-4:]
+    up = place_ref[4] == 1
     seen = {
-        (distance, slot): [
-            shown(
-                place_ref,
-                ranges_ref,
-                group * pair_count + slot,
-                position + distance,
-                (group - 1) * pair_count + key_slot,
-                position,
-            )
-            for key_slot in range(2 * pair_count)
-        ]
-        for distance in range(REACH + 1)
+        (distance, slot): crossing_flags(place_ref, ranges_ref, distance, slot, pair_count)
+        for distance in range(2)
         for slot in range(pair_count)
     }
     own_stats[...] = jnp.zeros_like(own_stats)
     near_stats[...] = jnp.zeros_like(near_stats)
-    far_stats = [jnp.zeros((1, BLOCK), jnp.float32)] * STAT_ROWS
     for head in range(head_count):
         columns = head_columns(head)
-        keys, values = keys_and_values((prior_kv, own_kv), head, head_count)
-        for distance, query_ref in ((2, far_q), (1, near_q), (0, own_q)):
-            for slot in range(pair_count):
-                rows = stretch_rows(slot)
-                attended, log_total = attend(
-                    query_ref[rows, columns], keys, values, seen[distance, slot]
-                )
-                index = slot * head_count + head
-                if distance == 0:
-                    own_out[rows, columns] = attended
-                    own_stats[index : index + 1, :] = log_total
-                elif distance == 1:
-                    near_out[rows, columns] = attended
-                    near_stats[index : index + 1, :] = log_total
-                else:
-                    far_payload[rows, columns] = attended.astype(jnp.bfloat16)
-                    far_stats[index] = log_total
-    put_stats(far_payload, jnp.concatenate(far_stats, axis=0), token_rows)
+        keys, values = crossing_keys(own_k, own_v, prior_kv, base, head, head_count)
+        for slot in range(pair_count):
+            rows = stretch_rows(slot)
+            index = slot * head_count + head
+            query = pick(up, (backward_q, forward_q), rows, columns)
+            near_out[rows, columns], near_stats[index : index + 1, :] = attend(
+                query, keys, values, seen[1, slot]
+            )
+            query = own_q[rows, head_columns(base + head)]
+            own_out[rows, columns], own_stats[index : index + 1, :] = attend(
+                query, keys, values, seen[0, slot]
+            )
 
 
 def keys_moved_kernel(
-    head_count,
-    place_ref,
-    ranges_ref,
-    own_q,
-    next_q,
-    own_kv,
-    near_kv,
-    far_kv,
-    *rest,
-    pair_count,
+    head_count, place_ref, ranges_ref, own_q, own_k, own_v, next_q, *rest, base, pair_count, counts
 ):
     own_out, own_stats, next_payload = rest[-3:]
     group, position = place_ref[0], place_ref[1]
-    token_rows = pair_count * BLOCK
+    up = place_ref[4] == 1
+    parts = len(counts)
+    came = [
+        [rest[2 * (hop * parts + part) : 2 * (hop * parts + part) + 2] for part in range(parts)]
+        for hop in range(REACH)
+    ]
+
+    def moved_block(hop, unit):
+        part = 0
+        while unit >= counts[part]:
+            unit -= counts[part]
+            part += 1
+        return pick(up, came[hop][part], slice(None), head_columns(unit))
+
     seen = {
         (ahead, slot): [
             shown(
@@ -195,22 +289,28 @@
     own_stats[...] = jnp.zeros_like(own_stats)
     next_stats = [jnp.zeros((1, BLOCK), jnp.float32)] * STAT_ROWS
     for head in range(head_count):
-        columns = head_columns(head)
-        keys, values = keys_and_values((own_kv, near_kv, far_kv), head, head_count)
-        for ahead, query_ref in ((1, next_q), (0, own_q)):
-            for slot in range(pair_count):
-                rows = stretch_rows(slot)
-                attended, log_total = attend(
-                    query_ref[rows, columns], keys, values, seen[ahead, slot]
-                )
-                index = slot * head_count + head
-                if ahead:
-                    next_payload[rows, columns] = attended.astype(jnp.bfloat16)
-                    next_stats[index] = log_total
-                else:
-                    own_out[rows, columns] = attended
-                    own_stats[index : index + 1, :] = log_total
-    put_stats(next_payload, jnp.concatenate(next_stats, axis=0), token_rows)
+        columns, own_columns = head_columns(head), head_columns(base + head)
+        keys = jnp.concatenate(
+            [own_k[:, own_columns]] + [moved_block(hop, head) for hop in range(REACH)], axis=0
+        )
+        values = jnp.transpose(
+            jnp.concatenate(
+                [own_v[:, own_columns]]
+                + [moved_block(hop, head_count + head) for hop in range(REACH)],
+                axis=0,
+            )
+        )
+        for slot in range(pair_count):
+            rows = stretch_rows(slot)
+            index = slot * head_count + head
+            attended, next_stats[index] = attend(
+                next_q[rows, columns], keys, values, seen[1, slot]
+            )
+            next_payload[rows, columns] = attended.astype(jnp.bfloat16)
+            own_out[rows, columns], own_stats[index : index + 1, :] = attend(
+                own_q[rows, own_columns], keys, values, seen[0, slot]
+            )
+    put_stats(next_payload, jnp.concatenate(next_stats, axis=0), pair_count * BLOCK)
 
 
 def joined(sender_index, local_out, local_stats, payload_ref, head_count):
@@ -240,10 +340,11 @@
 def relay_kernel(
     head_count, place_ref, local_out, local_stats, payload_in, *rest, axis
 ):
-    payload_out = rest[-1]
+    payload_out, stats_out = rest[-2:]
     parts, log_total = joined(place_ref[axis], local_out, local_stats, payload_in, head_count)
     for (slot, head), part in parts.items():
         payload_out[stretch_rows(slot), head_columns(head)] = part.astype(jnp.bfloat16)
+    stats_out[...] = log_total
     put_stats(payload_out, log_total, local_out.shape[0])
 
 
@@ -305,24 +406,20 @@
             lax.axis_index("cp"),
             jnp.int32(kv_ranges.shape[1]),
             jnp.int32(kv_ranges.shape[2]),
+            goes_up(),
         ]
     ).astype(jnp.int32)
     queries, keys, values = (
         array.reshape(token_rows, width_dev) for array in (query_rows, key_rows, value_rows)
     )
     head_counts = CHUNKS + (KEYS_MOVED,)
-    assert sum(head_counts) == head_total
-    starts = [sum(head_counts[:i]) * HEAD_DIM for i in range(len(head_counts))]
+    assert sum(head_counts) == head_total and 2 * KEYS_MOVED == sum(CHUNKS)
+    assert lax.axis_size("stretch") == 2
+    bases = [sum(head_counts[:i]) for i in range(len(head_counts))]
     widths = [count * HEAD_DIM for count in head_counts]
     chunks = range(len(CHUNKS))
     last = len(CHUNKS)
 
-    def cut(array, chunk):
-        return lax.slice_in_dim(array, starts[chunk], starts[chunk] + widths[chunk], axis=1)
-
-    def cut_kv(chunk):
-        return jnp.concatenate([cut(keys, chunk), cut(values, chunk)], axis=1)
-
     def float_shape(chunk):
         return jax.ShapeDtypeStruct((token_rows, widths[chunk]), jnp.float32)
 
@@ -332,7 +429,7 @@
     stats_shape = jax.ShapeDtypeStruct((STAT_ROWS, BLOCK), jnp.float32)
     squares_shape = jax.ShapeDtypeStruct((8, BLOCK), jnp.float32)
 
-    def run(kernel, chunk, microseconds, out_shape, smem, vmem, after=()):
+    def run(name, kernel, chunk, microseconds, out_shape, smem, vmem, after=()):
         return pl.pallas_call(
             functools.partial(kernel, head_counts[chunk]),
             out_shape=out_shape,
@@ -342,63 +439,100 @@
             out_specs=(VMEM,) * len(out_shape),
             compiler_params=PARAMS,
             cost_estimate=cost(microseconds),
+            name=name,
         )(*smem, *vmem, *after)
 
-    own_q = [cut(queries, i) for i in chunks]
-    own_kv = [cut_kv(i) for i in chunks]
-    near_q = [moved(own_q[i], "cp", -1) for i in chunks]
-    first_q = cut(queries, last)
-    first_kv = cut_kv(last)
-    near_kv = moved(first_kv, "cp", 1)
-    next_q = moved(first_q, "stretch", -1)
-    prior_kv = [moved(own_kv[i], "stretch", 1) for i in chunks]
-    far_q = [moved(near_q[i], "cp", -1) for i in chunks]
-    far_kv = moved(near_kv, "cp", 1)
+    def block_shape(units):
+        return jax.ShapeDtypeStruct((token_rows, units * HEAD_DIM), jnp.bfloat16)
+
+    packed = pl.pallas_call(
+        functools.partial(pack_kernel, CHUNKS, KEYS_MOVED),
+        out_shape=(block_shape(head_total),) * 3
+        + tuple(block_shape(units) for count in CHUNKS for units in (2 * count, count, count)),
+        in_specs=[SMEM] + [pl.BlockSpec(memory_space=pltpu.HBM)] * 3,
+        out_specs=(VMEM,) * (3 + 3 * len(CHUNKS)),
+        scratch_shapes=[pltpu.SemaphoreType.DMA((3,))],
+        compiler_params=pltpu.CompilerParams(vmem_limit_bytes=PACK_LIMIT),
+        cost_estimate=cost(1.0),
+        name="pack",
+    )(place, queries, keys, values)
+    queries, keys, values = packed[:3]
+    prior_kv, hops = [], [[], []]
+    for i in chunks:
+        crossing, forward, backward = packed[3 * i + 3 : 3 * i + 6]
+        prior_kv.append(exchanged(crossing))
+        hops[0].append((round_trip(forward, True), round_trip(backward, False)))
+    for i in chunks:
+        forward, backward = hops[0][i]
+        hops[1].append((round_trip(forward, True), round_trip(backward, False)))
 
     own_parts, near_parts, arrived = [], [], []
+    turn = ()
     for i in chunks:
-        own_out, own_stats, near_out, near_stats, far_payload = run(
-            functools.partial(queries_moved_kernel, pair_count=pair_count),
+        near = run(
+            "near",
+            functools.partial(near_kernel, base=bases[i], pair_count=pair_count),
             i,
-            1.0 * head_counts[i],
-            (float_shape(i), stats_shape, float_shape(i), stats_shape, payload_shape(i)),
+            NEAR_COST[i],
+            (float_shape(i), stats_shape) * 2,
             (place, kv_ranges),
-            (own_q[i], near_q[i], far_q[i], own_kv[i], prior_kv[i]),
-        )
-        own_parts.append((own_out, own_stats))
-        near_parts.append((near_out, near_stats))
-        arrived.append(moved(far_payload, "cp", 1))
+            (queries, keys, values, *hops[0][i], prior_kv[i]),
+            turn,
+        )
+        own_parts.append(near[:2])
+        near_parts.append(near[2:])
+        far_payload, far_stats = run(
+            "far",
+            functools.partial(far_kernel, base=bases[i], pair_count=pair_count),
+            i,
+            FAR_COST[i],
+            (payload_shape(i), stats_shape),
+            (place, kv_ranges),
+            (keys, values, *hops[1][i], prior_kv[i]),
+            (near[1],),
+        )
+        turn = (far_stats,)
+        arrived.append(passed_up(far_payload))
     own_out, own_stats, next_payload = run(
-        functools.partial(keys_moved_kernel, pair_count=pair_count),
+        "keys_moved",
+        functools.partial(
+            keys_moved_kernel, base=bases[last], pair_count=pair_count, counts=CHUNKS
+        ),
         last,
-        1.0 * head_counts[last],
+        KEYS_COST,
         (float_shape(last), stats_shape, payload_shape(last)),
         (place, kv_ranges),
-        (first_q, next_q, first_kv, near_kv, far_kv),
+        (queries, keys, values, prior_kv[0], *[ref for hop in hops for pair in hop for ref in pair]),
+        turn,
     )
     own_parts.append((own_out, own_stats))
-    prior_payload = moved(next_payload, "stretch", 1)
+    turn = (own_stats,)
+    arrived.append(exchanged(next_payload))
     for i in chunks:
-        (relayed,) = run(
+        relayed, relayed_stats = run(
+            "relay",
             functools.partial(relay_kernel, axis=1),
             i,
             0.7,
-            (payload_shape(i),),
+            (payload_shape(i), stats_shape),
             (place,),
             (*near_parts[i], arrived[i]),
-        )
-        arrived[i] = moved(relayed, "cp", 1)
-    arrived.append(prior_payload)
+            turn,
+        )
+        turn = (relayed_stats,)
+        arrived[i] = passed_up(relayed)
     squares = jnp.zeros(squares_shape.shape, jnp.float32)
     finished = [None] * len(head_counts)
     for i in FINISH_ORDER:
         finished[i], squares = run(
+            "finish",
             functools.partial(finish_kernel, axis=0 if i == last else 1),
             i,
             0.8,
             (float_shape(i), squares_shape),
             (place,),
             (*own_parts[i], arrived[i], squares),
+            turn,
         )
     squares = lax.psum(squares, "tp")
     out = pl.pallas_call(

time: 74.4 us -> 66.4 us (0.89)
  starting transfers between devices: 41.8 us -> 16.5 us
  waiting for transfers between devices: 7.42 us -> 22.1 us
  Pallas kernels: 16.2 us -> 21 us
  local copies, waits for them, and re-layouts: 2.19 us -> 0.66 us
    ppermute x14 -> x15, starting transfers between devices: 41.8 us -> 16.5 us  [the longest x8 8.1 us: round_trip(): return lax.ppermute(block, ('cp', 'tp'), route)]
    ppermute x14 -> x15, waiting for transfers between devices: 7.42 us -> 22.1 us  [the longest x8 12.3 us: round_trip(): return lax.ppermute(block, ('cp', 'tp'), route)]
    pallas_call x8 -> x10, Pallas kernels: 14.5 us -> 16.9 us  [run(): pl.pallas_call(functools.partial(kernel, head_counts[chunk]), out_shape=o...]
    pallas_call x0 -> x1, Pallas kernels: none -> 2.37 us  [on_device(): pl.pallas_call(functools.partial(pack_kernel, CHUNKS, KEYS_MOVED), out_sh...]
    slice x2 -> x0, local copies, waits for them, and re-layouts: 1.52 us -> none  [cut(): lax.slice_in_dim(array, starts[chunk], starts[chunk] + widths[chunk], axi...]
  transfers between devices with their start and end apart: 14 -> 15, of which waited for: 4 -> 10; matrix products, arithmetic and copies ran while one was open for 0% -> 0% of each run, Pallas kernels for 19% -> 24%
where the time goes in v2:
time: 66.4 us; the launch traced here: 66.2 us
  waiting for transfers between devices  22.1 us (33%)
  Pallas kernels  21 us (32%)
  starting transfers between devices  16.5 us (25%)
  blocking collectives  5.77 us (9%)
    pallas_call x10, Pallas kernels, run(): pl.pallas_call(functools.partial(kernel, head_counts[chunk]), out_shape=o...  16.9 us
    ppermute x8, waiting for transfers between devices, round_trip(): return lax.ppermute(block, ('cp', 'tp'), route)  12.3 us
    ppermute x8, starting transfers between devices, round_trip(): return lax.ppermute(block, ('cp', 'tp'), route)  8.1 us
    ppermute x4, waiting for transfers between devices, passed_up(): return lax.ppermute(block, 'cp', route)  8.1 us
    psum x1, blocking collectives, on_device(): squares = lax.psum(squares, 'tp')  5.77 us
    ppermute x4, starting transfers between devices, passed_up(): return lax.ppermute(block, 'cp', route)  4.81 us
    ppermute x3, starting transfers between devices, exchanged(): return lax.ppermute(block, 'stretch', [(0, 1), (1, 0)])  3.63 us
    pallas_call x1, Pallas kernels, on_device(): pl.pallas_call(functools.partial(pack_kernel, CHUNKS, KEYS_MOVED), out_sh...  2.37 us
  transfers between devices with their start and end apart: 15, of which 10 were waited for; matrix products, arithmetic and copies ran while one was open for 0% of the time, Pallas kernels for 24%

profile of v2, /device:TPU:0, one launch (start us, length us, event | category | flops | bytes accessed | tf_op | source)
XLA Modules:
  0.0 66.2 jit_solution(4730284855542985225)
XLA Ops:
  0.0 0.1 pad_add_fusion.place_ref
  0.1 2.4 %pack.1 = (bf16[256,1536]{1,0:T(8,128)(2,1)S(1)}, bf16[256,1536]{1,0:T(8,128)(2,1)S(1)}, bf16[256,1536]{1,0:T(8,128)(2,1)S(1)}, bf16[256,1280]{1,0:T(8,128)(2,1)...) custom-call(s32[5]{0:T(128)S(1)} %pad_add_fusion.place_ref, ...), custom_call_target="tpu_custom_call" | custom-call | flops 1000000000 | bytes 1000000 | tf_op jit(solution)/shard_map/pack/pallas_call | solution.py:448
  2.5 0.0 copy-start.2
  2.5 3.0 %collective-permute-start.7 = (bf16[256,1280]{1,0:T(8,128)(2,1)S(1)}, bf16[256,1280]{1,0:T(8,128)(2,1)S(1)}, u32[]{:S(2)}, u32[]{:S(2)}) collective-permute-start(bf16[256,1280]{1,0:T(8,128)(2,1)S(1)} %get-tuple-element.47), channel_id=1, source_target_pairs={{0,16},{16,0},{1,17},{17,1},{2,18},{18,2},{3,19},{19,3},{4,20},{20... | collective-permute-start | bytes 1966088 | tf_op jit(solution)/shard_map/ppermute | solution.py:29
  5.5 1.6 %collective-permute-start.3 = (bf16[256,640]{1,0:T(8,128)(2,1)S(1)}, bf16[256,640]{1,0:T(8,128)(2,1)S(1)}, u32[]{:S(2)}, u32[]{:S(2)}) collective-permute-start(bf16[256,640]{1,0:T(8,128)(2,1)S(1)} %get-tuple-element.45), channel_id=1, source_target_pairs={{0,4},{4,8},{8,12},{12,14},{14,10},{10,6},{6,2},{2,0},{1,5},{5,9},... | collective-permute-start | bytes 983048 | tf_op jit(solution)/shard_map/ppermute | solution.py:45
  7.1 0.4 collective-permute-start.5
  7.5 1.6 %collective-permute-start = (bf16[256,384]{1,0:T(8,128)(2,1)S(1)}, bf16[256,384]{1,0:T(8,128)(2,1)S(1)}, u32[]{:S(2)}, u32[]{:S(2)}) collective-permute-start(bf16[256,384]{1,0:T(8,128)(2,1)S(1)} %get-tuple-element.42), channel_id=1, source_target_pairs={{0,4},{4,8},{8,12},{12,14},{14,10},{10,6},{6,2},{2,0},{1,5},{5,9},... | collective-permute-start | bytes 589832 | tf_op jit(solution)/shard_map/ppermute | solution.py:45
  9.1 0.4 collective-permute-start.1
  9.5 6.6 %collective-permute-done.3.forward_q.rest_0_ = bf16[256,640]{1,0:T(8,128)(2,1)S(1)} collective-permute-done((bf16[256,640]{1,0:T(8,128)(2,1)S(1)}, bf16[256,640]{1,0:T(8,128)(2,1)S(1)}, u32[]{:S(2)}, u32[]{:S(2)}) %collective-permute-start.3) | collective-permute-done | bytes 327712 | tf_op jit(solution)/shard_map/ppermute | solution.py:45
  16.1 1.6 %collective-permute-start.4 = (bf16[256,640]{1,0:T(8,128)(2,1)S(1)}, bf16[256,640]{1,0:T(8,128)(2,1)S(1)}, u32[]{:S(2)}, u32[]{:S(2)}) collective-permute-start(bf16[256,640]{1,0:T(8,128)(2,1)S(1)} %collective-permute-done.3.forward_q.rest_0_), channel_id=1, source_target_pairs={{0,4},{4,8},{8,12},{12,14},{14,10},{10,6},{6,2},{2,0},{1,5},{5,9},... | collective-permute-start | bytes 983048 | tf_op jit(solution)/shard_map/ppermute | solution.py:45
  17.7 0.0 collective-permute-done.5.backward_q.rest_1_
  17.7 0.4 collective-permute-start.6
  18.2 2.2 %collective-permute-done.forward_q.rest_2_ = bf16[256,384]{1,0:T(8,128)(2,1)S(1)} collective-permute-done((bf16[256,384]{1,0:T(8,128)(2,1)S(1)}, bf16[256,384]{1,0:T(8,128)(2,1)S(1)}, u32[]{:S(2)}, u32[]{:S(2)}) %collective-permute-start) | collective-permute-done | bytes 196640 | tf_op jit(solution)/shard_map/ppermute | solution.py:45
  20.3 0.0 collective-permute-start.2
  20.4 1.6 %collective-permute-done.1.backward_q.rest_3_ = bf16[256,384]{1,0:T(8,128)(2,1)S(1)} collective-permute-done((bf16[256,384]{1,0:T(8,128)(2,1)S(1)}, bf16[256,384]{1,0:T(8,128)(2,1)S(1)}, u32[]{:S(2)}, u32[]{:S(2)}) %collective-permute-start.1) | collective-permute-done | bytes 196640 | tf_op jit(solution)/shard_map/ppermute | solution.py:45
  21.9 1.6 %collective-permute-start.8 = (bf16[256,384]{1,0:T(8,128)(2,1)S(1)}, bf16[256,384]{1,0:T(8,128)(2,1)S(1)}, u32[]{:S(2)}, u32[]{:S(2)}) collective-permute-start(bf16[256,384]{1,0:T(8,128)(2,1)S(1)} %collective-permute-done.forward_q.rest_2_), channel_id=1, source_target_pairs={{0,4},{4,8},{8,12},{12,14},{14,10},{10,6},{6,2},{2,0},{1,5},{5,9},... | collective-permute-start | bytes 589832 | tf_op jit(solution)/shard_map/ppermute | solution.py:45
  23.5 0.0 collective-permute-done.7.prior_kv.next_q
  23.5 0.5 collective-permute-start.9
  24.0 0.0 copy-done.2
  24.0 3.0 %near.2 = (f32[256,640]{1,0:T(8,128)S(1)}, f32[16,128]{1,0:T(8,128)S(1)}, f32[256,640]{1,0:T(8,128)S(1)}, f32[16,128]{1,0:T(8,128)S(1)}) custom-call(s32[5]{0:T(128)S(1)} %pad_add_fusion.place_ref, s32[2,4,4,4]{3,2,1,0:T(4,128)S(1)} %copy-done.2, bf16[256,1536]{1,0:T(8,128)(2,1)S(1)} %get-tuple-element.39.own_q, ...), custom_call_target="tpu_custom_call" | custom-call | flops 3000000000 | bytes 3000000 | tf_op jit(solution)/shard_map/near/pallas_call | solution.py:433
  27.0 0.4 collective-permute-done.4.forward_q.rest_4_
  27.4 1.6 %collective-permute-done.6.backward_q.rest_5_ = bf16[256,640]{1,0:T(8,128)(2,1)S(1)} collective-permute-done((bf16[256,640]{1,0:T(8,128)(2,1)S(1)}, bf16[256,640]{1,0:T(8,128)(2,1)S(1)}, u32[]{:S(2)}, u32[]{:S(2)}) %collective-permute-start.6) | collective-permute-done | bytes 327712 | tf_op jit(solution)/shard_map/ppermute | solution.py:45
  29.0 2.2 %far.2 = (bf16[272,640]{1,0:T(8,128)(2,1)S(1)}, f32[16,128]{1,0:T(8,128)S(1)}) custom-call(s32[5]{0:T(128)S(1)} %pad_add_fusion.place_ref, s32[2,4,4,4]{3,2,1,0:T(4,128)S(1)} %copy-done.2, bf16[256,1536]{1,0:T(8,128)(2,1)S(1)} %get-tuple-element.40.own_k, bf16[256,1536]{1,0:T(8,128)(2,1)S(1)} %get-tuple-element.41.own_v, ...), custom_call_target="tpu_custom_call" | custom-call | flops 1500000000 | bytes 1500000 | tf_op jit(solution)/shard_map/far/pallas_call | solution.py:433
  31.2 1.6 %collective-permute-start.11 = (bf16[272,640]{1,0:T(8,128)(2,1)S(1)}, bf16[272,640]{1,0:T(8,128)(2,1)S(1)}, u32[]{:S(2)}, u32[]{:S(2)}) collective-permute-start(bf16[272,640]{1,0:T(8,128)(2,1)S(1)} %get-tuple-element.57), channel_id=1, source_target_pairs={{0,4},{4,8},{8,12},{12,0},{1,5},{5,9},{9,13},{13,1},{2,6},{6,10},{... | collective-permute-start | bytes 1044488 | tf_op jit(solution)/shard_map/ppermute | solution.py:51
  32.8 0.0 collective-permute-done.2.prior_kv
  32.8 2.3 %near.3 = (f32[256,384]{1,0:T(8,128)S(1)}, f32[16,128]{1,0:T(8,128)S(1)}, f32[256,384]{1,0:T(8,128)S(1)}, f32[16,128]{1,0:T(8,128)S(1)}) custom-call(s32[5]{0:T(128)S(1)} %pad_add_fusion.place_ref, s32[2,4,4,4]{3,2,1,0:T(4,128)S(1)} %copy-done.2, bf16[256,1536]{1,0:T(8,128)(2,1)S(1)} %get-tuple-element.39.own_q, ...), custom_call_target="tpu_custom_call" | custom-call | flops 1800000000 | bytes 1800000 | tf_op jit(solution)/shard_map/near/pallas_call | solution.py:433
  35.2 0.0 collective-permute-done.8.forward_q.rest_6_
  35.2 0.0 collective-permute-done.9.backward_q.rest_7_
  35.2 1.9 %far.3 = (bf16[272,384]{1,0:T(8,128)(2,1)S(1)}, f32[16,128]{1,0:T(8,128)S(1)}) custom-call(s32[5]{0:T(128)S(1)} %pad_add_fusion.place_ref, s32[2,4,4,4]{3,2,1,0:T(4,128)S(1)} %copy-done.2, bf16[256,1536]{1,0:T(8,128)(2,1)S(1)} %get-tuple-element.40.own_k, bf16[256,1536]{1,0:T(8,128)(2,1)S(1)} %get-tuple-element.41.own_v, ...), custom_call_target="tpu_custom_call" | custom-call | flops 900000000 | bytes 900000 | tf_op jit(solution)/shard_map/far/pallas_call | solution.py:433
  37.1 1.6 %collective-permute-start.10 = (bf16[272,384]{1,0:T(8,128)(2,1)S(1)}, bf16[272,384]{1,0:T(8,128)(2,1)S(1)}, u32[]{:S(2)}, u32[]{:S(2)}) collective-permute-start(bf16[272,384]{1,0:T(8,128)(2,1)S(1)} %get-tuple-element.54), channel_id=1, source_target_pairs={{0,4},{4,8},{8,12},{12,0},{1,5},{5,9},{9,13},{13,1},{2,6},{6,10},{... | collective-permute-start | bytes 626696 | tf_op jit(solution)/shard_map/ppermute | solution.py:51
  38.7 3.8 %keys_moved.1 = (f32[256,512]{1,0:T(8,128)S(1)}, f32[16,128]{1,0:T(8,128)S(1)}, bf16[272,512]{1,0:T(8,128)(2,1)S(1)}) custom-call(s32[5]{0:T(128)S(1)} %pad_add_fusion.place_ref, s32[2,4,4,4]{3,2,1,0:T(4,128)S(1)} %copy-done.2, bf16[256,1536]{1,0:T(8,128)(2,1)S(1)} %get-tuple-element.39.own_q, bf16[256,1536]{1,0:T(8,128)(2,1)S(1)} %get-tuple-element.40.own_k, ...), custom_call_target="tpu_custom_call" | custom-call | flops 2000000000 | bytes 2000000 | tf_op jit(solution)/shard_map/keys_moved/pallas_call | solution.py:433
  42.5 0.6 collective-permute-start.14
  43.1 0.1 collective-permute-done.11.payload_in
  43.1 0.7 %relay.2 = (bf16[272,640]{1,0:T(8,128)(2,1)S(1)}, f32[16,128]{1,0:T(8,128)S(1)}) custom-call(s32[5]{0:T(128)S(1)} %pad_add_fusion.place_ref, f32[256,640]{1,0:T(8,128)S(1)} %get-tuple-element.55.local_out, f32[16,128]{1,0:T(8,128)S(1)} %get-tuple-element.56.local_stats, bf16[272,640]{1,0:T(8,128)(2,1)S(1)} %collective-permute-done.11.payload_in, ...), custom_call_target="tpu_custom_call" | custom-call | flops 700000000 | bytes 700000 | tf_op jit(solution)/shard_map/relay/pallas_call | solution.py:433
  43.8 1.5 %collective-permute-start.13 = (bf16[272,640]{1,0:T(8,128)(2,1)S(1)}, bf16[272,640]{1,0:T(8,128)(2,1)S(1)}, u32[]{:S(2)}, u32[]{:S(2)}) collective-permute-start(bf16[272,640]{1,0:T(8,128)(2,1)S(1)} %get-tuple-element.63), channel_id=1, source_target_pairs={{0,4},{4,8},{8,12},{12,0},{1,5},{5,9},{9,13},{13,1},{2,6},{6,10},{... | collective-permute-start | bytes 1044488 | tf_op jit(solution)/shard_map/ppermute | solution.py:51
  45.3 1.4 %collective-permute-done.10.payload_in = bf16[272,384]{1,0:T(8,128)(2,1)S(1)} collective-permute-done((bf16[272,384]{1,0:T(8,128)(2,1)S(1)}, bf16[272,384]{1,0:T(8,128)(2,1)S(1)}, u32[]{:S(2)}, u32[]{:S(2)}) %collective-permute-start.10) | collective-permute-done | bytes 208928 | tf_op jit(solution)/shard_map/ppermute | solution.py:51
  46.7 0.6 relay.3
  47.4 0.1 collective-permute-start.12
  47.4 1.7 %collective-permute-done.14.payload_in = bf16[272,512]{1,0:T(8,128)(2,1)S(1)} collective-permute-done((bf16[272,512]{1,0:T(8,128)(2,1)S(1)}, bf16[272,512]{1,0:T(8,128)(2,1)S(1)}, u32[]{:S(2)}, u32[]{:S(2)}) %collective-permute-start.14) | collective-permute-done | bytes 278560 | tf_op jit(solution)/shard_map/ppermute | solution.py:29
  49.1 0.8 %finish.3 = (f32[256,512]{1,0:T(8,128)S(1)}, f32[8,128]{1,0:T(8,128)S(1)}) custom-call(s32[5]{0:T(128)S(1)} %pad_add_fusion.place_ref, f32[256,512]{1,0:T(8,128)S(1)} %get-tuple-element.64.local_out, f32[16,128]{1,0:T(8,128)S(1)} %get-tuple-element.59.rest_0_.local_stats, bf16[272,512]{1,0:T(8,128)(2,1)S(1)} %collective-permute-done.14.payload_in, ...), custom_call_target="tpu_custom_call" | custom-call | flops 800000000 | bytes 800000 | tf_op jit(solution)/shard_map/finish/pallas_call | solution.py:433
  49.9 5.2 %collective-permute-done.13.payload_in = bf16[272,640]{1,0:T(8,128)(2,1)S(1)} collective-permute-done((bf16[272,640]{1,0:T(8,128)(2,1)S(1)}, bf16[272,640]{1,0:T(8,128)(2,1)S(1)}, u32[]{:S(2)}, u32[]{:S(2)}) %collective-permute-start.13) | collective-permute-done | bytes 348192 | tf_op jit(solution)/shard_map/ppermute | solution.py:51
  55.1 0.8 %finish.4 = (f32[256,640]{1,0:T(8,128)S(1)}, f32[8,128]{1,0:T(8,128)S(1)}) custom-call(s32[5]{0:T(128)S(1)} %pad_add_fusion.place_ref, f32[256,640]{1,0:T(8,128)S(1)} %get-tuple-element.62.local_out, f32[16,128]{1,0:T(8,128)S(1)} %get-tuple-element.48.rest_0_.local_stats, bf16[272,640]{1,0:T(8,128)(2,1)S(1)} %collective-permute-done.13.payload_in, ...), custom_call_target="tpu_custom_call" | custom-call | flops 800000000 | bytes 800000 | tf_op jit(solution)/shard_map/finish/pallas_call | solution.py:433
  55.9 1.4 %collective-permute-done.12.payload_in = bf16[272,384]{1,0:T(8,128)(2,1)S(1)} collective-permute-done((bf16[272,384]{1,0:T(8,128)(2,1)S(1)}, bf16[272,384]{1,0:T(8,128)(2,1)S(1)}, u32[]{:S(2)}, u32[]{:S(2)}) %collective-permute-start.12) | collective-permute-done | bytes 208928 | tf_op jit(solution)/shard_map/ppermute | solution.py:51
  57.3 0.0 copy-start
  57.3 0.7 %finish.5 = (f32[256,384]{1,0:T(8,128)S(1)}, f32[8,128]{1,0:T(8,128)S(1)}) custom-call(s32[5]{0:T(128)S(1)} %pad_add_fusion.place_ref, f32[256,384]{1,0:T(8,128)S(1)} %get-tuple-element.50.local_out, f32[16,128]{1,0:T(8,128)S(1)} %get-tuple-element.51.rest_0_.local_stats, bf16[272,384]{1,0:T(8,128)(2,1)S(1)} %collective-permute-done.12.payload_in, ...), custom_call_target="tpu_custom_call" | custom-call | flops 800000000 | bytes 800000 | tf_op jit(solution)/shard_map/finish/pallas_call | solution.py:433
  58.1 5.8 %psum.7.squares = f32[8,128]{1,0:T(8,128)S(1)} all-reduce(f32[8,128]{1,0:T(8,128)S(1)} %get-tuple-element.69), channel_id=1, replica_groups=mesh['stretch'=2,'cp'=4,'tp'=4] {'tp'}, use_global_device_ids=true, to_apply=%region_0.0 | all-reduce | flops 1024 | bytes 8192 | tf_op jit(solution)/shard_map/psum | solution.py:537
  63.8 0.0 copy-start.1
  63.8 0.0 copy-done
  63.8 0.6 copy-done.1
  64.5 1.7 %shard_map.64 = bf16[256,1536]{1,0:T(8,128)(2,1)} custom-call(s32[5]{0:T(128)S(1)} %pad_add_fusion.place_ref, s32[4]{0:T(128)S(1)} %copy-done.1, f32[8,128]{1,0:T(8,128)S(1)} %psum.7.squares, bf16[16,1536]{1,0:T(8,128)(2,1)S(1)} %copy-done, f32[256,640]{1,0:T(8,128)S(1)} %get-tuple-element.70.refs_0_, f32[256,384]{1,0:T(8,128)S(1)} %get-tuple-element.71.refs_1_, ...), custom_call_target="tpu_custom_call" | custom-call | tf_op jit(solution)/shard_map/pallas_call | solution.py:538
  (2 shorter events, 0.0 us)
Async XLA Ops:
  2.5 21.5 %copy-start.2 = (s32[2,4,4,4]{3,2,1,0:T(4,128)S(1)}, s32[2,4,4,4]{3,2,1,0:T(4,128)}, u32[]{:S(2)}) copy-start(s32[2,4,4,4]{3,2,1,0:T(4,128)} %ranges_ref.9) | copy-start | bytes 1540
  2.5 21.0 %collective-permute-start.7 = (bf16[256,1280]{1,0:T(8,128)(2,1)S(1)}, bf16[256,1280]{1,0:T(8,128)(2,1)S(1)}, u32[]{:S(2)}, u32[]{:S(2)}) collective-permute-start(bf16[256,1280]{1,0:T(8,128)(2,1)S(1)} %get-tuple-element.47), channel_id=1, source_target_pairs={{0,16},{16,0},{1,17},{17,1},{2,18},{18,2},{3,19},{19,3},{4,20},{20... | collective-permute-start | bytes 1966088 | tf_op jit(solution)/shard_map/ppermute | solution.py:29
  5.5 10.6 %collective-permute-start.3 = (bf16[256,640]{1,0:T(8,128)(2,1)S(1)}, bf16[256,640]{1,0:T(8,128)(2,1)S(1)}, u32[]{:S(2)}, u32[]{:S(2)}) collective-permute-start(bf16[256,640]{1,0:T(8,128)(2,1)S(1)} %get-tuple-element.45), channel_id=1, source_target_pairs={{0,4},{4,8},{8,12},{12,14},{14,10},{10,6},{6,2},{2,0},{1,5},{5,9},... | collective-permute-start | bytes 983048 | tf_op jit(solution)/shard_map/ppermute | solution.py:45
  7.1 10.7 %collective-permute-start.5 = (bf16[256,640]{1,0:T(8,128)(2,1)S(1)}, bf16[256,640]{1,0:T(8,128)(2,1)S(1)}, u32[]{:S(2)}, u32[]{:S(2)}) collective-permute-start(bf16[256,640]{1,0:T(8,128)(2,1)S(1)} %get-tuple-element.46), channel_id=1, source_target_pairs={{4,0},{8,4},{12,8},{14,12},{10,14},{6,10},{2,6},{0,2},{5,1},{9,5},... | collective-permute-start | bytes 983048 | tf_op jit(solution)/shard_map/ppermute | solution.py:45
  7.5 12.8 %collective-permute-start = (bf16[256,384]{1,0:T(8,128)(2,1)S(1)}, bf16[256,384]{1,0:T(8,128)(2,1)S(1)}, u32[]{:S(2)}, u32[]{:S(2)}) collective-permute-start(bf16[256,384]{1,0:T(8,128)(2,1)S(1)} %get-tuple-element.42), channel_id=1, source_target_pairs={{0,4},{4,8},{8,12},{12,14},{14,10},{10,6},{6,2},{2,0},{1,5},{5,9},... | collective-permute-start | bytes 589832 | tf_op jit(solution)/shard_map/ppermute | solution.py:45
  9.1 12.8 %collective-permute-start.1 = (bf16[256,384]{1,0:T(8,128)(2,1)S(1)}, bf16[256,384]{1,0:T(8,128)(2,1)S(1)}, u32[]{:S(2)}, u32[]{:S(2)}) collective-permute-start(bf16[256,384]{1,0:T(8,128)(2,1)S(1)} %get-tuple-element.43), channel_id=1, source_target_pairs={{4,0},{8,4},{12,8},{14,12},{10,14},{6,10},{2,6},{0,2},{5,1},{9,5},... | collective-permute-start | bytes 589832 | tf_op jit(solution)/shard_map/ppermute | solution.py:45
  16.1 11.2 %collective-permute-start.4 = (bf16[256,640]{1,0:T(8,128)(2,1)S(1)}, bf16[256,640]{1,0:T(8,128)(2,1)S(1)}, u32[]{:S(2)}, u32[]{:S(2)}) collective-permute-start(bf16[256,640]{1,0:T(8,128)(2,1)S(1)} %collective-permute-done.3.forward_q.rest_0_), channel_id=1, source_target_pairs={{0,4},{4,8},{8,12},{12,14},{14,10},{10,6},{6,2},{2,0},{1,5},{5,9},... | collective-permute-start | bytes 983048 | tf_op jit(solution)/shard_map/ppermute | solution.py:45
  17.7 11.2 %collective-permute-start.6 = (bf16[256,640]{1,0:T(8,128)(2,1)S(1)}, bf16[256,640]{1,0:T(8,128)(2,1)S(1)}, u32[]{:S(2)}, u32[]{:S(2)}) collective-permute-start(bf16[256,640]{1,0:T(8,128)(2,1)S(1)} %collective-permute-done.5.backward_q.rest_1_), channel_id=1, source_target_pairs={{4,0},{8,4},{12,8},{14,12},{10,14},{6,10},{2,6},{0,2},{5,1},{9,5},... | collective-permute-start | bytes 983048 | tf_op jit(solution)/shard_map/ppermute | solution.py:45
  20.3 12.5 %collective-permute-start.2 = (bf16[256,768]{1,0:T(8,128)(2,1)S(1)}, bf16[256,768]{1,0:T(8,128)(2,1)S(1)}, u32[]{:S(2)}, u32[]{:S(2)}) collective-permute-start(bf16[256,768]{1,0:T(8,128)(2,1)S(1)} %get-tuple-element.44), channel_id=1, source_target_pairs={{0,16},{16,0},{1,17},{17,1},{2,18},{18,2},{3,19},{19,3},{4,20},{20... | collective-permute-start | bytes 1179656 | tf_op jit(solution)/shard_map/ppermute | solution.py:29
  21.9 13.2 %collective-permute-start.8 = (bf16[256,384]{1,0:T(8,128)(2,1)S(1)}, bf16[256,384]{1,0:T(8,128)(2,1)S(1)}, u32[]{:S(2)}, u32[]{:S(2)}) collective-permute-start(bf16[256,384]{1,0:T(8,128)(2,1)S(1)} %collective-permute-done.forward_q.rest_2_), channel_id=1, source_target_pairs={{0,4},{4,8},{8,12},{12,14},{14,10},{10,6},{6,2},{2,0},{1,5},{5,9},... | collective-permute-start | bytes 589832 | tf_op jit(solution)/shard_map/ppermute | solution.py:45
  23.5 11.7 %collective-permute-start.9 = (bf16[256,384]{1,0:T(8,128)(2,1)S(1)}, bf16[256,384]{1,0:T(8,128)(2,1)S(1)}, u32[]{:S(2)}, u32[]{:S(2)}) collective-permute-start(bf16[256,384]{1,0:T(8,128)(2,1)S(1)} %collective-permute-done.1.backward_q.rest_3_), channel_id=1, source_target_pairs={{4,0},{8,4},{12,8},{14,12},{10,14},{6,10},{2,6},{0,2},{5,1},{9,5},... | collective-permute-start | bytes 589832 | tf_op jit(solution)/shard_map/ppermute | solution.py:45
  31.2 11.9 %collective-permute-start.11 = (bf16[272,640]{1,0:T(8,128)(2,1)S(1)}, bf16[272,640]{1,0:T(8,128)(2,1)S(1)}, u32[]{:S(2)}, u32[]{:S(2)}) collective-permute-start(bf16[272,640]{1,0:T(8,128)(2,1)S(1)} %get-tuple-element.57), channel_id=1, source_target_pairs={{0,4},{4,8},{8,12},{12,0},{1,5},{5,9},{9,13},{13,1},{2,6},{6,10},{... | collective-permute-start | bytes 1044488 | tf_op jit(solution)/shard_map/ppermute | solution.py:51
  37.1 9.7 %collective-permute-start.10 = (bf16[272,384]{1,0:T(8,128)(2,1)S(1)}, bf16[272,384]{1,0:T(8,128)(2,1)S(1)}, u32[]{:S(2)}, u32[]{:S(2)}) collective-permute-start(bf16[272,384]{1,0:T(8,128)(2,1)S(1)} %get-tuple-element.54), channel_id=1, source_target_pairs={{0,4},{4,8},{8,12},{12,0},{1,5},{5,9},{9,13},{13,1},{2,6},{6,10},{... | collective-permute-start | bytes 626696 | tf_op jit(solution)/shard_map/ppermute | solution.py:51
  42.5 6.6 %collective-permute-start.14 = (bf16[272,512]{1,0:T(8,128)(2,1)S(1)}, bf16[272,512]{1,0:T(8,128)(2,1)S(1)}, u32[]{:S(2)}, u32[]{:S(2)}) collective-permute-start(bf16[272,512]{1,0:T(8,128)(2,1)S(1)} %get-tuple-element.65), channel_id=1, source_target_pairs={{0,16},{16,0},{1,17},{17,1},{2,18},{18,2},{3,19},{19,3},{4,20},{20... | collective-permute-start | bytes 835592 | tf_op jit(solution)/shard_map/ppermute | solution.py:29
  43.8 11.2 %collective-permute-start.13 = (bf16[272,640]{1,0:T(8,128)(2,1)S(1)}, bf16[272,640]{1,0:T(8,128)(2,1)S(1)}, u32[]{:S(2)}, u32[]{:S(2)}) collective-permute-start(bf16[272,640]{1,0:T(8,128)(2,1)S(1)} %get-tuple-element.63), channel_id=1, source_target_pairs={{0,4},{4,8},{8,12},{12,0},{1,5},{5,9},{9,13},{13,1},{2,6},{6,10},{... | collective-permute-start | bytes 1044488 | tf_op jit(solution)/shard_map/ppermute | solution.py:51
  47.4 9.9 %collective-permute-start.12 = (bf16[272,384]{1,0:T(8,128)(2,1)S(1)}, bf16[272,384]{1,0:T(8,128)(2,1)S(1)}, u32[]{:S(2)}, u32[]{:S(2)}) collective-permute-start(bf16[272,384]{1,0:T(8,128)(2,1)S(1)} %get-tuple-element.61), channel_id=1, source_target_pairs={{0,4},{4,8},{8,12},{12,0},{1,5},{5,9},{9,13},{13,1},{2,6},{6,10},{... | collective-permute-start | bytes 626696 | tf_op jit(solution)/shard_map/ppermute | solution.py:51
  57.3 6.5 %copy-start = (bf16[16,1536]{1,0:T(8,128)(2,1)S(1)}, bf16[16,1536]{1,0:T(8,128)(2,1)}, u32[]{:S(2)}) copy-start(bf16[16,1536]{1,0:T(8,128)(2,1)} %gate_table.1) | copy-start | bytes 147460
  63.8 0.7 copy-start.1

commit v3 on v2

--- a/solution.py
+++ b/solution.py
@@ -349,7 +349,7 @@
 
 
 def finish_kernel(
-    head_count, place_ref, local_out, local_stats, payload_in, squares_in, *rest, axis
+    head_count, place_ref, local_out, local_stats, payload_in, gates, squares_in, *rest, axis, base
 ):
     out, squares_out = rest[-2:]
     parts, _ = joined(place_ref[axis], local_out, local_stats, payload_in, head_count)
@@ -359,27 +359,35 @@
         for head in range(head_count):
             part = parts[slot, head]
             total = total + jnp.sum(part * part, axis=0, keepdims=True)
-            out[stretch_rows(slot), head_columns(head)] = jnp.transpose(part)
+            gate_row = gates[slot : slot + 1, head_columns(base + head)]
+            out[stretch_rows(slot), head_columns(head)] = jnp.transpose(part) * gate_row
         squares_out[slot : slot + 1, :] += total
 
 
-def scale_kernel(head_counts, feature_count, place_ref, levels_ref, squares, gate_table, *refs):
-    parts, out = refs[:-1], refs[-1]
-    factors = as_columns(lax.rsqrt(squares[...] / feature_count + 1e-06))
-    pair_count = out.shape[0] // BLOCK
+def gates_kernel(pair_count, place_ref, levels_ref, gate_table, *rest):
+    out = rest[-1]
     gates = gate_table[...].astype(jnp.float32)
     level_ids = lax.broadcasted_iota(jnp.int32, gates.shape, 0)
+    out[...] = jnp.zeros_like(out)
     for slot in range(pair_count):
         level = levels_ref[place_ref[0] * pair_count + slot]
-        gate_row = jnp.sum(jnp.where(level_ids == level, gates, 0.0), axis=0, keepdims=True)
+        out[slot : slot + 1, :] = jnp.sum(
+            jnp.where(level_ids == level, gates, 0.0), axis=0, keepdims=True
+        )
+
+
+def scale_kernel(head_counts, feature_count, device_count, *refs):
+    squares = sum(ref[...] for ref in refs[:device_count])
+    parts, out = refs[device_count:-1], refs[-1]
+    factors = as_columns(lax.rsqrt(squares / feature_count + 1e-06))
+    for slot in range(out.shape[0] // BLOCK):
         rows = stretch_rows(slot)
         factor = factors[:, slot : slot + 1]
         base = 0
         for part, head_count in zip(parts, head_counts):
             for head in range(head_count):
-                columns = head_columns(base + head)
-                out[rows, columns] = (
-                    part[rows, head_columns(head)] * factor * gate_row[:, columns]
+                out[rows, head_columns(base + head)] = (
+                    part[rows, head_columns(head)] * factor
                 ).astype(jnp.bfloat16)
             base += head_count
 
@@ -467,7 +475,16 @@
         hops[1].append((round_trip(forward, True), round_trip(backward, False)))
 
     own_parts, near_parts, arrived = [], [], []
-    turn = ()
+    gates = pl.pallas_call(
+        functools.partial(gates_kernel, pair_count),
+        out_shape=jax.ShapeDtypeStruct((8, width_dev), jnp.float32),
+        in_specs=[SMEM, SMEM, VMEM],
+        out_specs=VMEM,
+        compiler_params=PARAMS,
+        cost_estimate=cost(0.6),
+        name="gates",
+    )(place, levels, gate_table)
+    turn = (gates,)
     for i in chunks:
         near = run(
             "near",
@@ -526,22 +543,27 @@
     for i in FINISH_ORDER:
         finished[i], squares = run(
             "finish",
-            functools.partial(finish_kernel, axis=0 if i == last else 1),
+            functools.partial(finish_kernel, axis=0 if i == last else 1, base=bases[i]),
             i,
             0.8,
             (float_shape(i), squares_shape),
             (place,),
-            (*own_parts[i], arrived[i], squares),
+            (*own_parts[i], arrived[i], gates, squares),
             turn,
         )
-    squares = lax.psum(squares, "tp")
+    device_count = lax.axis_size("tp")
+    shares = [squares]
+    for distance in range(1, device_count):
+        route = [(i, (i + distance) % device_count) for i in range(device_count)]
+        shares.append(lax.ppermute(squares, "tp", route))
     out = pl.pallas_call(
-        functools.partial(scale_kernel, head_counts, float(HEADS * HEAD_DIM)),
+        functools.partial(scale_kernel, head_counts, float(HEADS * HEAD_DIM), device_count),
         out_shape=jax.ShapeDtypeStruct((token_rows, width_dev), jnp.bfloat16),
-        in_specs=[SMEM, SMEM] + [VMEM] * (2 + len(finished)),
+        in_specs=[VMEM] * (device_count + len(finished)),
         out_specs=VMEM,
         compiler_params=PARAMS,
-    )(place, levels, squares, gate_table, *finished)
+        name="scale",
+    )(*shares, *finished)
     return out.reshape(query_rows.shape)
 
 

time: 66.4 us -> 63.8 us (0.961); the launches traced: 66.2 us -> 62.9 us
  blocking collectives: 5.77 us -> 0 us
  starting transfers between devices: 16.5 us -> 18.4 us
  waiting for transfers between devices: 22.1 us -> 23.3 us
    psum x1 -> x0, blocking collectives: 5.77 us -> none  [on_device(): squares = lax.psum(squares, 'tp')]
    ppermute x0 -> x3, waiting for transfers between devices: none -> 1.91 us  [on_device(): shares.append(lax.ppermute(squares, 'tp', route))]
    ppermute x0 -> x3, starting transfers between devices: none -> 1.82 us  [on_device(): shares.append(lax.ppermute(squares, 'tp', route))]
  transfers between devices with their start and end apart: 15 -> 18, of which waited for: 10 -> 12; matrix products, arithmetic and copies ran while one was open for 0% -> 0% of each run, Pallas kernels for 24% -> 27%
where the time goes in v3:
time: 63.8 us; the launch traced here: 62.9 us
  waiting for transfers between devices  23.3 us (37%)
  Pallas kernels  21 us (33%)
  starting transfers between devices  18.4 us (29%)
    pallas_call x10, Pallas kernels, run(): pl.pallas_call(functools.partial(kernel, head_counts[chunk]), out_shape=o...  16.9 us
    ppermute x8, waiting for transfers between devices, round_trip(): return lax.ppermute(block, ('cp', 'tp'), route)  11.7 us
    ppermute x8, starting transfers between devices, round_trip(): return lax.ppermute(block, ('cp', 'tp'), route)  8.1 us
    ppermute x4, waiting for transfers between devices, passed_up(): return lax.ppermute(block, 'cp', route)  8.03 us
    ppermute x4, starting transfers between devices, passed_up(): return lax.ppermute(block, 'cp', route)  4.83 us
    ppermute x3, starting transfers between devices, exchanged(): return lax.ppermute(block, 'stretch', [(0, 1), (1, 0)])  3.63 us
    pallas_call x1, Pallas kernels, on_device(): pl.pallas_call(functools.partial(pack_kernel, CHUNKS, KEYS_MOVED), out_sh...  2.37 us
    ppermute x3, waiting for transfers between devices, on_device(): shares.append(lax.ppermute(squares, 'tp', route))  1.91 us
  transfers between devices with their start and end apart: 18, of which 12 were waited for; matrix products, arithmetic and copies ran while one was open for 0% of the time, Pallas kernels for 27%

profile of v3, /device:TPU:0, one launch (start us, length us, event | category | flops | bytes accessed | tf_op | source)
XLA Modules:
  0.0 62.9 jit_solution(566929711171564795)
XLA Ops:
  0.0 0.1 pad_add_fusion.place_ref
  0.1 0.0 copy-start
  0.1 2.4 %pack.1 = (bf16[256,1536]{1,0:T(8,128)(2,1)S(1)}, bf16[256,1536]{1,0:T(8,128)(2,1)S(1)}, bf16[256,1536]{1,0:T(8,128)(2,1)S(1)}, bf16[256,1280]{1,0:T(8,128)(2,1)...) custom-call(s32[5]{0:T(128)S(1)} %pad_add_fusion.place_ref, ...), custom_call_target="tpu_custom_call" | custom-call | flops 1000000000 | bytes 1000000 | tf_op jit(solution)/shard_map/pack/pallas_call | solution.py:456
  2.5 3.0 %collective-permute-start.7 = (bf16[256,1280]{1,0:T(8,128)(2,1)S(1)}, bf16[256,1280]{1,0:T(8,128)(2,1)S(1)}, u32[]{:S(2)}, u32[]{:S(2)}) collective-permute-start(bf16[256,1280]{1,0:T(8,128)(2,1)S(1)} %get-tuple-element.47), channel_id=1, source_target_pairs={{0,16},{16,0},{1,17},{17,1},{2,18},{18,2},{3,19},{19,3},{4,20},{20... | collective-permute-start | bytes 1966088 | tf_op jit(solution)/shard_map/ppermute | solution.py:29
  5.5 1.6 %collective-permute-start.3 = (bf16[256,640]{1,0:T(8,128)(2,1)S(1)}, bf16[256,640]{1,0:T(8,128)(2,1)S(1)}, u32[]{:S(2)}, u32[]{:S(2)}) collective-permute-start(bf16[256,640]{1,0:T(8,128)(2,1)S(1)} %get-tuple-element.45), channel_id=1, source_target_pairs={{0,4},{4,8},{8,12},{12,14},{14,10},{10,6},{6,2},{2,0},{1,5},{5,9},... | collective-permute-start | bytes 983048 | tf_op jit(solution)/shard_map/ppermute | solution.py:45
  7.1 0.4 collective-permute-start.5
  7.5 0.0 copy-start.2
  7.5 1.6 %collective-permute-start = (bf16[256,384]{1,0:T(8,128)(2,1)S(1)}, bf16[256,384]{1,0:T(8,128)(2,1)S(1)}, u32[]{:S(2)}, u32[]{:S(2)}) collective-permute-start(bf16[256,384]{1,0:T(8,128)(2,1)S(1)} %get-tuple-element.42), channel_id=1, source_target_pairs={{0,4},{4,8},{8,12},{12,14},{14,10},{10,6},{6,2},{2,0},{1,5},{5,9},... | collective-permute-start | bytes 589832 | tf_op jit(solution)/shard_map/ppermute | solution.py:45
  9.1 0.0 copy-start.1
  9.1 0.4 collective-permute-start.1
  9.5 6.6 %collective-permute-done.3.forward_q.rest_0_ = bf16[256,640]{1,0:T(8,128)(2,1)S(1)} collective-permute-done((bf16[256,640]{1,0:T(8,128)(2,1)S(1)}, bf16[256,640]{1,0:T(8,128)(2,1)S(1)}, u32[]{:S(2)}, u32[]{:S(2)}) %collective-permute-start.3) | collective-permute-done | bytes 327712 | tf_op jit(solution)/shard_map/ppermute | solution.py:45
  16.1 1.6 %collective-permute-start.4 = (bf16[256,640]{1,0:T(8,128)(2,1)S(1)}, bf16[256,640]{1,0:T(8,128)(2,1)S(1)}, u32[]{:S(2)}, u32[]{:S(2)}) collective-permute-start(bf16[256,640]{1,0:T(8,128)(2,1)S(1)} %collective-permute-done.3.forward_q.rest_0_), channel_id=1, source_target_pairs={{0,4},{4,8},{8,12},{12,14},{14,10},{10,6},{6,2},{2,0},{1,5},{5,9},... | collective-permute-start | bytes 983048 | tf_op jit(solution)/shard_map/ppermute | solution.py:45
  17.7 0.0 collective-permute-done.5.backward_q.rest_1_
  17.7 0.4 collective-permute-start.6
  18.2 0.0 copy-done
  18.2 0.0 copy-done.2
  18.2 0.6 gates.1.rest_0_
  18.8 1.6 %collective-permute-done.forward_q.rest_2_ = bf16[256,384]{1,0:T(8,128)(2,1)S(1)} collective-permute-done((bf16[256,384]{1,0:T(8,128)(2,1)S(1)}, bf16[256,384]{1,0:T(8,128)(2,1)S(1)}, u32[]{:S(2)}, u32[]{:S(2)}) %collective-permute-start) | collective-permute-done | bytes 196640 | tf_op jit(solution)/shard_map/ppermute | solution.py:45
  20.3 0.0 collective-permute-start.2
  20.4 1.6 %collective-permute-done.1.backward_q.rest_3_ = bf16[256,384]{1,0:T(8,128)(2,1)S(1)} collective-permute-done((bf16[256,384]{1,0:T(8,128)(2,1)S(1)}, bf16[256,384]{1,0:T(8,128)(2,1)S(1)}, u32[]{:S(2)}, u32[]{:S(2)}) %collective-permute-start.1) | collective-permute-done | bytes 196640 | tf_op jit(solution)/shard_map/ppermute | solution.py:45
  21.9 1.6 %collective-permute-start.8 = (bf16[256,384]{1,0:T(8,128)(2,1)S(1)}, bf16[256,384]{1,0:T(8,128)(2,1)S(1)}, u32[]{:S(2)}, u32[]{:S(2)}) collective-permute-start(bf16[256,384]{1,0:T(8,128)(2,1)S(1)} %collective-permute-done.forward_q.rest_2_), channel_id=1, source_target_pairs={{0,4},{4,8},{8,12},{12,14},{14,10},{10,6},{6,2},{2,0},{1,5},{5,9},... | collective-permute-start | bytes 589832 | tf_op jit(solution)/shard_map/ppermute | solution.py:45
  23.5 0.0 collective-permute-done.7.prior_kv.next_q
  23.5 0.5 collective-permute-start.9
  24.0 0.0 copy-done.1
  24.0 3.0 %near.2 = (f32[256,640]{1,0:T(8,128)S(1)}, f32[16,128]{1,0:T(8,128)S(1)}, f32[256,640]{1,0:T(8,128)S(1)}, f32[16,128]{1,0:T(8,128)S(1)}) custom-call(s32[5]{0:T(128)S(1)} %pad_add_fusion.place_ref, s32[2,4,4,4]{3,2,1,0:T(4,128)S(1)} %copy-done.1, bf16[256,1536]{1,0:T(8,128)(2,1)S(1)} %get-tuple-element.39.own_q, ...), custom_call_target="tpu_custom_call" | custom-call | flops 3000000000 | bytes 3000000 | tf_op jit(solution)/shard_map/near/pallas_call | solution.py:441
  27.0 0.4 collective-permute-done.4.forward_q.rest_4_
  27.4 1.6 %collective-permute-done.6.backward_q.rest_5_ = bf16[256,640]{1,0:T(8,128)(2,1)S(1)} collective-permute-done((bf16[256,640]{1,0:T(8,128)(2,1)S(1)}, bf16[256,640]{1,0:T(8,128)(2,1)S(1)}, u32[]{:S(2)}, u32[]{:S(2)}) %collective-permute-start.6) | collective-permute-done | bytes 327712 | tf_op jit(solution)/shard_map/ppermute | solution.py:45
  28.9 2.2 %far.2 = (bf16[272,640]{1,0:T(8,128)(2,1)S(1)}, f32[16,128]{1,0:T(8,128)S(1)}) custom-call(s32[5]{0:T(128)S(1)} %pad_add_fusion.place_ref, s32[2,4,4,4]{3,2,1,0:T(4,128)S(1)} %copy-done.1, bf16[256,1536]{1,0:T(8,128)(2,1)S(1)} %get-tuple-element.40.own_k, bf16[256,1536]{1,0:T(8,128)(2,1)S(1)} %get-tuple-element.41.own_v, ...), custom_call_target="tpu_custom_call" | custom-call | flops 1500000000 | bytes 1500000 | tf_op jit(solution)/shard_map/far/pallas_call | solution.py:441
  31.2 1.6 %collective-permute-start.11 = (bf16[272,640]{1,0:T(8,128)(2,1)S(1)}, bf16[272,640]{1,0:T(8,128)(2,1)S(1)}, u32[]{:S(2)}, u32[]{:S(2)}) collective-permute-start(bf16[272,640]{1,0:T(8,128)(2,1)S(1)} %get-tuple-element.57), channel_id=1, source_target_pairs={{0,4},{4,8},{8,12},{12,0},{1,5},{5,9},{9,13},{13,1},{2,6},{6,10},{... | collective-permute-start | bytes 1044488 | tf_op jit(solution)/shard_map/ppermute | solution.py:51
  32.8 0.0 collective-permute-done.2.prior_kv
  32.8 2.3 %near.3 = (f32[256,384]{1,0:T(8,128)S(1)}, f32[16,128]{1,0:T(8,128)S(1)}, f32[256,384]{1,0:T(8,128)S(1)}, f32[16,128]{1,0:T(8,128)S(1)}) custom-call(s32[5]{0:T(128)S(1)} %pad_add_fusion.place_ref, s32[2,4,4,4]{3,2,1,0:T(4,128)S(1)} %copy-done.1, bf16[256,1536]{1,0:T(8,128)(2,1)S(1)} %get-tuple-element.39.own_q, ...), custom_call_target="tpu_custom_call" | custom-call | flops 1800000000 | bytes 1800000 | tf_op jit(solution)/shard_map/near/pallas_call | solution.py:441
  35.2 0.0 collective-permute-done.8.forward_q.rest_6_
  35.2 0.0 collective-permute-done.9.backward_q.rest_7_
  35.2 1.9 %far.3 = (bf16[272,384]{1,0:T(8,128)(2,1)S(1)}, f32[16,128]{1,0:T(8,128)S(1)}) custom-call(s32[5]{0:T(128)S(1)} %pad_add_fusion.place_ref, s32[2,4,4,4]{3,2,1,0:T(4,128)S(1)} %copy-done.1, bf16[256,1536]{1,0:T(8,128)(2,1)S(1)} %get-tuple-element.40.own_k, bf16[256,1536]{1,0:T(8,128)(2,1)S(1)} %get-tuple-element.41.own_v, ...), custom_call_target="tpu_custom_call" | custom-call | flops 900000000 | bytes 900000 | tf_op jit(solution)/shard_map/far/pallas_call | solution.py:441
  37.1 1.6 %collective-permute-start.10 = (bf16[272,384]{1,0:T(8,128)(2,1)S(1)}, bf16[272,384]{1,0:T(8,128)(2,1)S(1)}, u32[]{:S(2)}, u32[]{:S(2)}) collective-permute-start(bf16[272,384]{1,0:T(8,128)(2,1)S(1)} %get-tuple-element.54), channel_id=1, source_target_pairs={{0,4},{4,8},{8,12},{12,0},{1,5},{5,9},{9,13},{13,1},{2,6},{6,10},{... | collective-permute-start | bytes 626696 | tf_op jit(solution)/shard_map/ppermute | solution.py:51
  38.7 3.8 %keys_moved.1 = (f32[256,512]{1,0:T(8,128)S(1)}, f32[16,128]{1,0:T(8,128)S(1)}, bf16[272,512]{1,0:T(8,128)(2,1)S(1)}) custom-call(s32[5]{0:T(128)S(1)} %pad_add_fusion.place_ref, s32[2,4,4,4]{3,2,1,0:T(4,128)S(1)} %copy-done.1, bf16[256,1536]{1,0:T(8,128)(2,1)S(1)} %get-tuple-element.39.own_q, bf16[256,1536]{1,0:T(8,128)(2,1)S(1)} %get-tuple-element.40.own_k, ...), custom_call_target="tpu_custom_call" | custom-call | flops 2000000000 | bytes 2000000 | tf_op jit(solution)/shard_map/keys_moved/pallas_call | solution.py:441
  42.5 0.6 collective-permute-start.14
  43.1 0.1 collective-permute-done.11.payload_in
  43.1 0.7 %relay.2 = (bf16[272,640]{1,0:T(8,128)(2,1)S(1)}, f32[16,128]{1,0:T(8,128)S(1)}) custom-call(s32[5]{0:T(128)S(1)} %pad_add_fusion.place_ref, f32[256,640]{1,0:T(8,128)S(1)} %get-tuple-element.55.local_out, f32[16,128]{1,0:T(8,128)S(1)} %get-tuple-element.56.local_stats, bf16[272,640]{1,0:T(8,128)(2,1)S(1)} %collective-permute-done.11.payload_in, ...), custom_call_target="tpu_custom_call" | custom-call | flops 700000000 | bytes 700000 | tf_op jit(solution)/shard_map/relay/pallas_call | solution.py:441
  43.8 1.5 %collective-permute-start.13 = (bf16[272,640]{1,0:T(8,128)(2,1)S(1)}, bf16[272,640]{1,0:T(8,128)(2,1)S(1)}, u32[]{:S(2)}, u32[]{:S(2)}) collective-permute-start(bf16[272,640]{1,0:T(8,128)(2,1)S(1)} %get-tuple-element.63), channel_id=1, source_target_pairs={{0,4},{4,8},{8,12},{12,0},{1,5},{5,9},{9,13},{13,1},{2,6},{6,10},{... | collective-permute-start | bytes 1044488 | tf_op jit(solution)/shard_map/ppermute | solution.py:51
  45.3 1.4 %collective-permute-done.10.payload_in = bf16[272,384]{1,0:T(8,128)(2,1)S(1)} collective-permute-done((bf16[272,384]{1,0:T(8,128)(2,1)S(1)}, bf16[272,384]{1,0:T(8,128)(2,1)S(1)}, u32[]{:S(2)}, u32[]{:S(2)}) %collective-permute-start.10) | collective-permute-done | bytes 208928 | tf_op jit(solution)/shard_map/ppermute | solution.py:51
  46.7 0.6 %relay.3 = (bf16[272,384]{1,0:T(8,128)(2,1)S(1)}, f32[16,128]{1,0:T(8,128)S(1)}) custom-call(s32[5]{0:T(128)S(1)} %pad_add_fusion.place_ref, f32[256,384]{1,0:T(8,128)S(1)} %get-tuple-element.52.local_out, f32[16,128]{1,0:T(8,128)S(1)} %get-tuple-element.53.local_stats, bf16[272,384]{1,0:T(8,128)(2,1)S(1)} %collective-permute-done.10.payload_in, ...), custom_call_target="tpu_custom_call" | custom-call | flops 700000000 | bytes 700000 | tf_op jit(solution)/shard_map/relay/pallas_call | solution.py:441
  47.3 0.1 collective-permute-start.12
  47.4 1.7 %collective-permute-done.14.payload_in = bf16[272,512]{1,0:T(8,128)(2,1)S(1)} collective-permute-done((bf16[272,512]{1,0:T(8,128)(2,1)S(1)}, bf16[272,512]{1,0:T(8,128)(2,1)S(1)}, u32[]{:S(2)}, u32[]{:S(2)}) %collective-permute-start.14) | collective-permute-done | bytes 278560 | tf_op jit(solution)/shard_map/ppermute | solution.py:29
  49.1 0.8 %finish.3 = (f32[256,512]{1,0:T(8,128)S(1)}, f32[8,128]{1,0:T(8,128)S(1)}) custom-call(s32[5]{0:T(128)S(1)} %pad_add_fusion.place_ref, f32[256,512]{1,0:T(8,128)S(1)} %get-tuple-element.64.local_out, f32[16,128]{1,0:T(8,128)S(1)} %get-tuple-element.59.rest_0_.local_stats, bf16[272,512]{1,0:T(8,128)(2,1)S(1)} %collective-permute-done.14.payload_in, ...), custom_call_target="tpu_custom_call" | custom-call | flops 800000000 | bytes 800000 | tf_op jit(solution)/shard_map/finish/pallas_call | solution.py:441
  49.9 5.2 %collective-permute-done.13.payload_in = bf16[272,640]{1,0:T(8,128)(2,1)S(1)} collective-permute-done((bf16[272,640]{1,0:T(8,128)(2,1)S(1)}, bf16[272,640]{1,0:T(8,128)(2,1)S(1)}, u32[]{:S(2)}, u32[]{:S(2)}) %collective-permute-start.13) | collective-permute-done | bytes 348192 | tf_op jit(solution)/shard_map/ppermute | solution.py:51
  55.1 0.8 %finish.4 = (f32[256,640]{1,0:T(8,128)S(1)}, f32[8,128]{1,0:T(8,128)S(1)}) custom-call(s32[5]{0:T(128)S(1)} %pad_add_fusion.place_ref, f32[256,640]{1,0:T(8,128)S(1)} %get-tuple-element.62.local_out, f32[16,128]{1,0:T(8,128)S(1)} %get-tuple-element.48.rest_0_.local_stats, bf16[272,640]{1,0:T(8,128)(2,1)S(1)} %collective-permute-done.13.payload_in, ...), custom_call_target="tpu_custom_call" | custom-call | flops 800000000 | bytes 800000 | tf_op jit(solution)/shard_map/finish/pallas_call | solution.py:441
  55.9 1.4 %collective-permute-done.12.payload_in = bf16[272,384]{1,0:T(8,128)(2,1)S(1)} collective-permute-done((bf16[272,384]{1,0:T(8,128)(2,1)S(1)}, bf16[272,384]{1,0:T(8,128)(2,1)S(1)}, u32[]{:S(2)}, u32[]{:S(2)}) %collective-permute-start.12) | collective-permute-done | bytes 208928 | tf_op jit(solution)/shard_map/ppermute | solution.py:51
  57.3 0.7 %finish.5 = (f32[256,384]{1,0:T(8,128)S(1)}, f32[8,128]{1,0:T(8,128)S(1)}) custom-call(s32[5]{0:T(128)S(1)} %pad_add_fusion.place_ref, f32[256,384]{1,0:T(8,128)S(1)} %get-tuple-element.50.local_out, f32[16,128]{1,0:T(8,128)S(1)} %get-tuple-element.51.rest_0_.local_stats, bf16[272,384]{1,0:T(8,128)(2,1)S(1)} %collective-permute-done.12.payload_in, ...), custom_call_target="tpu_custom_call" | custom-call | flops 800000000 | bytes 800000 | tf_op jit(solution)/shard_map/finish/pallas_call | solution.py:441
  58.0 0.1 collective-permute-start.15
  58.1 0.3 collective-permute-start.16
  58.4 1.5 %collective-permute-start.17 = (f32[8,128]{1,0:T(8,128)S(1)}, f32[8,128]{1,0:T(8,128)S(1)}, u32[]{:S(2)}, u32[]{:S(2)}) collective-permute-start(f32[8,128]{1,0:T(8,128)S(1)} %get-tuple-element.69.refs_0_), channel_id=1, source_target_pairs={{0,3},{1,0},{2,1},{3,2},{4,7},{5,4},{6,5},{7,6},{8,11},{9,8},{10,9... | collective-permute-start | bytes 12296 | tf_op jit(solution)/shard_map/ppermute | solution.py:558
  59.9 1.3 %collective-permute-done.15.refs_1_ = f32[8,128]{1,0:T(8,128)S(1)} collective-permute-done((f32[8,128]{1,0:T(8,128)S(1)}, f32[8,128]{1,0:T(8,128)S(1)}, u32[]{:S(2)}, u32[]{:S(2)}) %collective-permute-start.15) | collective-permute-done | bytes 4128 | tf_op jit(solution)/shard_map/ppermute | solution.py:558
  61.1 0.7 %collective-permute-done.16.refs_2_ = f32[8,128]{1,0:T(8,128)S(1)} collective-permute-done((f32[8,128]{1,0:T(8,128)S(1)}, f32[8,128]{1,0:T(8,128)S(1)}, u32[]{:S(2)}, u32[]{:S(2)}) %collective-permute-start.16) | collective-permute-done | bytes 4128 | tf_op jit(solution)/shard_map/ppermute | solution.py:558
  61.8 0.0 collective-permute-done.17.refs_3_
  61.8 1.2 %scale.1 = bf16[256,1536]{1,0:T(8,128)(2,1)} custom-call(f32[8,128]{1,0:T(8,128)S(1)} %get-tuple-element.69.refs_0_, f32[8,128]{1,0:T(8,128)S(1)} %collective-permute-done.15.refs_1_, f32[8,128]{1,0:T(8,128)S(1)} %collective-permute-done.16.refs_2_, f32[8,128]{1,0:T(8,128)S(1)} %collective-permute-done.17.refs_3_, f32[256,640]{1,0:T(8,128)S(1)} %get-tuple-element.70.refs_4_, ...), custom_call_target="tpu_custom_call" | custom-call | tf_op jit(solution)/shard_map/scale/pallas_call | solution.py:559
  (2 shorter events, 0.0 us)
Async XLA Ops:
  0.1 18.1 %copy-start = (bf16[16,1536]{1,0:T(8,128)(2,1)S(1)}, bf16[16,1536]{1,0:T(8,128)(2,1)}, u32[]{:S(2)}) copy-start(bf16[16,1536]{1,0:T(8,128)(2,1)} %gate_table.1) | copy-start | bytes 147460
  2.5 21.0 %collective-permute-start.7 = (bf16[256,1280]{1,0:T(8,128)(2,1)S(1)}, bf16[256,1280]{1,0:T(8,128)(2,1)S(1)}, u32[]{:S(2)}, u32[]{:S(2)}) collective-permute-start(bf16[256,1280]{1,0:T(8,128)(2,1)S(1)} %get-tuple-element.47), channel_id=1, source_target_pairs={{0,16},{16,0},{1,17},{17,1},{2,18},{18,2},{3,19},{19,3},{4,20},{20... | collective-permute-start | bytes 1966088 | tf_op jit(solution)/shard_map/ppermute | solution.py:29
  5.5 10.6 %collective-permute-start.3 = (bf16[256,640]{1,0:T(8,128)(2,1)S(1)}, bf16[256,640]{1,0:T(8,128)(2,1)S(1)}, u32[]{:S(2)}, u32[]{:S(2)}) collective-permute-start(bf16[256,640]{1,0:T(8,128)(2,1)S(1)} %get-tuple-element.45), channel_id=1, source_target_pairs={{0,4},{4,8},{8,12},{12,14},{14,10},{10,6},{6,2},{2,0},{1,5},{5,9},... | collective-permute-start | bytes 983048 | tf_op jit(solution)/shard_map/ppermute | solution.py:45
  7.1 10.7 %collective-permute-start.5 = (bf16[256,640]{1,0:T(8,128)(2,1)S(1)}, bf16[256,640]{1,0:T(8,128)(2,1)S(1)}, u32[]{:S(2)}, u32[]{:S(2)}) collective-permute-start(bf16[256,640]{1,0:T(8,128)(2,1)S(1)} %get-tuple-element.46), channel_id=1, source_target_pairs={{4,0},{8,4},{12,8},{14,12},{10,14},{6,10},{2,6},{0,2},{5,1},{9,5},... | collective-permute-start | bytes 983048 | tf_op jit(solution)/shard_map/ppermute | solution.py:45
  7.5 10.7 %copy-start.2 = (s32[4]{0:T(128)S(1)}, s32[4]{0:T(128)}, u32[]{:S(2)}) copy-start(s32[4]{0:T(128)} %levels_ref.1) | copy-start | bytes 52
  7.5 12.8 %collective-permute-start = (bf16[256,384]{1,0:T(8,128)(2,1)S(1)}, bf16[256,384]{1,0:T(8,128)(2,1)S(1)}, u32[]{:S(2)}, u32[]{:S(2)}) collective-permute-start(bf16[256,384]{1,0:T(8,128)(2,1)S(1)} %get-tuple-element.42), channel_id=1, source_target_pairs={{0,4},{4,8},{8,12},{12,14},{14,10},{10,6},{6,2},{2,0},{1,5},{5,9},... | collective-permute-start | bytes 589832 | tf_op jit(solution)/shard_map/ppermute | solution.py:45
  9.1 14.9 %copy-start.1 = (s32[2,4,4,4]{3,2,1,0:T(4,128)S(1)}, s32[2,4,4,4]{3,2,1,0:T(4,128)}, u32[]{:S(2)}) copy-start(s32[2,4,4,4]{3,2,1,0:T(4,128)} %ranges_ref.9) | copy-start | bytes 1540
  9.1 12.8 %collective-permute-start.1 = (bf16[256,384]{1,0:T(8,128)(2,1)S(1)}, bf16[256,384]{1,0:T(8,128)(2,1)S(1)}, u32[]{:S(2)}, u32[]{:S(2)}) collective-permute-start(bf16[256,384]{1,0:T(8,128)(2,1)S(1)} %get-tuple-element.43), channel_id=1, source_target_pairs={{4,0},{8,4},{12,8},{14,12},{10,14},{6,10},{2,6},{0,2},{5,1},{9,5},... | collective-permute-start | bytes 589832 | tf_op jit(solution)/shard_map/ppermute | solution.py:45
  16.1 11.2 %collective-permute-start.4 = (bf16[256,640]{1,0:T(8,128)(2,1)S(1)}, bf16[256,640]{1,0:T(8,128)(2,1)S(1)}, u32[]{:S(2)}, u32[]{:S(2)}) collective-permute-start(bf16[256,640]{1,0:T(8,128)(2,1)S(1)} %collective-permute-done.3.forward_q.rest_0_), channel_id=1, source_target_pairs={{0,4},{4,8},{8,12},{12,14},{14,10},{10,6},{6,2},{2,0},{1,5},{5,9},... | collective-permute-start | bytes 983048 | tf_op jit(solution)/shard_map/ppermute | solution.py:45
  17.7 11.2 %collective-permute-start.6 = (bf16[256,640]{1,0:T(8,128)(2,1)S(1)}, bf16[256,640]{1,0:T(8,128)(2,1)S(1)}, u32[]{:S(2)}, u32[]{:S(2)}) collective-permute-start(bf16[256,640]{1,0:T(8,128)(2,1)S(1)} %collective-permute-done.5.backward_q.rest_1_), channel_id=1, source_target_pairs={{4,0},{8,4},{12,8},{14,12},{10,14},{6,10},{2,6},{0,2},{5,1},{9,5},... | collective-permute-start | bytes 983048 | tf_op jit(solution)/shard_map/ppermute | solution.py:45
  20.3 12.5 %collective-permute-start.2 = (bf16[256,768]{1,0:T(8,128)(2,1)S(1)}, bf16[256,768]{1,0:T(8,128)(2,1)S(1)}, u32[]{:S(2)}, u32[]{:S(2)}) collective-permute-start(bf16[256,768]{1,0:T(8,128)(2,1)S(1)} %get-tuple-element.44), channel_id=1, source_target_pairs={{0,16},{16,0},{1,17},{17,1},{2,18},{18,2},{3,19},{19,3},{4,20},{20... | collective-permute-start | bytes 1179656 | tf_op jit(solution)/shard_map/ppermute | solution.py:29
  21.9 13.2 %collective-permute-start.8 = (bf16[256,384]{1,0:T(8,128)(2,1)S(1)}, bf16[256,384]{1,0:T(8,128)(2,1)S(1)}, u32[]{:S(2)}, u32[]{:S(2)}) collective-permute-start(bf16[256,384]{1,0:T(8,128)(2,1)S(1)} %collective-permute-done.forward_q.rest_2_), channel_id=1, source_target_pairs={{0,4},{4,8},{8,12},{12,14},{14,10},{10,6},{6,2},{2,0},{1,5},{5,9},... | collective-permute-start | bytes 589832 | tf_op jit(solution)/shard_map/ppermute | solution.py:45
  23.5 11.7 %collective-permute-start.9 = (bf16[256,384]{1,0:T(8,128)(2,1)S(1)}, bf16[256,384]{1,0:T(8,128)(2,1)S(1)}, u32[]{:S(2)}, u32[]{:S(2)}) collective-permute-start(bf16[256,384]{1,0:T(8,128)(2,1)S(1)} %collective-permute-done.1.backward_q.rest_3_), channel_id=1, source_target_pairs={{4,0},{8,4},{12,8},{14,12},{10,14},{6,10},{2,6},{0,2},{5,1},{9,5},... | collective-permute-start | bytes 589832 | tf_op jit(solution)/shard_map/ppermute | solution.py:45
  31.2 11.9 %collective-permute-start.11 = (bf16[272,640]{1,0:T(8,128)(2,1)S(1)}, bf16[272,640]{1,0:T(8,128)(2,1)S(1)}, u32[]{:S(2)}, u32[]{:S(2)}) collective-permute-start(bf16[272,640]{1,0:T(8,128)(2,1)S(1)} %get-tuple-element.57), channel_id=1, source_target_pairs={{0,4},{4,8},{8,12},{12,0},{1,5},{5,9},{9,13},{13,1},{2,6},{6,10},{... | collective-permute-start | bytes 1044488 | tf_op jit(solution)/shard_map/ppermute | solution.py:51
  37.1 9.6 %collective-permute-start.10 = (bf16[272,384]{1,0:T(8,128)(2,1)S(1)}, bf16[272,384]{1,0:T(8,128)(2,1)S(1)}, u32[]{:S(2)}, u32[]{:S(2)}) collective-permute-start(bf16[272,384]{1,0:T(8,128)(2,1)S(1)} %get-tuple-element.54), channel_id=1, source_target_pairs={{0,4},{4,8},{8,12},{12,0},{1,5},{5,9},{9,13},{13,1},{2,6},{6,10},{... | collective-permute-start | bytes 626696 | tf_op jit(solution)/shard_map/ppermute | solution.py:51
  42.5 6.6 %collective-permute-start.14 = (bf16[272,512]{1,0:T(8,128)(2,1)S(1)}, bf16[272,512]{1,0:T(8,128)(2,1)S(1)}, u32[]{:S(2)}, u32[]{:S(2)}) collective-permute-start(bf16[272,512]{1,0:T(8,128)(2,1)S(1)} %get-tuple-element.65), channel_id=1, source_target_pairs={{0,16},{16,0},{1,17},{17,1},{2,18},{18,2},{3,19},{19,3},{4,20},{20... | collective-permute-start | bytes 835592 | tf_op jit(solution)/shard_map/ppermute | solution.py:29
  43.8 11.2 %collective-permute-start.13 = (bf16[272,640]{1,0:T(8,128)(2,1)S(1)}, bf16[272,640]{1,0:T(8,128)(2,1)S(1)}, u32[]{:S(2)}, u32[]{:S(2)}) collective-permute-start(bf16[272,640]{1,0:T(8,128)(2,1)S(1)} %get-tuple-element.63), channel_id=1, source_target_pairs={{0,4},{4,8},{8,12},{12,0},{1,5},{5,9},{9,13},{13,1},{2,6},{6,10},{... | collective-permute-start | bytes 1044488 | tf_op jit(solution)/shard_map/ppermute | solution.py:51
  47.3 10.0 %collective-permute-start.12 = (bf16[272,384]{1,0:T(8,128)(2,1)S(1)}, bf16[272,384]{1,0:T(8,128)(2,1)S(1)}, u32[]{:S(2)}, u32[]{:S(2)}) collective-permute-start(bf16[272,384]{1,0:T(8,128)(2,1)S(1)} %get-tuple-element.61), channel_id=1, source_target_pairs={{0,4},{4,8},{8,12},{12,0},{1,5},{5,9},{9,13},{13,1},{2,6},{6,10},{... | collective-permute-start | bytes 626696 | tf_op jit(solution)/shard_map/ppermute | solution.py:51
  58.0 3.1 %collective-permute-start.15 = (f32[8,128]{1,0:T(8,128)S(1)}, f32[8,128]{1,0:T(8,128)S(1)}, u32[]{:S(2)}, u32[]{:S(2)}) collective-permute-start(f32[8,128]{1,0:T(8,128)S(1)} %get-tuple-element.69.refs_0_), channel_id=1, source_target_pairs={{0,1},{1,2},{2,3},{3,0},{4,5},{5,6},{6,7},{7,4},{8,9},{9,10},{10,1... | collective-permute-start | bytes 12296 | tf_op jit(solution)/shard_map/ppermute | solution.py:558
  58.1 3.7 %collective-permute-start.16 = (f32[8,128]{1,0:T(8,128)S(1)}, f32[8,128]{1,0:T(8,128)S(1)}, u32[]{:S(2)}, u32[]{:S(2)}) collective-permute-start(f32[8,128]{1,0:T(8,128)S(1)} %get-tuple-element.69.refs_0_), channel_id=1, source_target_pairs={{0,2},{1,3},{2,0},{3,1},{4,6},{5,7},{6,4},{7,5},{8,10},{9,11},{10,... | collective-permute-start | bytes 12296 | tf_op jit(solution)/shard_map/ppermute | solution.py:558
  58.4 3.4 %collective-permute-start.17 = (f32[8,128]{1,0:T(8,128)S(1)}, f32[8,128]{1,0:T(8,128)S(1)}, u32[]{:S(2)}, u32[]{:S(2)}) collective-permute-start(f32[8,128]{1,0:T(8,128)S(1)} %get-tuple-element.69.refs_0_), channel_id=1, source_target_pairs={{0,3},{1,0},{2,1},{3,2},{4,7},{5,4},{6,5},{7,6},{8,11},{9,8},{10,9... | collective-permute-start | bytes 12296 | tf_op jit(solution)/shard_map/ppermute | solution.py:558

commit v4 on v3

--- a/solution.py
+++ b/solution.py
@@ -21,6 +21,7 @@
 KEYS_COST = 2.0
 PACK_LIMIT = 49 * 1024 * 1024
 STAT_ROWS = 16
+FLAGS = 64
 HIDDEN = -1e30
 EXPONENT_SCALE = math.log2(math.e) / math.sqrt(HEAD_DIM)
 
@@ -45,9 +46,9 @@
     return lax.ppermute(block, ("cp", "tp"), route)
 
 
-def passed_up(block):
+def passed_up(block, wrap):
     count = lax.axis_size("cp")
-    route = [(i, (i + 1) % count) for i in range(count if WRAP else count - 1)]
+    route = [(i, (i + 1) % count) for i in range(count if wrap else count - 1)]
     return lax.ppermute(block, "cp", route)
 
 
@@ -186,29 +187,67 @@
     return keys, jnp.transpose(values)
 
 
-def crossing_flags(place_ref, ranges_ref, distance, slot, pair_count):
+def plan_kernel(pair_count, place_ref, ranges_ref, levels_ref, gate_table, *rest):
+    gates_out, flags_out = rest[-2:]
+    gates = gate_table[...].astype(jnp.float32)
+    level_ids = lax.broadcasted_iota(jnp.int32, gates.shape, 0)
+    gates_out[...] = jnp.zeros_like(gates_out)
+    for slot in range(pair_count):
+        level = levels_ref[place_ref[0] * pair_count + slot]
+        gates_out[slot : slot + 1, :] = jnp.sum(
+            jnp.where(level_ids == level, gates, 0.0), axis=0, keepdims=True
+        )
     group, position = place_ref[0], place_ref[1]
-    return [
-        shown(
-            place_ref,
-            ranges_ref,
-            group * pair_count + slot,
-            position + distance,
-            (group - behind) * pair_count + key_slot,
-            position,
-        )
-        for behind in range(2)
-        for key_slot in range(pair_count)
-    ]
+    flags_out[0] = place_ref[4]
+    index = 1
+    for distance in range(REACH + 1):
+        for slot in range(pair_count):
+            for behind in range(2):
+                for key_slot in range(pair_count):
+                    flag = shown(
+                        place_ref,
+                        ranges_ref,
+                        group * pair_count + slot,
+                        position + distance,
+                        (group - behind) * pair_count + key_slot,
+                        position,
+                    )
+                    flags_out[index] = flag.astype(jnp.int32)
+                    index += 1
+    for ahead in range(2):
+        for slot in range(pair_count):
+            for distance in range(REACH + 1):
+                for key_slot in range(pair_count):
+                    flag = shown(
+                        place_ref,
+                        ranges_ref,
+                        (group + ahead) * pair_count + slot,
+                        position,
+                        group * pair_count + key_slot,
+                        position - distance,
+                    )
+                    flags_out[index] = flag.astype(jnp.int32)
+                    index += 1
+
+
+def crossing_flags(flags_ref, distance, slot, pair_count):
+    base = 1 + (distance * pair_count + slot) * 2 * pair_count
+    return [flags_ref[base + j] == 1 for j in range(2 * pair_count)]
+
+
+def moved_flags(flags_ref, ahead, slot, pair_count):
+    count = (REACH + 1) * pair_count
+    base = 1 + count * 2 * pair_count + (ahead * pair_count + slot) * count
+    return [flags_ref[base + j] == 1 for j in range(count)]
 
 
 def far_kernel(
-    head_count, place_ref, ranges_ref, own_k, own_v, forward_q, backward_q, prior_kv, *rest,
+    head_count, flags_ref, own_k, own_v, forward_q, backward_q, prior_kv, *rest,
     base, pair_count,
 ):
     far_payload, far_stats = rest[-2:]
-    up = place_ref[4] == 1
-    seen = [crossing_flags(place_ref, ranges_ref, 2, slot, pair_count) for slot in range(pair_count)]
+    up = flags_ref[0] == 1
+    seen = [crossing_flags(flags_ref, 2, slot, pair_count) for slot in range(pair_count)]
     stats = [jnp.zeros((1, BLOCK), jnp.float32)] * STAT_ROWS
     for head in range(head_count):
         columns = head_columns(head)
@@ -223,13 +262,13 @@
 
 
 def near_kernel(
-    head_count, place_ref, ranges_ref, own_q, own_k, own_v, forward_q, backward_q, prior_kv,
+    head_count, flags_ref, own_q, own_k, own_v, forward_q, backward_q, prior_kv,
     *rest, base, pair_count,
 ):
     own_out, own_stats, near_out, near_stats = rest[-4:]
-    up = place_ref[4] == 1
+    up = flags_ref[0] == 1
     seen = {
-        (distance, slot): crossing_flags(place_ref, ranges_ref, distance, slot, pair_count)
+        (distance, slot): crossing_flags(flags_ref, distance, slot, pair_count)
         for distance in range(2)
         for slot in range(pair_count)
     }
@@ -252,11 +291,10 @@
 
 
 def keys_moved_kernel(
-    head_count, place_ref, ranges_ref, own_q, own_k, own_v, next_q, *rest, base, pair_count, counts
+    head_count, flags_ref, own_q, own_k, own_v, next_q, *rest, base, pair_count, counts
 ):
     own_out, own_stats, next_payload = rest[-3:]
-    group, position = place_ref[0], place_ref[1]
-    up = place_ref[4] == 1
+    up = flags_ref[0] == 1
     parts = len(counts)
     came = [
         [rest[2 * (hop * parts + part) : 2 * (hop * parts + part) + 2] for part in range(parts)]
@@ -271,18 +309,7 @@
         return pick(up, came[hop][part], slice(None), head_columns(unit))
 
     seen = {
-        (ahead, slot): [
-            shown(
-                place_ref,
-                ranges_ref,
-                (group + ahead) * pair_count + slot,
-                position,
-                group * pair_count + key_slot,
-                position - distance,
-            )
-            for distance in range(REACH + 1)
-            for key_slot in range(pair_count)
-        ]
+        (ahead, slot): moved_flags(flags_ref, ahead, slot, pair_count)
         for ahead in range(2)
         for slot in range(pair_count)
     }
@@ -364,18 +391,6 @@
         squares_out[slot : slot + 1, :] += total
 
 
-def gates_kernel(pair_count, place_ref, levels_ref, gate_table, *rest):
-    out = rest[-1]
-    gates = gate_table[...].astype(jnp.float32)
-    level_ids = lax.broadcasted_iota(jnp.int32, gates.shape, 0)
-    out[...] = jnp.zeros_like(out)
-    for slot in range(pair_count):
-        level = levels_ref[place_ref[0] * pair_count + slot]
-        out[slot : slot + 1, :] = jnp.sum(
-            jnp.where(level_ids == level, gates, 0.0), axis=0, keepdims=True
-        )
-
-
 def scale_kernel(head_counts, feature_count, device_count, *refs):
     squares = sum(ref[...] for ref in refs[:device_count])
     parts, out = refs[device_count:-1], refs[-1]
@@ -475,16 +490,19 @@
         hops[1].append((round_trip(forward, True), round_trip(backward, False)))
 
     own_parts, near_parts, arrived = [], [], []
-    gates = pl.pallas_call(
-        functools.partial(gates_kernel, pair_count),
-        out_shape=jax.ShapeDtypeStruct((8, width_dev), jnp.float32),
-        in_specs=[SMEM, SMEM, VMEM],
-        out_specs=VMEM,
+    gates, flags = pl.pallas_call(
+        functools.partial(plan_kernel, pair_count),
+        out_shape=(
+            jax.ShapeDtypeStruct((8, width_dev), jnp.float32),
+            jax.ShapeDtypeStruct((FLAGS,), jnp.int32),
+        ),
+        in_specs=[SMEM] * 3 + [VMEM],
+        out_specs=(VMEM, SMEM),
         compiler_params=PARAMS,
         cost_estimate=cost(0.6),
-        name="gates",
-    )(place, levels, gate_table)
-    turn = (gates,)
+        name="plan",
+    )(place, kv_ranges, levels, gate_table)
+    turn = ()
     for i in chunks:
         near = run(
             "near",
@@ -492,7 +510,7 @@
             i,
             NEAR_COST[i],
             (float_shape(i), stats_shape) * 2,
-            (place, kv_ranges),
+            (flags,),
             (queries, keys, values, *hops[0][i], prior_kv[i]),
             turn,
         )
@@ -504,12 +522,12 @@
             i,
             FAR_COST[i],
             (payload_shape(i), stats_shape),
-            (place, kv_ranges),
+            (flags,),
             (keys, values, *hops[1][i], prior_kv[i]),
             (near[1],),
         )
         turn = (far_stats,)
-        arrived.append(passed_up(far_payload))
+        arrived.append(passed_up(far_payload, True))
     own_out, own_stats, next_payload = run(
         "keys_moved",
         functools.partial(
@@ -518,7 +536,7 @@
         last,
         KEYS_COST,
         (float_shape(last), stats_shape, payload_shape(last)),
-        (place, kv_ranges),
+        (flags,),
         (queries, keys, values, prior_kv[0], *[ref for hop in hops for pair in hop for ref in pair]),
         turn,
     )
@@ -537,7 +555,7 @@
             turn,
         )
         turn = (relayed_stats,)
-        arrived[i] = passed_up(relayed)
+        arrived[i] = passed_up(relayed, i == 0)
     squares = jnp.zeros(squares_shape.shape, jnp.float32)
     finished = [None] * len(head_counts)
     for i in FINISH_ORDER:

time: 63.8 us -> 60.4 us (0.947)
  waiting for transfers between devices: 23.3 us -> 19.2 us
  starting transfers between devices: 18.4 us -> 19.2 us
    ppermute x3, waiting for transfers between devices: 1.69 us -> 0.01 us  [exchanged(): return lax.ppermute(block, 'stretch', [(0, 1), (1, 0)])]
    pallas_call x10, Pallas kernels: 16.9 us -> 15.6 us  [run(): pl.pallas_call(functools.partial(kernel, head_counts[chunk]), out_shape=o...]
    pallas_call x1, Pallas kernels: 0.59 us -> 1.68 us  [on_device(): pl.pallas_call(functools.partial(plan_kernel, pair_count), out_shape=(jax...]
    ppermute x4, waiting for transfers between devices: 8.03 us -> 7.02 us  [passed_up(): return lax.ppermute(block, 'cp', route)]
    ppermute x8, waiting for transfers between devices: 11.7 us -> 10.8 us  [round_trip(): return lax.ppermute(block, ('cp', 'tp'), route)]
    ppermute x3, starting transfers between devices: 1.82 us -> 2.48 us  [on_device(): shares.append(lax.ppermute(squares, 'tp', route))]
  transfers between devices with their start and end apart: 18 -> 18, of which waited for: 12 -> 11; matrix products, arithmetic and copies ran while one was open for 0% -> 0% of each run, Pallas kernels for 27% -> 28%
where the time goes in v4:
time: 60.4 us; the launch traced here: 59.5 us
  Pallas kernels  20.8 us (34%)
  starting transfers between devices  19.2 us (32%)
  waiting for transfers between devices  19.2 us (32%)
    pallas_call x10, Pallas kernels, run(): pl.pallas_call(functools.partial(kernel, head_counts[chunk]), out_shape=o...  15.6 us
    ppermute x8, waiting for transfers between devices, round_trip(): return lax.ppermute(block, ('cp', 'tp'), route)  10.8 us
    ppermute x8, starting transfers between devices, round_trip(): return lax.ppermute(block, ('cp', 'tp'), route)  8.1 us
    ppermute x4, waiting for transfers between devices, passed_up(): return lax.ppermute(block, 'cp', route)  7.02 us
    ppermute x4, starting transfers between devices, passed_up(): return lax.ppermute(block, 'cp', route)  5.03 us
    ppermute x3, starting transfers between devices, exchanged(): return lax.ppermute(block, 'stretch', [(0, 1), (1, 0)])  3.63 us
    ppermute x3, starting transfers between devices, on_device(): shares.append(lax.ppermute(squares, 'tp', route))  2.48 us
    pallas_call x1, Pallas kernels, on_device(): pl.pallas_call(functools.partial(pack_kernel, CHUNKS, KEYS_MOVED), out_sh...  2.37 us
  transfers between devices with their start and end apart: 18, of which 11 were waited for; matrix products, arithmetic and copies ran while one was open for 0% of the time, Pallas kernels for 28%

profile of v4, /device:TPU:0, one launch (start us, length us, event | category | flops | bytes accessed | tf_op | source)
XLA Modules:
  0.0 59.5 jit_solution(6457776461901354847)
XLA Ops:
  0.0 0.1 pad_add_fusion.place_ref
  0.1 0.0 copy-start
  0.1 0.0 copy-start.1
  0.1 2.4 %pack.1 = (bf16[256,1536]{1,0:T(8,128)(2,1)S(1)}, bf16[256,1536]{1,0:T(8,128)(2,1)S(1)}, bf16[256,1536]{1,0:T(8,128)(2,1)S(1)}, bf16[256,1280]{1,0:T(8,128)(2,1)...) custom-call(s32[5]{0:T(128)S(1)} %pad_add_fusion.place_ref, ...), custom_call_target="tpu_custom_call" | custom-call | flops 1000000000 | bytes 1000000 | tf_op jit(solution)/shard_map/pack/pallas_call | solution.py:471
  2.5 3.0 %collective-permute-start.7 = (bf16[256,1280]{1,0:T(8,128)(2,1)S(1)}, bf16[256,1280]{1,0:T(8,128)(2,1)S(1)}, u32[]{:S(2)}, u32[]{:S(2)}) collective-permute-start(bf16[256,1280]{1,0:T(8,128)(2,1)S(1)} %get-tuple-element.50), channel_id=1, source_target_pairs={{0,16},{16,0},{1,17},{17,1},{2,18},{18,2},{3,19},{19,3},{4,20},{20... | collective-permute-start | bytes 1966088 | tf_op jit(solution)/shard_map/ppermute | solution.py:30
  5.5 1.6 %collective-permute-start.3 = (bf16[256,640]{1,0:T(8,128)(2,1)S(1)}, bf16[256,640]{1,0:T(8,128)(2,1)S(1)}, u32[]{:S(2)}, u32[]{:S(2)}) collective-permute-start(bf16[256,640]{1,0:T(8,128)(2,1)S(1)} %get-tuple-element.48), channel_id=1, source_target_pairs={{0,4},{4,8},{8,12},{12,14},{14,10},{10,6},{6,2},{2,0},{1,5},{5,9},... | collective-permute-start | bytes 983048 | tf_op jit(solution)/shard_map/ppermute | solution.py:46
  7.1 0.4 collective-permute-start.5
  7.5 0.0 copy-start.2
  7.5 1.6 %collective-permute-start = (bf16[256,384]{1,0:T(8,128)(2,1)S(1)}, bf16[256,384]{1,0:T(8,128)(2,1)S(1)}, u32[]{:S(2)}, u32[]{:S(2)}) collective-permute-start(bf16[256,384]{1,0:T(8,128)(2,1)S(1)} %get-tuple-element.45), channel_id=1, source_target_pairs={{0,4},{4,8},{8,12},{12,14},{14,10},{10,6},{6,2},{2,0},{1,5},{5,9},... | collective-permute-start | bytes 589832 | tf_op jit(solution)/shard_map/ppermute | solution.py:46
  9.1 0.4 collective-permute-start.1
  9.5 6.6 %collective-permute-done.3.forward_q.rest_0_ = bf16[256,640]{1,0:T(8,128)(2,1)S(1)} collective-permute-done((bf16[256,640]{1,0:T(8,128)(2,1)S(1)}, bf16[256,640]{1,0:T(8,128)(2,1)S(1)}, u32[]{:S(2)}, u32[]{:S(2)}) %collective-permute-start.3) | collective-permute-done | bytes 327712 | tf_op jit(solution)/shard_map/ppermute | solution.py:46
  16.1 1.6 %collective-permute-start.4 = (bf16[256,640]{1,0:T(8,128)(2,1)S(1)}, bf16[256,640]{1,0:T(8,128)(2,1)S(1)}, u32[]{:S(2)}, u32[]{:S(2)}) collective-permute-start(bf16[256,640]{1,0:T(8,128)(2,1)S(1)} %collective-permute-done.3.forward_q.rest_0_), channel_id=1, source_target_pairs={{0,4},{4,8},{8,12},{12,14},{14,10},{10,6},{6,2},{2,0},{1,5},{5,9},... | collective-permute-start | bytes 983048 | tf_op jit(solution)/shard_map/ppermute | solution.py:46
  17.7 0.0 collective-permute-done.5.backward_q.rest_1_
  17.7 0.4 collective-permute-start.6
  18.2 0.0 copy-done
  18.2 0.0 copy-done.1
  18.2 0.0 copy-done.2
  18.2 1.7 %plan.1 = (f32[8,1536]{1,0:T(8,128)S(1)}, s32[64]{0:T(128)S(1)}) custom-call(s32[5]{0:T(128)S(1)} %pad_add_fusion.place_ref, s32[2,4,4,4]{3,2,1,0:T(4,128)S(1)} %copy-done.1, s32[4]{0:T(128)S(1)} %copy-done.2, bf16[16,1536]{1,0:T(8,128)(2,1)S(1)} %copy-done), custom_call_target="tpu_custom_call" | custom-call | flops 600000000 | bytes 600000 | tf_op jit(solution)/shard_map/plan/pallas_call | solution.py:493
  19.9 0.5 collective-permute-done.forward_q.rest_2_
  20.3 0.0 collective-permute-start.2
  20.4 1.6 %collective-permute-done.1.backward_q.rest_3_ = bf16[256,384]{1,0:T(8,128)(2,1)S(1)} collective-permute-done((bf16[256,384]{1,0:T(8,128)(2,1)S(1)}, bf16[256,384]{1,0:T(8,128)(2,1)S(1)}, u32[]{:S(2)}, u32[]{:S(2)}) %collective-permute-start.1) | collective-permute-done | bytes 196640 | tf_op jit(solution)/shard_map/ppermute | solution.py:46
  21.9 1.6 %collective-permute-start.8 = (bf16[256,384]{1,0:T(8,128)(2,1)S(1)}, bf16[256,384]{1,0:T(8,128)(2,1)S(1)}, u32[]{:S(2)}, u32[]{:S(2)}) collective-permute-start(bf16[256,384]{1,0:T(8,128)(2,1)S(1)} %collective-permute-done.forward_q.rest_2_), channel_id=1, source_target_pairs={{0,4},{4,8},{8,12},{12,14},{14,10},{10,6},{6,2},{2,0},{1,5},{5,9},... | collective-permute-start | bytes 589832 | tf_op jit(solution)/shard_map/ppermute | solution.py:46
  23.5 0.0 collective-permute-done.7.prior_kv.next_q
  23.5 0.5 collective-permute-start.9
  24.0 2.8 %near.2 = (f32[256,640]{1,0:T(8,128)S(1)}, f32[16,128]{1,0:T(8,128)S(1)}, f32[256,640]{1,0:T(8,128)S(1)}, f32[16,128]{1,0:T(8,128)S(1)}) custom-call(s32[64]{0:T(128)S(1)} %get-tuple-element.41.flags_ref, bf16[256,1536]{1,0:T(8,128)(2,1)S(1)} %get-tuple-element.42.own_q, bf16[256,1536]{1,0:T(8,128)(2,1)S(1)} %get-tuple-element.43.own_k, ...), custom_call_target="tpu_custom_call" | custom-call | flops 3000000000 | bytes 3000000 | tf_op jit(solution)/shard_map/near/pallas_call | solution.py:456
  26.8 0.6 %collective-permute-done.4.forward_q.rest_4_ = bf16[256,640]{1,0:T(8,128)(2,1)S(1)} collective-permute-done((bf16[256,640]{1,0:T(8,128)(2,1)S(1)}, bf16[256,640]{1,0:T(8,128)(2,1)S(1)}, u32[]{:S(2)}, u32[]{:S(2)}) %collective-permute-start.4) | collective-permute-done | bytes 327712 | tf_op jit(solution)/shard_map/ppermute | solution.py:46
  27.4 1.6 %collective-permute-done.6.backward_q.rest_5_ = bf16[256,640]{1,0:T(8,128)(2,1)S(1)} collective-permute-done((bf16[256,640]{1,0:T(8,128)(2,1)S(1)}, bf16[256,640]{1,0:T(8,128)(2,1)S(1)}, u32[]{:S(2)}, u32[]{:S(2)}) %collective-permute-start.6) | collective-permute-done | bytes 327712 | tf_op jit(solution)/shard_map/ppermute | solution.py:46
  28.9 2.0 %far.2 = (bf16[272,640]{1,0:T(8,128)(2,1)S(1)}, f32[16,128]{1,0:T(8,128)S(1)}) custom-call(s32[64]{0:T(128)S(1)} %get-tuple-element.41.flags_ref, bf16[256,1536]{1,0:T(8,128)(2,1)S(1)} %get-tuple-element.43.own_k, bf16[256,1536]{1,0:T(8,128)(2,1)S(1)} %get-tuple-element.44.own_v, bf16[256,640]{1,0:T(8,128)(2,1)S(1)} %collective-permute-done.4.forward_q.rest_4_, ...), custom_call_target="tpu_custom_call" | custom-call | flops 1500000000 | bytes 1500000 | tf_op jit(solution)/shard_map/far/pallas_call | solution.py:456
  30.9 1.6 %collective-permute-start.11 = (bf16[272,640]{1,0:T(8,128)(2,1)S(1)}, bf16[272,640]{1,0:T(8,128)(2,1)S(1)}, u32[]{:S(2)}, u32[]{:S(2)}) collective-permute-start(bf16[272,640]{1,0:T(8,128)(2,1)S(1)} %get-tuple-element.60), channel_id=1, source_target_pairs={{0,4},{4,8},{8,12},{12,0},{1,5},{5,9},{9,13},{13,1},{2,6},{6,10},{... | collective-permute-start | bytes 1044488 | tf_op jit(solution)/shard_map/ppermute | solution.py:52
  32.5 0.0 collective-permute-done.2.prior_kv
  32.5 2.1 %near.3 = (f32[256,384]{1,0:T(8,128)S(1)}, f32[16,128]{1,0:T(8,128)S(1)}, f32[256,384]{1,0:T(8,128)S(1)}, f32[16,128]{1,0:T(8,128)S(1)}) custom-call(s32[64]{0:T(128)S(1)} %get-tuple-element.41.flags_ref, bf16[256,1536]{1,0:T(8,128)(2,1)S(1)} %get-tuple-element.42.own_q, bf16[256,1536]{1,0:T(8,128)(2,1)S(1)} %get-tuple-element.43.own_k, ...), custom_call_target="tpu_custom_call" | custom-call | flops 1800000000 | bytes 1800000 | tf_op jit(solution)/shard_map/near/pallas_call | solution.py:456
  34.7 0.0 collective-permute-done.8.forward_q.rest_6_
  34.7 0.0 collective-permute-done.9.backward_q.rest_7_
  34.7 1.6 %far.3 = (bf16[272,384]{1,0:T(8,128)(2,1)S(1)}, f32[16,128]{1,0:T(8,128)S(1)}) custom-call(s32[64]{0:T(128)S(1)} %get-tuple-element.41.flags_ref, bf16[256,1536]{1,0:T(8,128)(2,1)S(1)} %get-tuple-element.43.own_k, bf16[256,1536]{1,0:T(8,128)(2,1)S(1)} %get-tuple-element.44.own_v, bf16[256,384]{1,0:T(8,128)(2,1)S(1)} %collective-permute-done.8.forward_q.rest_6_, ...), custom_call_target="tpu_custom_call" | custom-call | flops 900000000 | bytes 900000 | tf_op jit(solution)/shard_map/far/pallas_call | solution.py:456
  36.3 1.6 %collective-permute-start.10 = (bf16[272,384]{1,0:T(8,128)(2,1)S(1)}, bf16[272,384]{1,0:T(8,128)(2,1)S(1)}, u32[]{:S(2)}, u32[]{:S(2)}) collective-permute-start(bf16[272,384]{1,0:T(8,128)(2,1)S(1)} %get-tuple-element.57), channel_id=1, source_target_pairs={{0,4},{4,8},{8,12},{12,0},{1,5},{5,9},{9,13},{13,1},{2,6},{6,10},{... | collective-permute-start | bytes 626696 | tf_op jit(solution)/shard_map/ppermute | solution.py:52
  37.9 3.5 %keys_moved.1 = (f32[256,512]{1,0:T(8,128)S(1)}, f32[16,128]{1,0:T(8,128)S(1)}, bf16[272,512]{1,0:T(8,128)(2,1)S(1)}) custom-call(s32[64]{0:T(128)S(1)} %get-tuple-element.41.flags_ref, bf16[256,1536]{1,0:T(8,128)(2,1)S(1)} %get-tuple-element.42.own_q, bf16[256,1536]{1,0:T(8,128)(2,1)S(1)} %get-tuple-element.43.own_k, ...), custom_call_target="tpu_custom_call" | custom-call | flops 2000000000 | bytes 2000000 | tf_op jit(solution)/shard_map/keys_moved/pallas_call | solution.py:456
  41.4 0.6 collective-permute-start.14
  42.0 1.1 %collective-permute-done.11.payload_in = bf16[272,640]{1,0:T(8,128)(2,1)S(1)} collective-permute-done((bf16[272,640]{1,0:T(8,128)(2,1)S(1)}, bf16[272,640]{1,0:T(8,128)(2,1)S(1)}, u32[]{:S(2)}, u32[]{:S(2)}) %collective-permute-start.11) | collective-permute-done | bytes 348192 | tf_op jit(solution)/shard_map/ppermute | solution.py:52
  43.1 0.7 %relay.2 = (bf16[272,640]{1,0:T(8,128)(2,1)S(1)}, f32[16,128]{1,0:T(8,128)S(1)}) custom-call(s32[5]{0:T(128)S(1)} %pad_add_fusion.place_ref, f32[256,640]{1,0:T(8,128)S(1)} %get-tuple-element.58.local_out, f32[16,128]{1,0:T(8,128)S(1)} %get-tuple-element.59.local_stats, bf16[272,640]{1,0:T(8,128)(2,1)S(1)} %collective-permute-done.11.payload_in, ...), custom_call_target="tpu_custom_call" | custom-call | flops 700000000 | bytes 700000 | tf_op jit(solution)/shard_map/relay/pallas_call | solution.py:456
  43.8 0.5 collective-permute-start.13
  44.3 3.2 %collective-permute-done.10.payload_in = bf16[272,384]{1,0:T(8,128)(2,1)S(1)} collective-permute-done((bf16[272,384]{1,0:T(8,128)(2,1)S(1)}, bf16[272,384]{1,0:T(8,128)(2,1)S(1)}, u32[]{:S(2)}, u32[]{:S(2)}) %collective-permute-start.10) | collective-permute-done | bytes 208928 | tf_op jit(solution)/shard_map/ppermute | solution.py:52
  47.5 0.6 %relay.3 = (bf16[272,384]{1,0:T(8,128)(2,1)S(1)}, f32[16,128]{1,0:T(8,128)S(1)}) custom-call(s32[5]{0:T(128)S(1)} %pad_add_fusion.place_ref, f32[256,384]{1,0:T(8,128)S(1)} %get-tuple-element.55.local_out, f32[16,128]{1,0:T(8,128)S(1)} %get-tuple-element.56.local_stats, bf16[272,384]{1,0:T(8,128)(2,1)S(1)} %collective-permute-done.10.payload_in, ...), custom_call_target="tpu_custom_call" | custom-call | flops 700000000 | bytes 700000 | tf_op jit(solution)/shard_map/relay/pallas_call | solution.py:456
  48.1 1.3 %collective-permute-start.12 = (bf16[272,384]{1,0:T(8,128)(2,1)S(1)}, bf16[272,384]{1,0:T(8,128)(2,1)S(1)}, u32[]{:S(2)}, u32[]{:S(2)}) collective-permute-start(bf16[272,384]{1,0:T(8,128)(2,1)S(1)} %get-tuple-element.64), channel_id=1, source_target_pairs={{0,4},{4,8},{8,12},{1,5},{5,9},{9,13},{2,6},{6,10},{10,14},{3,7},{... | collective-permute-start | bytes 626696 | tf_op jit(solution)/shard_map/ppermute | solution.py:52
  49.4 0.0 collective-permute-done.14.payload_in
  49.5 0.8 %finish.3 = (f32[256,512]{1,0:T(8,128)S(1)}, f32[8,128]{1,0:T(8,128)S(1)}) custom-call(s32[5]{0:T(128)S(1)} %pad_add_fusion.place_ref, f32[256,512]{1,0:T(8,128)S(1)} %get-tuple-element.68.local_out, f32[16,128]{1,0:T(8,128)S(1)} %get-tuple-element.62.rest_0_.local_stats, bf16[272,512]{1,0:T(8,128)(2,1)S(1)} %collective-permute-done.14.payload_in, ...), custom_call_target="tpu_custom_call" | custom-call | flops 800000000 | bytes 800000 | tf_op jit(solution)/shard_map/finish/pallas_call | solution.py:456
  50.2 2.7 %collective-permute-done.13.payload_in = bf16[272,640]{1,0:T(8,128)(2,1)S(1)} collective-permute-done((bf16[272,640]{1,0:T(8,128)(2,1)S(1)}, bf16[272,640]{1,0:T(8,128)(2,1)S(1)}, u32[]{:S(2)}, u32[]{:S(2)}) %collective-permute-start.13) | collective-permute-done | bytes 348192 | tf_op jit(solution)/shard_map/ppermute | solution.py:52
  53.0 0.8 %finish.4 = (f32[256,640]{1,0:T(8,128)S(1)}, f32[8,128]{1,0:T(8,128)S(1)}) custom-call(s32[5]{0:T(128)S(1)} %pad_add_fusion.place_ref, f32[256,640]{1,0:T(8,128)S(1)} %get-tuple-element.66.local_out, f32[16,128]{1,0:T(8,128)S(1)} %get-tuple-element.51.rest_0_.local_stats, bf16[272,640]{1,0:T(8,128)(2,1)S(1)} %collective-permute-done.13.payload_in, ...), custom_call_target="tpu_custom_call" | custom-call | flops 800000000 | bytes 800000 | tf_op jit(solution)/shard_map/finish/pallas_call | solution.py:456
  53.8 0.0 collective-permute-done.12.payload_in
  53.8 0.7 %finish.5 = (f32[256,384]{1,0:T(8,128)S(1)}, f32[8,128]{1,0:T(8,128)S(1)}) custom-call(s32[5]{0:T(128)S(1)} %pad_add_fusion.place_ref, f32[256,384]{1,0:T(8,128)S(1)} %get-tuple-element.53.local_out, f32[16,128]{1,0:T(8,128)S(1)} %get-tuple-element.54.rest_0_.local_stats, bf16[272,384]{1,0:T(8,128)(2,1)S(1)} %collective-permute-done.12.payload_in, ...), custom_call_target="tpu_custom_call" | custom-call | flops 800000000 | bytes 800000 | tf_op jit(solution)/shard_map/finish/pallas_call | solution.py:456
  54.5 0.1 collective-permute-start.15
  54.6 1.0 %collective-permute-start.16 = (f32[8,128]{1,0:T(8,128)S(1)}, f32[8,128]{1,0:T(8,128)S(1)}, u32[]{:S(2)}, u32[]{:S(2)}) collective-permute-start(f32[8,128]{1,0:T(8,128)S(1)} %get-tuple-element.73.refs_0_), channel_id=1, source_target_pairs={{0,2},{1,3},{2,0},{3,1},{4,6},{5,7},{6,4},{7,5},{8,10},{9,11},{10,... | collective-permute-start | bytes 12296 | tf_op jit(solution)/shard_map/ppermute | solution.py:576
  55.6 1.4 %collective-permute-start.17 = (f32[8,128]{1,0:T(8,128)S(1)}, f32[8,128]{1,0:T(8,128)S(1)}, u32[]{:S(2)}, u32[]{:S(2)}) collective-permute-start(f32[8,128]{1,0:T(8,128)S(1)} %get-tuple-element.73.refs_0_), channel_id=1, source_target_pairs={{0,3},{1,0},{2,1},{3,2},{4,7},{5,4},{6,5},{7,6},{8,11},{9,8},{10,9... | collective-permute-start | bytes 12296 | tf_op jit(solution)/shard_map/ppermute | solution.py:576
  57.0 0.6 %collective-permute-done.15.refs_1_ = f32[8,128]{1,0:T(8,128)S(1)} collective-permute-done((f32[8,128]{1,0:T(8,128)S(1)}, f32[8,128]{1,0:T(8,128)S(1)}, u32[]{:S(2)}, u32[]{:S(2)}) %collective-permute-start.15) | collective-permute-done | bytes 4128 | tf_op jit(solution)/shard_map/ppermute | solution.py:576
  57.6 0.7 %collective-permute-done.16.refs_2_ = f32[8,128]{1,0:T(8,128)S(1)} collective-permute-done((f32[8,128]{1,0:T(8,128)S(1)}, f32[8,128]{1,0:T(8,128)S(1)}, u32[]{:S(2)}, u32[]{:S(2)}) %collective-permute-start.16) | collective-permute-done | bytes 4128 | tf_op jit(solution)/shard_map/ppermute | solution.py:576
  58.3 0.1 collective-permute-done.17.refs_3_
  58.4 1.2 %scale.1 = bf16[256,1536]{1,0:T(8,128)(2,1)} custom-call(f32[8,128]{1,0:T(8,128)S(1)} %get-tuple-element.73.refs_0_, f32[8,128]{1,0:T(8,128)S(1)} %collective-permute-done.15.refs_1_, f32[8,128]{1,0:T(8,128)S(1)} %collective-permute-done.16.refs_2_, f32[8,128]{1,0:T(8,128)S(1)} %collective-permute-done.17.refs_3_, f32[256,640]{1,0:T(8,128)S(1)} %get-tuple-element.74.refs_4_, ...), custom_call_target="tpu_custom_call" | custom-call | tf_op jit(solution)/shard_map/scale/pallas_call | solution.py:577
  (2 shorter events, 0.0 us)
Async XLA Ops:
  0.1 18.1 %copy-start = (bf16[16,1536]{1,0:T(8,128)(2,1)S(1)}, bf16[16,1536]{1,0:T(8,128)(2,1)}, u32[]{:S(2)}) copy-start(bf16[16,1536]{1,0:T(8,128)(2,1)} %gate_table.1) | copy-start | bytes 147460
  0.1 18.1 %copy-start.1 = (s32[2,4,4,4]{3,2,1,0:T(4,128)S(1)}, s32[2,4,4,4]{3,2,1,0:T(4,128)}, u32[]{:S(2)}) copy-start(s32[2,4,4,4]{3,2,1,0:T(4,128)} %ranges_ref.1) | copy-start | bytes 1540
  2.5 21.0 %collective-permute-start.7 = (bf16[256,1280]{1,0:T(8,128)(2,1)S(1)}, bf16[256,1280]{1,0:T(8,128)(2,1)S(1)}, u32[]{:S(2)}, u32[]{:S(2)}) collective-permute-start(bf16[256,1280]{1,0:T(8,128)(2,1)S(1)} %get-tuple-element.50), channel_id=1, source_target_pairs={{0,16},{16,0},{1,17},{17,1},{2,18},{18,2},{3,19},{19,3},{4,20},{20... | collective-permute-start | bytes 1966088 | tf_op jit(solution)/shard_map/ppermute | solution.py:30
  5.5 10.6 %collective-permute-start.3 = (bf16[256,640]{1,0:T(8,128)(2,1)S(1)}, bf16[256,640]{1,0:T(8,128)(2,1)S(1)}, u32[]{:S(2)}, u32[]{:S(2)}) collective-permute-start(bf16[256,640]{1,0:T(8,128)(2,1)S(1)} %get-tuple-element.48), channel_id=1, source_target_pairs={{0,4},{4,8},{8,12},{12,14},{14,10},{10,6},{6,2},{2,0},{1,5},{5,9},... | collective-permute-start | bytes 983048 | tf_op jit(solution)/shard_map/ppermute | solution.py:46
  7.1 10.7 %collective-permute-start.5 = (bf16[256,640]{1,0:T(8,128)(2,1)S(1)}, bf16[256,640]{1,0:T(8,128)(2,1)S(1)}, u32[]{:S(2)}, u32[]{:S(2)}) collective-permute-start(bf16[256,640]{1,0:T(8,128)(2,1)S(1)} %get-tuple-element.49), channel_id=1, source_target_pairs={{4,0},{8,4},{12,8},{14,12},{10,14},{6,10},{2,6},{0,2},{5,1},{9,5},... | collective-permute-start | bytes 983048 | tf_op jit(solution)/shard_map/ppermute | solution.py:46
  7.5 10.7 %copy-start.2 = (s32[4]{0:T(128)S(1)}, s32[4]{0:T(128)}, u32[]{:S(2)}) copy-start(s32[4]{0:T(128)} %levels_ref.1) | copy-start | bytes 52
  7.5 12.8 %collective-permute-start = (bf16[256,384]{1,0:T(8,128)(2,1)S(1)}, bf16[256,384]{1,0:T(8,128)(2,1)S(1)}, u32[]{:S(2)}, u32[]{:S(2)}) collective-permute-start(bf16[256,384]{1,0:T(8,128)(2,1)S(1)} %get-tuple-element.45), channel_id=1, source_target_pairs={{0,4},{4,8},{8,12},{12,14},{14,10},{10,6},{6,2},{2,0},{1,5},{5,9},... | collective-permute-start | bytes 589832 | tf_op jit(solution)/shard_map/ppermute | solution.py:46
  9.1 12.8 %collective-permute-start.1 = (bf16[256,384]{1,0:T(8,128)(2,1)S(1)}, bf16[256,384]{1,0:T(8,128)(2,1)S(1)}, u32[]{:S(2)}, u32[]{:S(2)}) collective-permute-start(bf16[256,384]{1,0:T(8,128)(2,1)S(1)} %get-tuple-element.46), channel_id=1, source_target_pairs={{4,0},{8,4},{12,8},{14,12},{10,14},{6,10},{2,6},{0,2},{5,1},{9,5},... | collective-permute-start | bytes 589832 | tf_op jit(solution)/shard_map/ppermute | solution.py:46
  16.1 11.2 %collective-permute-start.4 = (bf16[256,640]{1,0:T(8,128)(2,1)S(1)}, bf16[256,640]{1,0:T(8,128)(2,1)S(1)}, u32[]{:S(2)}, u32[]{:S(2)}) collective-permute-start(bf16[256,640]{1,0:T(8,128)(2,1)S(1)} %collective-permute-done.3.forward_q.rest_0_), channel_id=1, source_target_pairs={{0,4},{4,8},{8,12},{12,14},{14,10},{10,6},{6,2},{2,0},{1,5},{5,9},... | collective-permute-start | bytes 983048 | tf_op jit(solution)/shard_map/ppermute | solution.py:46
  17.7 11.2 %collective-permute-start.6 = (bf16[256,640]{1,0:T(8,128)(2,1)S(1)}, bf16[256,640]{1,0:T(8,128)(2,1)S(1)}, u32[]{:S(2)}, u32[]{:S(2)}) collective-permute-start(bf16[256,640]{1,0:T(8,128)(2,1)S(1)} %collective-permute-done.5.backward_q.rest_1_), channel_id=1, source_target_pairs={{4,0},{8,4},{12,8},{14,12},{10,14},{6,10},{2,6},{0,2},{5,1},{9,5},... | collective-permute-start | bytes 983048 | tf_op jit(solution)/shard_map/ppermute | solution.py:46
  20.3 12.2 %collective-permute-start.2 = (bf16[256,768]{1,0:T(8,128)(2,1)S(1)}, bf16[256,768]{1,0:T(8,128)(2,1)S(1)}, u32[]{:S(2)}, u32[]{:S(2)}) collective-permute-start(bf16[256,768]{1,0:T(8,128)(2,1)S(1)} %get-tuple-element.47), channel_id=1, source_target_pairs={{0,16},{16,0},{1,17},{17,1},{2,18},{18,2},{3,19},{19,3},{4,20},{20... | collective-permute-start | bytes 1179656 | tf_op jit(solution)/shard_map/ppermute | solution.py:30
  21.9 12.7 %collective-permute-start.8 = (bf16[256,384]{1,0:T(8,128)(2,1)S(1)}, bf16[256,384]{1,0:T(8,128)(2,1)S(1)}, u32[]{:S(2)}, u32[]{:S(2)}) collective-permute-start(bf16[256,384]{1,0:T(8,128)(2,1)S(1)} %collective-permute-done.forward_q.rest_2_), channel_id=1, source_target_pairs={{0,4},{4,8},{8,12},{12,14},{14,10},{10,6},{6,2},{2,0},{1,5},{5,9},... | collective-permute-start | bytes 589832 | tf_op jit(solution)/shard_map/ppermute | solution.py:46
  23.5 11.2 %collective-permute-start.9 = (bf16[256,384]{1,0:T(8,128)(2,1)S(1)}, bf16[256,384]{1,0:T(8,128)(2,1)S(1)}, u32[]{:S(2)}, u32[]{:S(2)}) collective-permute-start(bf16[256,384]{1,0:T(8,128)(2,1)S(1)} %collective-permute-done.1.backward_q.rest_3_), channel_id=1, source_target_pairs={{4,0},{8,4},{12,8},{14,12},{10,14},{6,10},{2,6},{0,2},{5,1},{9,5},... | collective-permute-start | bytes 589832 | tf_op jit(solution)/shard_map/ppermute | solution.py:46
  30.9 12.2 %collective-permute-start.11 = (bf16[272,640]{1,0:T(8,128)(2,1)S(1)}, bf16[272,640]{1,0:T(8,128)(2,1)S(1)}, u32[]{:S(2)}, u32[]{:S(2)}) collective-permute-start(bf16[272,640]{1,0:T(8,128)(2,1)S(1)} %get-tuple-element.60), channel_id=1, source_target_pairs={{0,4},{4,8},{8,12},{12,0},{1,5},{5,9},{9,13},{13,1},{2,6},{6,10},{... | collective-permute-start | bytes 1044488 | tf_op jit(solution)/shard_map/ppermute | solution.py:52
  36.3 11.2 %collective-permute-start.10 = (bf16[272,384]{1,0:T(8,128)(2,1)S(1)}, bf16[272,384]{1,0:T(8,128)(2,1)S(1)}, u32[]{:S(2)}, u32[]{:S(2)}) collective-permute-start(bf16[272,384]{1,0:T(8,128)(2,1)S(1)} %get-tuple-element.57), channel_id=1, source_target_pairs={{0,4},{4,8},{8,12},{12,0},{1,5},{5,9},{9,13},{13,1},{2,6},{6,10},{... | collective-permute-start | bytes 626696 | tf_op jit(solution)/shard_map/ppermute | solution.py:52
  41.4 8.0 %collective-permute-start.14 = (bf16[272,512]{1,0:T(8,128)(2,1)S(1)}, bf16[272,512]{1,0:T(8,128)(2,1)S(1)}, u32[]{:S(2)}, u32[]{:S(2)}) collective-permute-start(bf16[272,512]{1,0:T(8,128)(2,1)S(1)} %get-tuple-element.69), channel_id=1, source_target_pairs={{0,16},{16,0},{1,17},{17,1},{2,18},{18,2},{3,19},{19,3},{4,20},{20... | collective-permute-start | bytes 835592 | tf_op jit(solution)/shard_map/ppermute | solution.py:30
  43.8 9.1 %collective-permute-start.13 = (bf16[272,640]{1,0:T(8,128)(2,1)S(1)}, bf16[272,640]{1,0:T(8,128)(2,1)S(1)}, u32[]{:S(2)}, u32[]{:S(2)}) collective-permute-start(bf16[272,640]{1,0:T(8,128)(2,1)S(1)} %get-tuple-element.67), channel_id=1, source_target_pairs={{0,4},{4,8},{8,12},{12,0},{1,5},{5,9},{9,13},{13,1},{2,6},{6,10},{... | collective-permute-start | bytes 1044488 | tf_op jit(solution)/shard_map/ppermute | solution.py:52
  48.1 5.6 %collective-permute-start.12 = (bf16[272,384]{1,0:T(8,128)(2,1)S(1)}, bf16[272,384]{1,0:T(8,128)(2,1)S(1)}, u32[]{:S(2)}, u32[]{:S(2)}) collective-permute-start(bf16[272,384]{1,0:T(8,128)(2,1)S(1)} %get-tuple-element.64), channel_id=1, source_target_pairs={{0,4},{4,8},{8,12},{1,5},{5,9},{9,13},{2,6},{6,10},{10,14},{3,7},{... | collective-permute-start | bytes 626696 | tf_op jit(solution)/shard_map/ppermute | solution.py:52
  54.5 3.1 %collective-permute-start.15 = (f32[8,128]{1,0:T(8,128)S(1)}, f32[8,128]{1,0:T(8,128)S(1)}, u32[]{:S(2)}, u32[]{:S(2)}) collective-permute-start(f32[8,128]{1,0:T(8,128)S(1)} %get-tuple-element.73.refs_0_), channel_id=1, source_target_pairs={{0,1},{1,2},{2,3},{3,0},{4,5},{5,6},{6,7},{7,4},{8,9},{9,10},{10,1... | collective-permute-start | bytes 12296 | tf_op jit(solution)/shard_map/ppermute | solution.py:576
  54.6 3.7 %collective-permute-start.16 = (f32[8,128]{1,0:T(8,128)S(1)}, f32[8,128]{1,0:T(8,128)S(1)}, u32[]{:S(2)}, u32[]{:S(2)}) collective-permute-start(f32[8,128]{1,0:T(8,128)S(1)} %get-tuple-element.73.refs_0_), channel_id=1, source_target_pairs={{0,2},{1,3},{2,0},{3,1},{4,6},{5,7},{6,4},{7,5},{8,10},{9,11},{10,... | collective-permute-start | bytes 12296 | tf_op jit(solution)/shard_map/ppermute | solution.py:576
  55.6 2.7 %collective-permute-start.17 = (f32[8,128]{1,0:T(8,128)S(1)}, f32[8,128]{1,0:T(8,128)S(1)}, u32[]{:S(2)}, u32[]{:S(2)}) collective-permute-start(f32[8,128]{1,0:T(8,128)S(1)} %get-tuple-element.73.refs_0_), channel_id=1, source_target_pairs={{0,3},{1,0},{2,1},{3,2},{4,7},{5,4},{6,5},{7,6},{8,11},{9,8},{10,9... | collective-permute-start | bytes 12296 | tf_op jit(solution)/shard_map/ppermute | solution.py:576

commit v5 on v4

--- a/solution.py
+++ b/solution.py
@@ -140,42 +140,49 @@
     ]
     for copy in copies:
         copy.start()
-    for copy in copies:
-        copy.wait()
     columns = [head_columns(head) for head in range(base + keys_moved)]
     moving = [(ref, part) for ref in (k_ref, v_ref) for part in columns[base:]]
-    start = 0
     up = place_ref[4] == 1
-
-    def fill(out, parts):
+    last_group = place_ref[0] > 0
+    bounds = [sum(counts[:i]) for i in range(len(counts) + 1)]
+
+    def fill(out, parts, source):
         for index, (ref, part) in enumerate(parts):
-            out[:, head_columns(index)] = ref[:, part]
-
-    for i, count in enumerate(counts):
-        cross_out, forward_out, backward_out = outs[3 * i : 3 * i + 3]
-        own = columns[start : start + count]
-        queries = [(q_ref, part) for part in own]
-        keys = moving[start : start + count]
-        crossing = [(ref, part) for ref in (k_ref, v_ref) for part in own]
+            if ref is source:
+                out[:, head_columns(index)] = ref[:, part]
+
+    for copy, source in zip(copies, (q_ref, k_ref, v_ref)):
+        copy.wait()
+        jobs = []
+        for i, (start, stop) in enumerate(zip(bounds, bounds[1:])):
+            own = columns[start:stop]
+            jobs.append(
+                (
+                    *outs[3 * i : 3 * i + 3],
+                    [(ref, part) for ref in (k_ref, v_ref) for part in own],
+                    [(q_ref, part) for part in own],
+                    moving[start:stop],
+                )
+            )
 
         @pl.when(up)
         def _():
-            fill(forward_out, keys)
-            fill(backward_out, queries)
+            for _, forward_out, backward_out, _, queries, keys in jobs:
+                fill(forward_out, keys, source)
+                fill(backward_out, queries, source)
 
         @pl.when(jnp.logical_not(up))
         def _():
-            fill(forward_out, queries)
-            fill(backward_out, keys)
-
-        fill(cross_out, crossing)
-        if i == 0:
-
-            @pl.when(place_ref[0] > 0)
-            def _():
-                fill(cross_out, [(q_ref, part) for part in columns[base:]])
-
-        start += count
+            for _, forward_out, backward_out, _, queries, keys in jobs:
+                fill(forward_out, queries, source)
+                fill(backward_out, keys, source)
+
+        for cross_out, _, _, crossing, _, _ in jobs:
+            fill(cross_out, crossing, source)
+
+    @pl.when(last_group)
+    def _():
+        fill(outs[0], [(q_ref, part) for part in columns[base:]], q_ref)
 
 
 def crossing_keys(own_k, own_v, prior_kv, base, head, head_count):
@@ -570,9 +577,10 @@
             turn,
         )
     device_count = lax.axis_size("tp")
+    assert device_count & (device_count - 1) == 0
     shares = [squares]
     for distance in range(1, device_count):
-        route = [(i, (i + distance) % device_count) for i in range(device_count)]
+        route = [(i, i ^ distance) for i in range(device_count)]
         shares.append(lax.ppermute(squares, "tp", route))
     out = pl.pallas_call(
         functools.partial(scale_kernel, head_counts, float(HEADS * HEAD_DIM), device_count),

time: 60.4 us -> 59.9 us (level); the launches traced: 59.5 us -> 59.7 us
  waiting for transfers between devices: 19.2 us -> 20.1 us
    ppermute x3, waiting for transfers between devices: 1.33 us -> 2.2 us  [on_device(): shares.append(lax.ppermute(squares, 'tp', route))]
  transfers between devices with their start and end apart: 18 -> 18, of which waited for: 11 -> 10; matrix products, arithmetic and copies ran while one was open for 0% -> 0% of each run, Pallas kernels for 28% -> 28%
where the time goes in v5:
time: 59.9 us; the launch traced here: 59.7 us
  Pallas kernels  20.7 us (35%)
  waiting for transfers between devices  20.1 us (34%)
  starting transfers between devices  18.7 us (31%)
    pallas_call x10, Pallas kernels, run(): pl.pallas_call(functools.partial(kernel, head_counts[chunk]), out_shape=o...  15.6 us
    ppermute x8, waiting for transfers between devices, round_trip(): return lax.ppermute(block, ('cp', 'tp'), route)  10.8 us
    ppermute x8, starting transfers between devices, round_trip(): return lax.ppermute(block, ('cp', 'tp'), route)  8.1 us
    ppermute x4, waiting for transfers between devices, passed_up(): return lax.ppermute(block, 'cp', route)  7.02 us
    ppermute x4, starting transfers between devices, passed_up(): return lax.ppermute(block, 'cp', route)  5.03 us
    ppermute x3, starting transfers between devices, exchanged(): return lax.ppermute(block, 'stretch', [(0, 1), (1, 0)])  3.63 us
    pallas_call x1, Pallas kernels, on_device(): pl.pallas_call(functools.partial(pack_kernel, CHUNKS, KEYS_MOVED), out_sh...  2.25 us
    ppermute x3, waiting for transfers between devices, on_device(): shares.append(lax.ppermute(squares, 'tp', route))  2.2 us
  transfers between devices with their start and end apart: 18, of which 10 were waited for; matrix products, arithmetic and copies ran while one was open for 0% of the time, Pallas kernels for 28%

profile of v5, /device:TPU:0, one launch (start us, length us, event | category | flops | bytes accessed | tf_op | source)
XLA Modules:
  0.0 59.7 jit_solution(5400776540472147131)
XLA Ops:
  0.0 0.1 pad_add_fusion.place_ref
  0.1 0.0 copy-start
  0.1 0.0 copy-start.1
  0.1 2.3 %pack.1 = (bf16[256,1536]{1,0:T(8,128)(2,1)S(1)}, bf16[256,1536]{1,0:T(8,128)(2,1)S(1)}, bf16[256,1536]{1,0:T(8,128)(2,1)S(1)}, bf16[256,1280]{1,0:T(8,128)(2,1)...) custom-call(s32[5]{0:T(128)S(1)} %pad_add_fusion.place_ref, ...), custom_call_target="tpu_custom_call" | custom-call | flops 1000000000 | bytes 1000000 | tf_op jit(solution)/shard_map/pack/pallas_call | solution.py:478
  2.3 3.0 %collective-permute-start.7 = (bf16[256,1280]{1,0:T(8,128)(2,1)S(1)}, bf16[256,1280]{1,0:T(8,128)(2,1)S(1)}, u32[]{:S(2)}, u32[]{:S(2)}) collective-permute-start(bf16[256,1280]{1,0:T(8,128)(2,1)S(1)} %get-tuple-element.50), channel_id=1, source_target_pairs={{0,16},{16,0},{1,17},{17,1},{2,18},{18,2},{3,19},{19,3},{4,20},{20... | collective-permute-start | bytes 1966088 | tf_op jit(solution)/shard_map/ppermute | solution.py:30
  5.4 1.6 %collective-permute-start.3 = (bf16[256,640]{1,0:T(8,128)(2,1)S(1)}, bf16[256,640]{1,0:T(8,128)(2,1)S(1)}, u32[]{:S(2)}, u32[]{:S(2)}) collective-permute-start(bf16[256,640]{1,0:T(8,128)(2,1)S(1)} %get-tuple-element.48), channel_id=1, source_target_pairs={{0,4},{4,8},{8,12},{12,14},{14,10},{10,6},{6,2},{2,0},{1,5},{5,9},... | collective-permute-start | bytes 983048 | tf_op jit(solution)/shard_map/ppermute | solution.py:46
  6.9 0.4 collective-permute-start.5
  7.4 0.0 copy-start.2
  7.4 1.6 %collective-permute-start = (bf16[256,384]{1,0:T(8,128)(2,1)S(1)}, bf16[256,384]{1,0:T(8,128)(2,1)S(1)}, u32[]{:S(2)}, u32[]{:S(2)}) collective-permute-start(bf16[256,384]{1,0:T(8,128)(2,1)S(1)} %get-tuple-element.45), channel_id=1, source_target_pairs={{0,4},{4,8},{8,12},{12,14},{14,10},{10,6},{6,2},{2,0},{1,5},{5,9},... | collective-permute-start | bytes 589832 | tf_op jit(solution)/shard_map/ppermute | solution.py:46
  9.0 0.4 collective-permute-start.1
  9.4 6.6 %collective-permute-done.3.forward_q.rest_0_ = bf16[256,640]{1,0:T(8,128)(2,1)S(1)} collective-permute-done((bf16[256,640]{1,0:T(8,128)(2,1)S(1)}, bf16[256,640]{1,0:T(8,128)(2,1)S(1)}, u32[]{:S(2)}, u32[]{:S(2)}) %collective-permute-start.3) | collective-permute-done | bytes 327712 | tf_op jit(solution)/shard_map/ppermute | solution.py:46
  16.0 1.6 %collective-permute-start.4 = (bf16[256,640]{1,0:T(8,128)(2,1)S(1)}, bf16[256,640]{1,0:T(8,128)(2,1)S(1)}, u32[]{:S(2)}, u32[]{:S(2)}) collective-permute-start(bf16[256,640]{1,0:T(8,128)(2,1)S(1)} %collective-permute-done.3.forward_q.rest_0_), channel_id=1, source_target_pairs={{0,4},{4,8},{8,12},{12,14},{14,10},{10,6},{6,2},{2,0},{1,5},{5,9},... | collective-permute-start | bytes 983048 | tf_op jit(solution)/shard_map/ppermute | solution.py:46
  17.6 0.0 collective-permute-done.5.backward_q.rest_1_
  17.6 0.4 collective-permute-start.6
  18.0 0.0 copy-done
  18.0 0.0 copy-done.1
  18.1 0.0 copy-done.2
  18.1 1.7 %plan.1 = (f32[8,1536]{1,0:T(8,128)S(1)}, s32[64]{0:T(128)S(1)}) custom-call(s32[5]{0:T(128)S(1)} %pad_add_fusion.place_ref, s32[2,4,4,4]{3,2,1,0:T(4,128)S(1)} %copy-done.1, s32[4]{0:T(128)S(1)} %copy-done.2, bf16[16,1536]{1,0:T(8,128)(2,1)S(1)} %copy-done), custom_call_target="tpu_custom_call" | custom-call | flops 600000000 | bytes 600000 | tf_op jit(solution)/shard_map/plan/pallas_call | solution.py:500
  19.7 0.5 collective-permute-done.forward_q.rest_2_
  20.2 0.0 collective-permute-start.2
  20.2 1.6 %collective-permute-done.1.backward_q.rest_3_ = bf16[256,384]{1,0:T(8,128)(2,1)S(1)} collective-permute-done((bf16[256,384]{1,0:T(8,128)(2,1)S(1)}, bf16[256,384]{1,0:T(8,128)(2,1)S(1)}, u32[]{:S(2)}, u32[]{:S(2)}) %collective-permute-start.1) | collective-permute-done | bytes 196640 | tf_op jit(solution)/shard_map/ppermute | solution.py:46
  21.8 1.6 %collective-permute-start.8 = (bf16[256,384]{1,0:T(8,128)(2,1)S(1)}, bf16[256,384]{1,0:T(8,128)(2,1)S(1)}, u32[]{:S(2)}, u32[]{:S(2)}) collective-permute-start(bf16[256,384]{1,0:T(8,128)(2,1)S(1)} %collective-permute-done.forward_q.rest_2_), channel_id=1, source_target_pairs={{0,4},{4,8},{8,12},{12,14},{14,10},{10,6},{6,2},{2,0},{1,5},{5,9},... | collective-permute-start | bytes 589832 | tf_op jit(solution)/shard_map/ppermute | solution.py:46
  23.4 0.0 collective-permute-done.7.prior_kv.next_q
  23.4 0.5 collective-permute-start.9
  23.8 2.8 %near.2 = (f32[256,640]{1,0:T(8,128)S(1)}, f32[16,128]{1,0:T(8,128)S(1)}, f32[256,640]{1,0:T(8,128)S(1)}, f32[16,128]{1,0:T(8,128)S(1)}) custom-call(s32[64]{0:T(128)S(1)} %get-tuple-element.41.flags_ref, bf16[256,1536]{1,0:T(8,128)(2,1)S(1)} %get-tuple-element.42.own_q, bf16[256,1536]{1,0:T(8,128)(2,1)S(1)} %get-tuple-element.43.own_k, ...), custom_call_target="tpu_custom_call" | custom-call | flops 3000000000 | bytes 3000000 | tf_op jit(solution)/shard_map/near/pallas_call | solution.py:463
  26.6 0.6 %collective-permute-done.4.forward_q.rest_4_ = bf16[256,640]{1,0:T(8,128)(2,1)S(1)} collective-permute-done((bf16[256,640]{1,0:T(8,128)(2,1)S(1)}, bf16[256,640]{1,0:T(8,128)(2,1)S(1)}, u32[]{:S(2)}, u32[]{:S(2)}) %collective-permute-start.4) | collective-permute-done | bytes 327712 | tf_op jit(solution)/shard_map/ppermute | solution.py:46
  27.2 1.6 %collective-permute-done.6.backward_q.rest_5_ = bf16[256,640]{1,0:T(8,128)(2,1)S(1)} collective-permute-done((bf16[256,640]{1,0:T(8,128)(2,1)S(1)}, bf16[256,640]{1,0:T(8,128)(2,1)S(1)}, u32[]{:S(2)}, u32[]{:S(2)}) %collective-permute-start.6) | collective-permute-done | bytes 327712 | tf_op jit(solution)/shard_map/ppermute | solution.py:46
  28.8 2.0 %far.2 = (bf16[272,640]{1,0:T(8,128)(2,1)S(1)}, f32[16,128]{1,0:T(8,128)S(1)}) custom-call(s32[64]{0:T(128)S(1)} %get-tuple-element.41.flags_ref, bf16[256,1536]{1,0:T(8,128)(2,1)S(1)} %get-tuple-element.43.own_k, bf16[256,1536]{1,0:T(8,128)(2,1)S(1)} %get-tuple-element.44.own_v, bf16[256,640]{1,0:T(8,128)(2,1)S(1)} %collective-permute-done.4.forward_q.rest_4_, ...), custom_call_target="tpu_custom_call" | custom-call | flops 1500000000 | bytes 1500000 | tf_op jit(solution)/shard_map/far/pallas_call | solution.py:463
  30.8 1.6 %collective-permute-start.11 = (bf16[272,640]{1,0:T(8,128)(2,1)S(1)}, bf16[272,640]{1,0:T(8,128)(2,1)S(1)}, u32[]{:S(2)}, u32[]{:S(2)}) collective-permute-start(bf16[272,640]{1,0:T(8,128)(2,1)S(1)} %get-tuple-element.60), channel_id=1, source_target_pairs={{0,4},{4,8},{8,12},{12,0},{1,5},{5,9},{9,13},{13,1},{2,6},{6,10},{... | collective-permute-start | bytes 1044488 | tf_op jit(solution)/shard_map/ppermute | solution.py:52
  32.4 0.0 collective-permute-done.2.prior_kv
  32.4 2.1 %near.3 = (f32[256,384]{1,0:T(8,128)S(1)}, f32[16,128]{1,0:T(8,128)S(1)}, f32[256,384]{1,0:T(8,128)S(1)}, f32[16,128]{1,0:T(8,128)S(1)}) custom-call(s32[64]{0:T(128)S(1)} %get-tuple-element.41.flags_ref, bf16[256,1536]{1,0:T(8,128)(2,1)S(1)} %get-tuple-element.42.own_q, bf16[256,1536]{1,0:T(8,128)(2,1)S(1)} %get-tuple-element.43.own_k, ...), custom_call_target="tpu_custom_call" | custom-call | flops 1800000000 | bytes 1800000 | tf_op jit(solution)/shard_map/near/pallas_call | solution.py:463
  34.5 0.0 collective-permute-done.8.forward_q.rest_6_
  34.5 0.0 collective-permute-done.9.backward_q.rest_7_
  34.6 1.6 %far.3 = (bf16[272,384]{1,0:T(8,128)(2,1)S(1)}, f32[16,128]{1,0:T(8,128)S(1)}) custom-call(s32[64]{0:T(128)S(1)} %get-tuple-element.41.flags_ref, bf16[256,1536]{1,0:T(8,128)(2,1)S(1)} %get-tuple-element.43.own_k, bf16[256,1536]{1,0:T(8,128)(2,1)S(1)} %get-tuple-element.44.own_v, bf16[256,384]{1,0:T(8,128)(2,1)S(1)} %collective-permute-done.8.forward_q.rest_6_, ...), custom_call_target="tpu_custom_call" | custom-call | flops 900000000 | bytes 900000 | tf_op jit(solution)/shard_map/far/pallas_call | solution.py:463
  36.2 1.6 %collective-permute-start.10 = (bf16[272,384]{1,0:T(8,128)(2,1)S(1)}, bf16[272,384]{1,0:T(8,128)(2,1)S(1)}, u32[]{:S(2)}, u32[]{:S(2)}) collective-permute-start(bf16[272,384]{1,0:T(8,128)(2,1)S(1)} %get-tuple-element.57), channel_id=1, source_target_pairs={{0,4},{4,8},{8,12},{12,0},{1,5},{5,9},{9,13},{13,1},{2,6},{6,10},{... | collective-permute-start | bytes 626696 | tf_op jit(solution)/shard_map/ppermute | solution.py:52
  37.8 3.5 %keys_moved.1 = (f32[256,512]{1,0:T(8,128)S(1)}, f32[16,128]{1,0:T(8,128)S(1)}, bf16[272,512]{1,0:T(8,128)(2,1)S(1)}) custom-call(s32[64]{0:T(128)S(1)} %get-tuple-element.41.flags_ref, bf16[256,1536]{1,0:T(8,128)(2,1)S(1)} %get-tuple-element.42.own_q, bf16[256,1536]{1,0:T(8,128)(2,1)S(1)} %get-tuple-element.43.own_k, ...), custom_call_target="tpu_custom_call" | custom-call | flops 2000000000 | bytes 2000000 | tf_op jit(solution)/shard_map/keys_moved/pallas_call | solution.py:463
  41.3 0.6 collective-permute-start.14
  41.9 1.1 %collective-permute-done.11.payload_in = bf16[272,640]{1,0:T(8,128)(2,1)S(1)} collective-permute-done((bf16[272,640]{1,0:T(8,128)(2,1)S(1)}, bf16[272,640]{1,0:T(8,128)(2,1)S(1)}, u32[]{:S(2)}, u32[]{:S(2)}) %collective-permute-start.11) | collective-permute-done | bytes 348192 | tf_op jit(solution)/shard_map/ppermute | solution.py:52
  43.0 0.7 %relay.2 = (bf16[272,640]{1,0:T(8,128)(2,1)S(1)}, f32[16,128]{1,0:T(8,128)S(1)}) custom-call(s32[5]{0:T(128)S(1)} %pad_add_fusion.place_ref, f32[256,640]{1,0:T(8,128)S(1)} %get-tuple-element.58.local_out, f32[16,128]{1,0:T(8,128)S(1)} %get-tuple-element.59.local_stats, bf16[272,640]{1,0:T(8,128)(2,1)S(1)} %collective-permute-done.11.payload_in, ...), custom_call_target="tpu_custom_call" | custom-call | flops 700000000 | bytes 700000 | tf_op jit(solution)/shard_map/relay/pallas_call | solution.py:463
  43.7 0.5 collective-permute-start.13
  44.2 3.2 %collective-permute-done.10.payload_in = bf16[272,384]{1,0:T(8,128)(2,1)S(1)} collective-permute-done((bf16[272,384]{1,0:T(8,128)(2,1)S(1)}, bf16[272,384]{1,0:T(8,128)(2,1)S(1)}, u32[]{:S(2)}, u32[]{:S(2)}) %collective-permute-start.10) | collective-permute-done | bytes 208928 | tf_op jit(solution)/shard_map/ppermute | solution.py:52
  47.4 0.6 %relay.3 = (bf16[272,384]{1,0:T(8,128)(2,1)S(1)}, f32[16,128]{1,0:T(8,128)S(1)}) custom-call(s32[5]{0:T(128)S(1)} %pad_add_fusion.place_ref, f32[256,384]{1,0:T(8,128)S(1)} %get-tuple-element.55.local_out, f32[16,128]{1,0:T(8,128)S(1)} %get-tuple-element.56.local_stats, bf16[272,384]{1,0:T(8,128)(2,1)S(1)} %collective-permute-done.10.payload_in, ...), custom_call_target="tpu_custom_call" | custom-call | flops 700000000 | bytes 700000 | tf_op jit(solution)/shard_map/relay/pallas_call | solution.py:463
  48.0 1.3 %collective-permute-start.12 = (bf16[272,384]{1,0:T(8,128)(2,1)S(1)}, bf16[272,384]{1,0:T(8,128)(2,1)S(1)}, u32[]{:S(2)}, u32[]{:S(2)}) collective-permute-start(bf16[272,384]{1,0:T(8,128)(2,1)S(1)} %get-tuple-element.64), channel_id=1, source_target_pairs={{0,4},{4,8},{8,12},{1,5},{5,9},{9,13},{2,6},{6,10},{10,14},{3,7},{... | collective-permute-start | bytes 626696 | tf_op jit(solution)/shard_map/ppermute | solution.py:52
  49.3 0.0 collective-permute-done.14.payload_in
  49.3 0.8 %finish.3 = (f32[256,512]{1,0:T(8,128)S(1)}, f32[8,128]{1,0:T(8,128)S(1)}) custom-call(s32[5]{0:T(128)S(1)} %pad_add_fusion.place_ref, f32[256,512]{1,0:T(8,128)S(1)} %get-tuple-element.68.local_out, f32[16,128]{1,0:T(8,128)S(1)} %get-tuple-element.62.rest_0_.local_stats, bf16[272,512]{1,0:T(8,128)(2,1)S(1)} %collective-permute-done.14.payload_in, ...), custom_call_target="tpu_custom_call" | custom-call | flops 800000000 | bytes 800000 | tf_op jit(solution)/shard_map/finish/pallas_call | solution.py:463
  50.1 2.7 %collective-permute-done.13.payload_in = bf16[272,640]{1,0:T(8,128)(2,1)S(1)} collective-permute-done((bf16[272,640]{1,0:T(8,128)(2,1)S(1)}, bf16[272,640]{1,0:T(8,128)(2,1)S(1)}, u32[]{:S(2)}, u32[]{:S(2)}) %collective-permute-start.13) | collective-permute-done | bytes 348192 | tf_op jit(solution)/shard_map/ppermute | solution.py:52
  52.8 0.8 %finish.4 = (f32[256,640]{1,0:T(8,128)S(1)}, f32[8,128]{1,0:T(8,128)S(1)}) custom-call(s32[5]{0:T(128)S(1)} %pad_add_fusion.place_ref, f32[256,640]{1,0:T(8,128)S(1)} %get-tuple-element.66.local_out, f32[16,128]{1,0:T(8,128)S(1)} %get-tuple-element.51.rest_0_.local_stats, bf16[272,640]{1,0:T(8,128)(2,1)S(1)} %collective-permute-done.13.payload_in, ...), custom_call_target="tpu_custom_call" | custom-call | flops 800000000 | bytes 800000 | tf_op jit(solution)/shard_map/finish/pallas_call | solution.py:463
  53.7 0.0 collective-permute-done.12.payload_in
  53.7 0.7 %finish.5 = (f32[256,384]{1,0:T(8,128)S(1)}, f32[8,128]{1,0:T(8,128)S(1)}) custom-call(s32[5]{0:T(128)S(1)} %pad_add_fusion.place_ref, f32[256,384]{1,0:T(8,128)S(1)} %get-tuple-element.53.local_out, f32[16,128]{1,0:T(8,128)S(1)} %get-tuple-element.54.rest_0_.local_stats, bf16[272,384]{1,0:T(8,128)(2,1)S(1)} %collective-permute-done.12.payload_in, ...), custom_call_target="tpu_custom_call" | custom-call | flops 800000000 | bytes 800000 | tf_op jit(solution)/shard_map/finish/pallas_call | solution.py:463
  54.4 0.1 collective-permute-start.15
  54.5 1.0 %collective-permute-start.16 = (f32[8,128]{1,0:T(8,128)S(1)}, f32[8,128]{1,0:T(8,128)S(1)}, u32[]{:S(2)}, u32[]{:S(2)}) collective-permute-start(f32[8,128]{1,0:T(8,128)S(1)} %get-tuple-element.73.refs_0_), channel_id=1, source_target_pairs={{0,2},{1,3},{2,0},{3,1},{4,6},{5,7},{6,4},{7,5},{8,10},{9,11},{10,... | collective-permute-start | bytes 12296 | tf_op jit(solution)/shard_map/ppermute | solution.py:584
  55.5 0.8 %collective-permute-start.17 = (f32[8,128]{1,0:T(8,128)S(1)}, f32[8,128]{1,0:T(8,128)S(1)}, u32[]{:S(2)}, u32[]{:S(2)}) collective-permute-start(f32[8,128]{1,0:T(8,128)S(1)} %get-tuple-element.73.refs_0_), channel_id=1, source_target_pairs={{0,3},{1,2},{2,1},{3,0},{4,7},{5,6},{6,5},{7,4},{8,11},{9,10},{10,... | collective-permute-start | bytes 12296 | tf_op jit(solution)/shard_map/ppermute | solution.py:584
  56.4 0.0 collective-permute-done.15.refs_1_
  56.4 1.8 %collective-permute-done.16.refs_2_ = f32[8,128]{1,0:T(8,128)S(1)} collective-permute-done((f32[8,128]{1,0:T(8,128)S(1)}, f32[8,128]{1,0:T(8,128)S(1)}, u32[]{:S(2)}, u32[]{:S(2)}) %collective-permute-start.16) | collective-permute-done | bytes 4128 | tf_op jit(solution)/shard_map/ppermute | solution.py:584
  58.2 0.4 collective-permute-done.17.refs_3_
  58.6 1.2 %scale.1 = bf16[256,1536]{1,0:T(8,128)(2,1)} custom-call(f32[8,128]{1,0:T(8,128)S(1)} %get-tuple-element.73.refs_0_, f32[8,128]{1,0:T(8,128)S(1)} %collective-permute-done.15.refs_1_, f32[8,128]{1,0:T(8,128)S(1)} %collective-permute-done.16.refs_2_, f32[8,128]{1,0:T(8,128)S(1)} %collective-permute-done.17.refs_3_, f32[256,640]{1,0:T(8,128)S(1)} %get-tuple-element.74.refs_4_, ...), custom_call_target="tpu_custom_call" | custom-call | tf_op jit(solution)/shard_map/scale/pallas_call | solution.py:585
  (2 shorter events, 0.0 us)
Async XLA Ops:
  0.1 18.0 %copy-start = (bf16[16,1536]{1,0:T(8,128)(2,1)S(1)}, bf16[16,1536]{1,0:T(8,128)(2,1)}, u32[]{:S(2)}) copy-start(bf16[16,1536]{1,0:T(8,128)(2,1)} %gate_table.1) | copy-start | bytes 147460
  0.1 18.0 %copy-start.1 = (s32[2,4,4,4]{3,2,1,0:T(4,128)S(1)}, s32[2,4,4,4]{3,2,1,0:T(4,128)}, u32[]{:S(2)}) copy-start(s32[2,4,4,4]{3,2,1,0:T(4,128)} %ranges_ref.1) | copy-start | bytes 1540
  2.3 21.0 %collective-permute-start.7 = (bf16[256,1280]{1,0:T(8,128)(2,1)S(1)}, bf16[256,1280]{1,0:T(8,128)(2,1)S(1)}, u32[]{:S(2)}, u32[]{:S(2)}) collective-permute-start(bf16[256,1280]{1,0:T(8,128)(2,1)S(1)} %get-tuple-element.50), channel_id=1, source_target_pairs={{0,16},{16,0},{1,17},{17,1},{2,18},{18,2},{3,19},{19,3},{4,20},{20... | collective-permute-start | bytes 1966088 | tf_op jit(solution)/shard_map/ppermute | solution.py:30
  5.4 10.6 %collective-permute-start.3 = (bf16[256,640]{1,0:T(8,128)(2,1)S(1)}, bf16[256,640]{1,0:T(8,128)(2,1)S(1)}, u32[]{:S(2)}, u32[]{:S(2)}) collective-permute-start(bf16[256,640]{1,0:T(8,128)(2,1)S(1)} %get-tuple-element.48), channel_id=1, source_target_pairs={{0,4},{4,8},{8,12},{12,14},{14,10},{10,6},{6,2},{2,0},{1,5},{5,9},... | collective-permute-start | bytes 983048 | tf_op jit(solution)/shard_map/ppermute | solution.py:46
  6.9 10.7 %collective-permute-start.5 = (bf16[256,640]{1,0:T(8,128)(2,1)S(1)}, bf16[256,640]{1,0:T(8,128)(2,1)S(1)}, u32[]{:S(2)}, u32[]{:S(2)}) collective-permute-start(bf16[256,640]{1,0:T(8,128)(2,1)S(1)} %get-tuple-element.49), channel_id=1, source_target_pairs={{4,0},{8,4},{12,8},{14,12},{10,14},{6,10},{2,6},{0,2},{5,1},{9,5},... | collective-permute-start | bytes 983048 | tf_op jit(solution)/shard_map/ppermute | solution.py:46
  7.4 10.7 %copy-start.2 = (s32[4]{0:T(128)S(1)}, s32[4]{0:T(128)}, u32[]{:S(2)}) copy-start(s32[4]{0:T(128)} %levels_ref.1) | copy-start | bytes 52
  7.4 12.8 %collective-permute-start = (bf16[256,384]{1,0:T(8,128)(2,1)S(1)}, bf16[256,384]{1,0:T(8,128)(2,1)S(1)}, u32[]{:S(2)}, u32[]{:S(2)}) collective-permute-start(bf16[256,384]{1,0:T(8,128)(2,1)S(1)} %get-tuple-element.45), channel_id=1, source_target_pairs={{0,4},{4,8},{8,12},{12,14},{14,10},{10,6},{6,2},{2,0},{1,5},{5,9},... | collective-permute-start | bytes 589832 | tf_op jit(solution)/shard_map/ppermute | solution.py:46
  9.0 12.8 %collective-permute-start.1 = (bf16[256,384]{1,0:T(8,128)(2,1)S(1)}, bf16[256,384]{1,0:T(8,128)(2,1)S(1)}, u32[]{:S(2)}, u32[]{:S(2)}) collective-permute-start(bf16[256,384]{1,0:T(8,128)(2,1)S(1)} %get-tuple-element.46), channel_id=1, source_target_pairs={{4,0},{8,4},{12,8},{14,12},{10,14},{6,10},{2,6},{0,2},{5,1},{9,5},... | collective-permute-start | bytes 589832 | tf_op jit(solution)/shard_map/ppermute | solution.py:46
  16.0 11.2 %collective-permute-start.4 = (bf16[256,640]{1,0:T(8,128)(2,1)S(1)}, bf16[256,640]{1,0:T(8,128)(2,1)S(1)}, u32[]{:S(2)}, u32[]{:S(2)}) collective-permute-start(bf16[256,640]{1,0:T(8,128)(2,1)S(1)} %collective-permute-done.3.forward_q.rest_0_), channel_id=1, source_target_pairs={{0,4},{4,8},{8,12},{12,14},{14,10},{10,6},{6,2},{2,0},{1,5},{5,9},... | collective-permute-start | bytes 983048 | tf_op jit(solution)/shard_map/ppermute | solution.py:46
  17.6 11.2 %collective-permute-start.6 = (bf16[256,640]{1,0:T(8,128)(2,1)S(1)}, bf16[256,640]{1,0:T(8,128)(2,1)S(1)}, u32[]{:S(2)}, u32[]{:S(2)}) collective-permute-start(bf16[256,640]{1,0:T(8,128)(2,1)S(1)} %collective-permute-done.5.backward_q.rest_1_), channel_id=1, source_target_pairs={{4,0},{8,4},{12,8},{14,12},{10,14},{6,10},{2,6},{0,2},{5,1},{9,5},... | collective-permute-start | bytes 983048 | tf_op jit(solution)/shard_map/ppermute | solution.py:46
  20.2 12.2 %collective-permute-start.2 = (bf16[256,768]{1,0:T(8,128)(2,1)S(1)}, bf16[256,768]{1,0:T(8,128)(2,1)S(1)}, u32[]{:S(2)}, u32[]{:S(2)}) collective-permute-start(bf16[256,768]{1,0:T(8,128)(2,1)S(1)} %get-tuple-element.47), channel_id=1, source_target_pairs={{0,16},{16,0},{1,17},{17,1},{2,18},{18,2},{3,19},{19,3},{4,20},{20... | collective-permute-start | bytes 1179656 | tf_op jit(solution)/shard_map/ppermute | solution.py:30
  21.8 12.7 %collective-permute-start.8 = (bf16[256,384]{1,0:T(8,128)(2,1)S(1)}, bf16[256,384]{1,0:T(8,128)(2,1)S(1)}, u32[]{:S(2)}, u32[]{:S(2)}) collective-permute-start(bf16[256,384]{1,0:T(8,128)(2,1)S(1)} %collective-permute-done.forward_q.rest_2_), channel_id=1, source_target_pairs={{0,4},{4,8},{8,12},{12,14},{14,10},{10,6},{6,2},{2,0},{1,5},{5,9},... | collective-permute-start | bytes 589832 | tf_op jit(solution)/shard_map/ppermute | solution.py:46
  23.4 11.2 %collective-permute-start.9 = (bf16[256,384]{1,0:T(8,128)(2,1)S(1)}, bf16[256,384]{1,0:T(8,128)(2,1)S(1)}, u32[]{:S(2)}, u32[]{:S(2)}) collective-permute-start(bf16[256,384]{1,0:T(8,128)(2,1)S(1)} %collective-permute-done.1.backward_q.rest_3_), channel_id=1, source_target_pairs={{4,0},{8,4},{12,8},{14,12},{10,14},{6,10},{2,6},{0,2},{5,1},{9,5},... | collective-permute-start | bytes 589832 | tf_op jit(solution)/shard_map/ppermute | solution.py:46
  30.8 12.2 %collective-permute-start.11 = (bf16[272,640]{1,0:T(8,128)(2,1)S(1)}, bf16[272,640]{1,0:T(8,128)(2,1)S(1)}, u32[]{:S(2)}, u32[]{:S(2)}) collective-permute-start(bf16[272,640]{1,0:T(8,128)(2,1)S(1)} %get-tuple-element.60), channel_id=1, source_target_pairs={{0,4},{4,8},{8,12},{12,0},{1,5},{5,9},{9,13},{13,1},{2,6},{6,10},{... | collective-permute-start | bytes 1044488 | tf_op jit(solution)/shard_map/ppermute | solution.py:52
  36.2 11.2 %collective-permute-start.10 = (bf16[272,384]{1,0:T(8,128)(2,1)S(1)}, bf16[272,384]{1,0:T(8,128)(2,1)S(1)}, u32[]{:S(2)}, u32[]{:S(2)}) collective-permute-start(bf16[272,384]{1,0:T(8,128)(2,1)S(1)} %get-tuple-element.57), channel_id=1, source_target_pairs={{0,4},{4,8},{8,12},{12,0},{1,5},{5,9},{9,13},{13,1},{2,6},{6,10},{... | collective-permute-start | bytes 626696 | tf_op jit(solution)/shard_map/ppermute | solution.py:52
  41.3 8.0 %collective-permute-start.14 = (bf16[272,512]{1,0:T(8,128)(2,1)S(1)}, bf16[272,512]{1,0:T(8,128)(2,1)S(1)}, u32[]{:S(2)}, u32[]{:S(2)}) collective-permute-start(bf16[272,512]{1,0:T(8,128)(2,1)S(1)} %get-tuple-element.69), channel_id=1, source_target_pairs={{0,16},{16,0},{1,17},{17,1},{2,18},{18,2},{3,19},{19,3},{4,20},{20... | collective-permute-start | bytes 835592 | tf_op jit(solution)/shard_map/ppermute | solution.py:30
  43.7 9.1 %collective-permute-start.13 = (bf16[272,640]{1,0:T(8,128)(2,1)S(1)}, bf16[272,640]{1,0:T(8,128)(2,1)S(1)}, u32[]{:S(2)}, u32[]{:S(2)}) collective-permute-start(bf16[272,640]{1,0:T(8,128)(2,1)S(1)} %get-tuple-element.67), channel_id=1, source_target_pairs={{0,4},{4,8},{8,12},{12,0},{1,5},{5,9},{9,13},{13,1},{2,6},{6,10},{... | collective-permute-start | bytes 1044488 | tf_op jit(solution)/shard_map/ppermute | solution.py:52
  48.0 5.7 %collective-permute-start.12 = (bf16[272,384]{1,0:T(8,128)(2,1)S(1)}, bf16[272,384]{1,0:T(8,128)(2,1)S(1)}, u32[]{:S(2)}, u32[]{:S(2)}) collective-permute-start(bf16[272,384]{1,0:T(8,128)(2,1)S(1)} %get-tuple-element.64), channel_id=1, source_target_pairs={{0,4},{4,8},{8,12},{1,5},{5,9},{9,13},{2,6},{6,10},{10,14},{3,7},{... | collective-permute-start | bytes 626696 | tf_op jit(solution)/shard_map/ppermute | solution.py:52
  54.4 1.9 %collective-permute-start.15 = (f32[8,128]{1,0:T(8,128)S(1)}, f32[8,128]{1,0:T(8,128)S(1)}, u32[]{:S(2)}, u32[]{:S(2)}) collective-permute-start(f32[8,128]{1,0:T(8,128)S(1)} %get-tuple-element.73.refs_0_), channel_id=1, source_target_pairs={{0,1},{1,0},{2,3},{3,2},{4,5},{5,4},{6,7},{7,6},{8,9},{9,8},{10,11... | collective-permute-start | bytes 12296 | tf_op jit(solution)/shard_map/ppermute | solution.py:584
  54.5 3.7 %collective-permute-start.16 = (f32[8,128]{1,0:T(8,128)S(1)}, f32[8,128]{1,0:T(8,128)S(1)}, u32[]{:S(2)}, u32[]{:S(2)}) collective-permute-start(f32[8,128]{1,0:T(8,128)S(1)} %get-tuple-element.73.refs_0_), channel_id=1, source_target_pairs={{0,2},{1,3},{2,0},{3,1},{4,6},{5,7},{6,4},{7,5},{8,10},{9,11},{10,... | collective-permute-start | bytes 12296 | tf_op jit(solution)/shard_map/ppermute | solution.py:584
  55.5 3.0 %collective-permute-start.17 = (f32[8,128]{1,0:T(8,128)S(1)}, f32[8,128]{1,0:T(8,128)S(1)}, u32[]{:S(2)}, u32[]{:S(2)}) collective-permute-start(f32[8,128]{1,0:T(8,128)S(1)} %get-tuple-element.73.refs_0_), channel_id=1, source_target_pairs={{0,3},{1,2},{2,1},{3,0},{4,7},{5,6},{6,5},{7,4},{8,11},{9,10},{10,... | collective-permute-start | bytes 12296 | tf_op jit(solution)/shard_map/ppermute | solution.py:584

commit v6 on v5

--- a/solution.py
+++ b/solution.py
@@ -579,7 +579,7 @@
     device_count = lax.axis_size("tp")
     assert device_count & (device_count - 1) == 0
     shares = [squares]
-    for distance in range(1, device_count):
+    for distance in reversed(range(1, device_count)):
         route = [(i, i ^ distance) for i in range(device_count)]
         shares.append(lax.ppermute(squares, "tp", route))
     out = pl.pallas_call(

time: 59.9 us -> 59.5 us (level)
  no operation moved by 1% of the time
where the time goes in v6:
time: 59.5 us; the launch traced here: 59.3 us
  Pallas kernels  20.7 us (35%)
  waiting for transfers between devices  19.7 us (33%)
  starting transfers between devices  18.7 us (31%)
    pallas_call x10, Pallas kernels, run(): pl.pallas_call(functools.partial(kernel, head_counts[chunk]), out_shape=o...  15.6 us
    ppermute x8, waiting for transfers between devices, round_trip(): return lax.ppermute(block, ('cp', 'tp'), route)  10.8 us
    ppermute x8, starting transfers between devices, round_trip(): return lax.ppermute(block, ('cp', 'tp'), route)  8.1 us
    ppermute x4, waiting for transfers between devices, passed_up(): return lax.ppermute(block, 'cp', route)  7.02 us
    ppermute x4, starting transfers between devices, passed_up(): return lax.ppermute(block, 'cp', route)  5.03 us
    ppermute x3, starting transfers between devices, exchanged(): return lax.ppermute(block, 'stretch', [(0, 1), (1, 0)])  3.63 us
    pallas_call x1, Pallas kernels, on_device(): pl.pallas_call(functools.partial(pack_kernel, CHUNKS, KEYS_MOVED), out_sh...  2.25 us
    ppermute x3, starting transfers between devices, on_device(): shares.append(lax.ppermute(squares, 'tp', route))  1.92 us
  transfers between devices with their start and end apart: 18, of which 10 were waited for; matrix products, arithmetic and copies ran while one was open for 0% of the time, Pallas kernels for 28%

profile of v6, /device:TPU:0, one launch (start us, length us, event | category | flops | bytes accessed | tf_op | source)
XLA Modules:
  0.0 59.3 jit_solution(11373239100471328778)
XLA Ops:
  0.0 0.1 pad_add_fusion.place_ref
  0.1 0.0 copy-start
  0.1 0.0 copy-start.1
  0.1 2.3 %pack.1 = (bf16[256,1536]{1,0:T(8,128)(2,1)S(1)}, bf16[256,1536]{1,0:T(8,128)(2,1)S(1)}, bf16[256,1536]{1,0:T(8,128)(2,1)S(1)}, bf16[256,1280]{1,0:T(8,128)(2,1)...) custom-call(s32[5]{0:T(128)S(1)} %pad_add_fusion.place_ref, ...), custom_call_target="tpu_custom_call" | custom-call | flops 1000000000 | bytes 1000000 | tf_op jit(solution)/shard_map/pack/pallas_call | solution.py:478
  2.3 3.0 %collective-permute-start.7 = (bf16[256,1280]{1,0:T(8,128)(2,1)S(1)}, bf16[256,1280]{1,0:T(8,128)(2,1)S(1)}, u32[]{:S(2)}, u32[]{:S(2)}) collective-permute-start(bf16[256,1280]{1,0:T(8,128)(2,1)S(1)} %get-tuple-element.50), channel_id=1, source_target_pairs={{0,16},{16,0},{1,17},{17,1},{2,18},{18,2},{3,19},{19,3},{4,20},{20... | collective-permute-start | bytes 1966088 | tf_op jit(solution)/shard_map/ppermute | solution.py:30
  5.4 1.6 %collective-permute-start.3 = (bf16[256,640]{1,0:T(8,128)(2,1)S(1)}, bf16[256,640]{1,0:T(8,128)(2,1)S(1)}, u32[]{:S(2)}, u32[]{:S(2)}) collective-permute-start(bf16[256,640]{1,0:T(8,128)(2,1)S(1)} %get-tuple-element.48), channel_id=1, source_target_pairs={{0,4},{4,8},{8,12},{12,14},{14,10},{10,6},{6,2},{2,0},{1,5},{5,9},... | collective-permute-start | bytes 983048 | tf_op jit(solution)/shard_map/ppermute | solution.py:46
  6.9 0.4 collective-permute-start.5
  7.4 0.0 copy-start.2
  7.4 1.6 %collective-permute-start = (bf16[256,384]{1,0:T(8,128)(2,1)S(1)}, bf16[256,384]{1,0:T(8,128)(2,1)S(1)}, u32[]{:S(2)}, u32[]{:S(2)}) collective-permute-start(bf16[256,384]{1,0:T(8,128)(2,1)S(1)} %get-tuple-element.45), channel_id=1, source_target_pairs={{0,4},{4,8},{8,12},{12,14},{14,10},{10,6},{6,2},{2,0},{1,5},{5,9},... | collective-permute-start | bytes 589832 | tf_op jit(solution)/shard_map/ppermute | solution.py:46
  9.0 0.4 collective-permute-start.1
  9.4 6.6 %collective-permute-done.3.forward_q.rest_0_ = bf16[256,640]{1,0:T(8,128)(2,1)S(1)} collective-permute-done((bf16[256,640]{1,0:T(8,128)(2,1)S(1)}, bf16[256,640]{1,0:T(8,128)(2,1)S(1)}, u32[]{:S(2)}, u32[]{:S(2)}) %collective-permute-start.3) | collective-permute-done | bytes 327712 | tf_op jit(solution)/shard_map/ppermute | solution.py:46
  16.0 1.6 %collective-permute-start.4 = (bf16[256,640]{1,0:T(8,128)(2,1)S(1)}, bf16[256,640]{1,0:T(8,128)(2,1)S(1)}, u32[]{:S(2)}, u32[]{:S(2)}) collective-permute-start(bf16[256,640]{1,0:T(8,128)(2,1)S(1)} %collective-permute-done.3.forward_q.rest_0_), channel_id=1, source_target_pairs={{0,4},{4,8},{8,12},{12,14},{14,10},{10,6},{6,2},{2,0},{1,5},{5,9},... | collective-permute-start | bytes 983048 | tf_op jit(solution)/shard_map/ppermute | solution.py:46
  17.6 0.0 collective-permute-done.5.backward_q.rest_1_
  17.6 0.4 collective-permute-start.6
  18.0 0.0 copy-done
  18.0 0.0 copy-done.1
  18.1 0.0 copy-done.2
  18.1 1.7 %plan.1 = (f32[8,1536]{1,0:T(8,128)S(1)}, s32[64]{0:T(128)S(1)}) custom-call(s32[5]{0:T(128)S(1)} %pad_add_fusion.place_ref, s32[2,4,4,4]{3,2,1,0:T(4,128)S(1)} %copy-done.1, s32[4]{0:T(128)S(1)} %copy-done.2, bf16[16,1536]{1,0:T(8,128)(2,1)S(1)} %copy-done), custom_call_target="tpu_custom_call" | custom-call | flops 600000000 | bytes 600000 | tf_op jit(solution)/shard_map/plan/pallas_call | solution.py:500
  19.7 0.5 collective-permute-done.forward_q.rest_2_
  20.2 0.0 collective-permute-start.2
  20.2 1.6 %collective-permute-done.1.backward_q.rest_3_ = bf16[256,384]{1,0:T(8,128)(2,1)S(1)} collective-permute-done((bf16[256,384]{1,0:T(8,128)(2,1)S(1)}, bf16[256,384]{1,0:T(8,128)(2,1)S(1)}, u32[]{:S(2)}, u32[]{:S(2)}) %collective-permute-start.1) | collective-permute-done | bytes 196640 | tf_op jit(solution)/shard_map/ppermute | solution.py:46
  21.8 1.6 %collective-permute-start.8 = (bf16[256,384]{1,0:T(8,128)(2,1)S(1)}, bf16[256,384]{1,0:T(8,128)(2,1)S(1)}, u32[]{:S(2)}, u32[]{:S(2)}) collective-permute-start(bf16[256,384]{1,0:T(8,128)(2,1)S(1)} %collective-permute-done.forward_q.rest_2_), channel_id=1, source_target_pairs={{0,4},{4,8},{8,12},{12,14},{14,10},{10,6},{6,2},{2,0},{1,5},{5,9},... | collective-permute-start | bytes 589832 | tf_op jit(solution)/shard_map/ppermute | solution.py:46
  23.4 0.0 collective-permute-done.7.prior_kv.next_q
  23.4 0.5 collective-permute-start.9
  23.8 2.8 %near.2 = (f32[256,640]{1,0:T(8,128)S(1)}, f32[16,128]{1,0:T(8,128)S(1)}, f32[256,640]{1,0:T(8,128)S(1)}, f32[16,128]{1,0:T(8,128)S(1)}) custom-call(s32[64]{0:T(128)S(1)} %get-tuple-element.41.flags_ref, bf16[256,1536]{1,0:T(8,128)(2,1)S(1)} %get-tuple-element.42.own_q, bf16[256,1536]{1,0:T(8,128)(2,1)S(1)} %get-tuple-element.43.own_k, ...), custom_call_target="tpu_custom_call" | custom-call | flops 3000000000 | bytes 3000000 | tf_op jit(solution)/shard_map/near/pallas_call | solution.py:463
  26.6 0.6 %collective-permute-done.4.forward_q.rest_4_ = bf16[256,640]{1,0:T(8,128)(2,1)S(1)} collective-permute-done((bf16[256,640]{1,0:T(8,128)(2,1)S(1)}, bf16[256,640]{1,0:T(8,128)(2,1)S(1)}, u32[]{:S(2)}, u32[]{:S(2)}) %collective-permute-start.4) | collective-permute-done | bytes 327712 | tf_op jit(solution)/shard_map/ppermute | solution.py:46
  27.2 1.6 %collective-permute-done.6.backward_q.rest_5_ = bf16[256,640]{1,0:T(8,128)(2,1)S(1)} collective-permute-done((bf16[256,640]{1,0:T(8,128)(2,1)S(1)}, bf16[256,640]{1,0:T(8,128)(2,1)S(1)}, u32[]{:S(2)}, u32[]{:S(2)}) %collective-permute-start.6) | collective-permute-done | bytes 327712 | tf_op jit(solution)/shard_map/ppermute | solution.py:46
  28.8 2.0 %far.2 = (bf16[272,640]{1,0:T(8,128)(2,1)S(1)}, f32[16,128]{1,0:T(8,128)S(1)}) custom-call(s32[64]{0:T(128)S(1)} %get-tuple-element.41.flags_ref, bf16[256,1536]{1,0:T(8,128)(2,1)S(1)} %get-tuple-element.43.own_k, bf16[256,1536]{1,0:T(8,128)(2,1)S(1)} %get-tuple-element.44.own_v, bf16[256,640]{1,0:T(8,128)(2,1)S(1)} %collective-permute-done.4.forward_q.rest_4_, ...), custom_call_target="tpu_custom_call" | custom-call | flops 1500000000 | bytes 1500000 | tf_op jit(solution)/shard_map/far/pallas_call | solution.py:463
  30.8 1.6 %collective-permute-start.11 = (bf16[272,640]{1,0:T(8,128)(2,1)S(1)}, bf16[272,640]{1,0:T(8,128)(2,1)S(1)}, u32[]{:S(2)}, u32[]{:S(2)}) collective-permute-start(bf16[272,640]{1,0:T(8,128)(2,1)S(1)} %get-tuple-element.60), channel_id=1, source_target_pairs={{0,4},{4,8},{8,12},{12,0},{1,5},{5,9},{9,13},{13,1},{2,6},{6,10},{... | collective-permute-start | bytes 1044488 | tf_op jit(solution)/shard_map/ppermute | solution.py:52
  32.4 0.0 collective-permute-done.2.prior_kv
  32.4 2.1 %near.3 = (f32[256,384]{1,0:T(8,128)S(1)}, f32[16,128]{1,0:T(8,128)S(1)}, f32[256,384]{1,0:T(8,128)S(1)}, f32[16,128]{1,0:T(8,128)S(1)}) custom-call(s32[64]{0:T(128)S(1)} %get-tuple-element.41.flags_ref, bf16[256,1536]{1,0:T(8,128)(2,1)S(1)} %get-tuple-element.42.own_q, bf16[256,1536]{1,0:T(8,128)(2,1)S(1)} %get-tuple-element.43.own_k, ...), custom_call_target="tpu_custom_call" | custom-call | flops 1800000000 | bytes 1800000 | tf_op jit(solution)/shard_map/near/pallas_call | solution.py:463
  34.5 0.0 collective-permute-done.8.forward_q.rest_6_
  34.5 0.0 collective-permute-done.9.backward_q.rest_7_
  34.6 1.6 %far.3 = (bf16[272,384]{1,0:T(8,128)(2,1)S(1)}, f32[16,128]{1,0:T(8,128)S(1)}) custom-call(s32[64]{0:T(128)S(1)} %get-tuple-element.41.flags_ref, bf16[256,1536]{1,0:T(8,128)(2,1)S(1)} %get-tuple-element.43.own_k, bf16[256,1536]{1,0:T(8,128)(2,1)S(1)} %get-tuple-element.44.own_v, bf16[256,384]{1,0:T(8,128)(2,1)S(1)} %collective-permute-done.8.forward_q.rest_6_, ...), custom_call_target="tpu_custom_call" | custom-call | flops 900000000 | bytes 900000 | tf_op jit(solution)/shard_map/far/pallas_call | solution.py:463
  36.2 1.6 %collective-permute-start.10 = (bf16[272,384]{1,0:T(8,128)(2,1)S(1)}, bf16[272,384]{1,0:T(8,128)(2,1)S(1)}, u32[]{:S(2)}, u32[]{:S(2)}) collective-permute-start(bf16[272,384]{1,0:T(8,128)(2,1)S(1)} %get-tuple-element.57), channel_id=1, source_target_pairs={{0,4},{4,8},{8,12},{12,0},{1,5},{5,9},{9,13},{13,1},{2,6},{6,10},{... | collective-permute-start | bytes 626696 | tf_op jit(solution)/shard_map/ppermute | solution.py:52
  37.8 3.5 %keys_moved.1 = (f32[256,512]{1,0:T(8,128)S(1)}, f32[16,128]{1,0:T(8,128)S(1)}, bf16[272,512]{1,0:T(8,128)(2,1)S(1)}) custom-call(s32[64]{0:T(128)S(1)} %get-tuple-element.41.flags_ref, bf16[256,1536]{1,0:T(8,128)(2,1)S(1)} %get-tuple-element.42.own_q, bf16[256,1536]{1,0:T(8,128)(2,1)S(1)} %get-tuple-element.43.own_k, ...), custom_call_target="tpu_custom_call" | custom-call | flops 2000000000 | bytes 2000000 | tf_op jit(solution)/shard_map/keys_moved/pallas_call | solution.py:463
  41.3 0.6 collective-permute-start.14
  41.9 1.1 %collective-permute-done.11.payload_in = bf16[272,640]{1,0:T(8,128)(2,1)S(1)} collective-permute-done((bf16[272,640]{1,0:T(8,128)(2,1)S(1)}, bf16[272,640]{1,0:T(8,128)(2,1)S(1)}, u32[]{:S(2)}, u32[]{:S(2)}) %collective-permute-start.11) | collective-permute-done | bytes 348192 | tf_op jit(solution)/shard_map/ppermute | solution.py:52
  43.0 0.7 %relay.2 = (bf16[272,640]{1,0:T(8,128)(2,1)S(1)}, f32[16,128]{1,0:T(8,128)S(1)}) custom-call(s32[5]{0:T(128)S(1)} %pad_add_fusion.place_ref, f32[256,640]{1,0:T(8,128)S(1)} %get-tuple-element.58.local_out, f32[16,128]{1,0:T(8,128)S(1)} %get-tuple-element.59.local_stats, bf16[272,640]{1,0:T(8,128)(2,1)S(1)} %collective-permute-done.11.payload_in, ...), custom_call_target="tpu_custom_call" | custom-call | flops 700000000 | bytes 700000 | tf_op jit(solution)/shard_map/relay/pallas_call | solution.py:463
  43.7 0.5 collective-permute-start.13
  44.2 3.2 %collective-permute-done.10.payload_in = bf16[272,384]{1,0:T(8,128)(2,1)S(1)} collective-permute-done((bf16[272,384]{1,0:T(8,128)(2,1)S(1)}, bf16[272,384]{1,0:T(8,128)(2,1)S(1)}, u32[]{:S(2)}, u32[]{:S(2)}) %collective-permute-start.10) | collective-permute-done | bytes 208928 | tf_op jit(solution)/shard_map/ppermute | solution.py:52
  47.4 0.6 %relay.3 = (bf16[272,384]{1,0:T(8,128)(2,1)S(1)}, f32[16,128]{1,0:T(8,128)S(1)}) custom-call(s32[5]{0:T(128)S(1)} %pad_add_fusion.place_ref, f32[256,384]{1,0:T(8,128)S(1)} %get-tuple-element.55.local_out, f32[16,128]{1,0:T(8,128)S(1)} %get-tuple-element.56.local_stats, bf16[272,384]{1,0:T(8,128)(2,1)S(1)} %collective-permute-done.10.payload_in, ...), custom_call_target="tpu_custom_call" | custom-call | flops 700000000 | bytes 700000 | tf_op jit(solution)/shard_map/relay/pallas_call | solution.py:463
  48.0 1.3 %collective-permute-start.12 = (bf16[272,384]{1,0:T(8,128)(2,1)S(1)}, bf16[272,384]{1,0:T(8,128)(2,1)S(1)}, u32[]{:S(2)}, u32[]{:S(2)}) collective-permute-start(bf16[272,384]{1,0:T(8,128)(2,1)S(1)} %get-tuple-element.64), channel_id=1, source_target_pairs={{0,4},{4,8},{8,12},{1,5},{5,9},{9,13},{2,6},{6,10},{10,14},{3,7},{... | collective-permute-start | bytes 626696 | tf_op jit(solution)/shard_map/ppermute | solution.py:52
  49.3 0.0 collective-permute-done.14.payload_in
  49.3 0.8 %finish.3 = (f32[256,512]{1,0:T(8,128)S(1)}, f32[8,128]{1,0:T(8,128)S(1)}) custom-call(s32[5]{0:T(128)S(1)} %pad_add_fusion.place_ref, f32[256,512]{1,0:T(8,128)S(1)} %get-tuple-element.68.local_out, f32[16,128]{1,0:T(8,128)S(1)} %get-tuple-element.62.rest_0_.local_stats, bf16[272,512]{1,0:T(8,128)(2,1)S(1)} %collective-permute-done.14.payload_in, ...), custom_call_target="tpu_custom_call" | custom-call | flops 800000000 | bytes 800000 | tf_op jit(solution)/shard_map/finish/pallas_call | solution.py:463
  50.1 2.7 %collective-permute-done.13.payload_in = bf16[272,640]{1,0:T(8,128)(2,1)S(1)} collective-permute-done((bf16[272,640]{1,0:T(8,128)(2,1)S(1)}, bf16[272,640]{1,0:T(8,128)(2,1)S(1)}, u32[]{:S(2)}, u32[]{:S(2)}) %collective-permute-start.13) | collective-permute-done | bytes 348192 | tf_op jit(solution)/shard_map/ppermute | solution.py:52
  52.8 0.8 %finish.4 = (f32[256,640]{1,0:T(8,128)S(1)}, f32[8,128]{1,0:T(8,128)S(1)}) custom-call(s32[5]{0:T(128)S(1)} %pad_add_fusion.place_ref, f32[256,640]{1,0:T(8,128)S(1)} %get-tuple-element.66.local_out, f32[16,128]{1,0:T(8,128)S(1)} %get-tuple-element.51.rest_0_.local_stats, bf16[272,640]{1,0:T(8,128)(2,1)S(1)} %collective-permute-done.13.payload_in, ...), custom_call_target="tpu_custom_call" | custom-call | flops 800000000 | bytes 800000 | tf_op jit(solution)/shard_map/finish/pallas_call | solution.py:463
  53.7 0.0 collective-permute-done.12.payload_in
  53.7 0.7 %finish.5 = (f32[256,384]{1,0:T(8,128)S(1)}, f32[8,128]{1,0:T(8,128)S(1)}) custom-call(s32[5]{0:T(128)S(1)} %pad_add_fusion.place_ref, f32[256,384]{1,0:T(8,128)S(1)} %get-tuple-element.53.local_out, f32[16,128]{1,0:T(8,128)S(1)} %get-tuple-element.54.rest_0_.local_stats, bf16[272,384]{1,0:T(8,128)(2,1)S(1)} %collective-permute-done.12.payload_in, ...), custom_call_target="tpu_custom_call" | custom-call | flops 800000000 | bytes 800000 | tf_op jit(solution)/shard_map/finish/pallas_call | solution.py:463
  54.4 0.1 collective-permute-start.15
  54.5 1.0 %collective-permute-start.16 = (f32[8,128]{1,0:T(8,128)S(1)}, f32[8,128]{1,0:T(8,128)S(1)}, u32[]{:S(2)}, u32[]{:S(2)}) collective-permute-start(f32[8,128]{1,0:T(8,128)S(1)} %get-tuple-element.73.refs_0_), channel_id=1, source_target_pairs={{0,2},{1,3},{2,0},{3,1},{4,6},{5,7},{6,4},{7,5},{8,10},{9,11},{10,... | collective-permute-start | bytes 12296 | tf_op jit(solution)/shard_map/ppermute | solution.py:584
  55.5 0.8 %collective-permute-start.17 = (f32[8,128]{1,0:T(8,128)S(1)}, f32[8,128]{1,0:T(8,128)S(1)}, u32[]{:S(2)}, u32[]{:S(2)}) collective-permute-start(f32[8,128]{1,0:T(8,128)S(1)} %get-tuple-element.73.refs_0_), channel_id=1, source_target_pairs={{0,1},{1,0},{2,3},{3,2},{4,5},{5,4},{6,7},{7,6},{8,9},{9,8},{10,11... | collective-permute-start | bytes 12296 | tf_op jit(solution)/shard_map/ppermute | solution.py:584
  56.3 1.2 %collective-permute-done.15.refs_1_ = f32[8,128]{1,0:T(8,128)S(1)} collective-permute-done((f32[8,128]{1,0:T(8,128)S(1)}, f32[8,128]{1,0:T(8,128)S(1)}, u32[]{:S(2)}, u32[]{:S(2)}) %collective-permute-start.15) | collective-permute-done | bytes 4128 | tf_op jit(solution)/shard_map/ppermute | solution.py:584
  57.5 0.7 %collective-permute-done.16.refs_2_ = f32[8,128]{1,0:T(8,128)S(1)} collective-permute-done((f32[8,128]{1,0:T(8,128)S(1)}, f32[8,128]{1,0:T(8,128)S(1)}, u32[]{:S(2)}, u32[]{:S(2)}) %collective-permute-start.16) | collective-permute-done | bytes 4128 | tf_op jit(solution)/shard_map/ppermute | solution.py:584
  58.2 0.0 collective-permute-done.17.refs_3_
  58.2 1.2 %scale.1 = bf16[256,1536]{1,0:T(8,128)(2,1)} custom-call(f32[8,128]{1,0:T(8,128)S(1)} %get-tuple-element.73.refs_0_, f32[8,128]{1,0:T(8,128)S(1)} %collective-permute-done.15.refs_1_, f32[8,128]{1,0:T(8,128)S(1)} %collective-permute-done.16.refs_2_, f32[8,128]{1,0:T(8,128)S(1)} %collective-permute-done.17.refs_3_, f32[256,640]{1,0:T(8,128)S(1)} %get-tuple-element.74.refs_4_, ...), custom_call_target="tpu_custom_call" | custom-call | tf_op jit(solution)/shard_map/scale/pallas_call | solution.py:585
  (2 shorter events, 0.0 us)
Async XLA Ops:
  0.1 18.0 %copy-start = (bf16[16,1536]{1,0:T(8,128)(2,1)S(1)}, bf16[16,1536]{1,0:T(8,128)(2,1)}, u32[]{:S(2)}) copy-start(bf16[16,1536]{1,0:T(8,128)(2,1)} %gate_table.1) | copy-start | bytes 147460
  0.1 18.0 %copy-start.1 = (s32[2,4,4,4]{3,2,1,0:T(4,128)S(1)}, s32[2,4,4,4]{3,2,1,0:T(4,128)}, u32[]{:S(2)}) copy-start(s32[2,4,4,4]{3,2,1,0:T(4,128)} %ranges_ref.1) | copy-start | bytes 1540
  2.3 21.0 %collective-permute-start.7 = (bf16[256,1280]{1,0:T(8,128)(2,1)S(1)}, bf16[256,1280]{1,0:T(8,128)(2,1)S(1)}, u32[]{:S(2)}, u32[]{:S(2)}) collective-permute-start(bf16[256,1280]{1,0:T(8,128)(2,1)S(1)} %get-tuple-element.50), channel_id=1, source_target_pairs={{0,16},{16,0},{1,17},{17,1},{2,18},{18,2},{3,19},{19,3},{4,20},{20... | collective-permute-start | bytes 1966088 | tf_op jit(solution)/shard_map/ppermute | solution.py:30
  5.4 10.6 %collective-permute-start.3 = (bf16[256,640]{1,0:T(8,128)(2,1)S(1)}, bf16[256,640]{1,0:T(8,128)(2,1)S(1)}, u32[]{:S(2)}, u32[]{:S(2)}) collective-permute-start(bf16[256,640]{1,0:T(8,128)(2,1)S(1)} %get-tuple-element.48), channel_id=1, source_target_pairs={{0,4},{4,8},{8,12},{12,14},{14,10},{10,6},{6,2},{2,0},{1,5},{5,9},... | collective-permute-start | bytes 983048 | tf_op jit(solution)/shard_map/ppermute | solution.py:46
  6.9 10.7 %collective-permute-start.5 = (bf16[256,640]{1,0:T(8,128)(2,1)S(1)}, bf16[256,640]{1,0:T(8,128)(2,1)S(1)}, u32[]{:S(2)}, u32[]{:S(2)}) collective-permute-start(bf16[256,640]{1,0:T(8,128)(2,1)S(1)} %get-tuple-element.49), channel_id=1, source_target_pairs={{4,0},{8,4},{12,8},{14,12},{10,14},{6,10},{2,6},{0,2},{5,1},{9,5},... | collective-permute-start | bytes 983048 | tf_op jit(solution)/shard_map/ppermute | solution.py:46
  7.4 10.7 %copy-start.2 = (s32[4]{0:T(128)S(1)}, s32[4]{0:T(128)}, u32[]{:S(2)}) copy-start(s32[4]{0:T(128)} %levels_ref.1) | copy-start | bytes 52
  7.4 12.8 %collective-permute-start = (bf16[256,384]{1,0:T(8,128)(2,1)S(1)}, bf16[256,384]{1,0:T(8,128)(2,1)S(1)}, u32[]{:S(2)}, u32[]{:S(2)}) collective-permute-start(bf16[256,384]{1,0:T(8,128)(2,1)S(1)} %get-tuple-element.45), channel_id=1, source_target_pairs={{0,4},{4,8},{8,12},{12,14},{14,10},{10,6},{6,2},{2,0},{1,5},{5,9},... | collective-permute-start | bytes 589832 | tf_op jit(solution)/shard_map/ppermute | solution.py:46
  9.0 12.8 %collective-permute-start.1 = (bf16[256,384]{1,0:T(8,128)(2,1)S(1)}, bf16[256,384]{1,0:T(8,128)(2,1)S(1)}, u32[]{:S(2)}, u32[]{:S(2)}) collective-permute-start(bf16[256,384]{1,0:T(8,128)(2,1)S(1)} %get-tuple-element.46), channel_id=1, source_target_pairs={{4,0},{8,4},{12,8},{14,12},{10,14},{6,10},{2,6},{0,2},{5,1},{9,5},... | collective-permute-start | bytes 589832 | tf_op jit(solution)/shard_map/ppermute | solution.py:46
  16.0 11.2 %collective-permute-start.4 = (bf16[256,640]{1,0:T(8,128)(2,1)S(1)}, bf16[256,640]{1,0:T(8,128)(2,1)S(1)}, u32[]{:S(2)}, u32[]{:S(2)}) collective-permute-start(bf16[256,640]{1,0:T(8,128)(2,1)S(1)} %collective-permute-done.3.forward_q.rest_0_), channel_id=1, source_target_pairs={{0,4},{4,8},{8,12},{12,14},{14,10},{10,6},{6,2},{2,0},{1,5},{5,9},... | collective-permute-start | bytes 983048 | tf_op jit(solution)/shard_map/ppermute | solution.py:46
  17.6 11.2 %collective-permute-start.6 = (bf16[256,640]{1,0:T(8,128)(2,1)S(1)}, bf16[256,640]{1,0:T(8,128)(2,1)S(1)}, u32[]{:S(2)}, u32[]{:S(2)}) collective-permute-start(bf16[256,640]{1,0:T(8,128)(2,1)S(1)} %collective-permute-done.5.backward_q.rest_1_), channel_id=1, source_target_pairs={{4,0},{8,4},{12,8},{14,12},{10,14},{6,10},{2,6},{0,2},{5,1},{9,5},... | collective-permute-start | bytes 983048 | tf_op jit(solution)/shard_map/ppermute | solution.py:46
  20.2 12.2 %collective-permute-start.2 = (bf16[256,768]{1,0:T(8,128)(2,1)S(1)}, bf16[256,768]{1,0:T(8,128)(2,1)S(1)}, u32[]{:S(2)}, u32[]{:S(2)}) collective-permute-start(bf16[256,768]{1,0:T(8,128)(2,1)S(1)} %get-tuple-element.47), channel_id=1, source_target_pairs={{0,16},{16,0},{1,17},{17,1},{2,18},{18,2},{3,19},{19,3},{4,20},{20... | collective-permute-start | bytes 1179656 | tf_op jit(solution)/shard_map/ppermute | solution.py:30
  21.8 12.7 %collective-permute-start.8 = (bf16[256,384]{1,0:T(8,128)(2,1)S(1)}, bf16[256,384]{1,0:T(8,128)(2,1)S(1)}, u32[]{:S(2)}, u32[]{:S(2)}) collective-permute-start(bf16[256,384]{1,0:T(8,128)(2,1)S(1)} %collective-permute-done.forward_q.rest_2_), channel_id=1, source_target_pairs={{0,4},{4,8},{8,12},{12,14},{14,10},{10,6},{6,2},{2,0},{1,5},{5,9},... | collective-permute-start | bytes 589832 | tf_op jit(solution)/shard_map/ppermute | solution.py:46
  23.4 11.2 %collective-permute-start.9 = (bf16[256,384]{1,0:T(8,128)(2,1)S(1)}, bf16[256,384]{1,0:T(8,128)(2,1)S(1)}, u32[]{:S(2)}, u32[]{:S(2)}) collective-permute-start(bf16[256,384]{1,0:T(8,128)(2,1)S(1)} %collective-permute-done.1.backward_q.rest_3_), channel_id=1, source_target_pairs={{4,0},{8,4},{12,8},{14,12},{10,14},{6,10},{2,6},{0,2},{5,1},{9,5},... | collective-permute-start | bytes 589832 | tf_op jit(solution)/shard_map/ppermute | solution.py:46
  30.8 12.2 %collective-permute-start.11 = (bf16[272,640]{1,0:T(8,128)(2,1)S(1)}, bf16[272,640]{1,0:T(8,128)(2,1)S(1)}, u32[]{:S(2)}, u32[]{:S(2)}) collective-permute-start(bf16[272,640]{1,0:T(8,128)(2,1)S(1)} %get-tuple-element.60), channel_id=1, source_target_pairs={{0,4},{4,8},{8,12},{12,0},{1,5},{5,9},{9,13},{13,1},{2,6},{6,10},{... | collective-permute-start | bytes 1044488 | tf_op jit(solution)/shard_map/ppermute | solution.py:52
  36.2 11.2 %collective-permute-start.10 = (bf16[272,384]{1,0:T(8,128)(2,1)S(1)}, bf16[272,384]{1,0:T(8,128)(2,1)S(1)}, u32[]{:S(2)}, u32[]{:S(2)}) collective-permute-start(bf16[272,384]{1,0:T(8,128)(2,1)S(1)} %get-tuple-element.57), channel_id=1, source_target_pairs={{0,4},{4,8},{8,12},{12,0},{1,5},{5,9},{9,13},{13,1},{2,6},{6,10},{... | collective-permute-start | bytes 626696 | tf_op jit(solution)/shard_map/ppermute | solution.py:52
  41.3 8.0 %collective-permute-start.14 = (bf16[272,512]{1,0:T(8,128)(2,1)S(1)}, bf16[272,512]{1,0:T(8,128)(2,1)S(1)}, u32[]{:S(2)}, u32[]{:S(2)}) collective-permute-start(bf16[272,512]{1,0:T(8,128)(2,1)S(1)} %get-tuple-element.69), channel_id=1, source_target_pairs={{0,16},{16,0},{1,17},{17,1},{2,18},{18,2},{3,19},{19,3},{4,20},{20... | collective-permute-start | bytes 835592 | tf_op jit(solution)/shard_map/ppermute | solution.py:30
  43.7 9.1 %collective-permute-start.13 = (bf16[272,640]{1,0:T(8,128)(2,1)S(1)}, bf16[272,640]{1,0:T(8,128)(2,1)S(1)}, u32[]{:S(2)}, u32[]{:S(2)}) collective-permute-start(bf16[272,640]{1,0:T(8,128)(2,1)S(1)} %get-tuple-element.67), channel_id=1, source_target_pairs={{0,4},{4,8},{8,12},{12,0},{1,5},{5,9},{9,13},{13,1},{2,6},{6,10},{... | collective-permute-start | bytes 1044488 | tf_op jit(solution)/shard_map/ppermute | solution.py:52
  48.0 5.7 %collective-permute-start.12 = (bf16[272,384]{1,0:T(8,128)(2,1)S(1)}, bf16[272,384]{1,0:T(8,128)(2,1)S(1)}, u32[]{:S(2)}, u32[]{:S(2)}) collective-permute-start(bf16[272,384]{1,0:T(8,128)(2,1)S(1)} %get-tuple-element.64), channel_id=1, source_target_pairs={{0,4},{4,8},{8,12},{1,5},{5,9},{9,13},{2,6},{6,10},{10,14},{3,7},{... | collective-permute-start | bytes 626696 | tf_op jit(solution)/shard_map/ppermute | solution.py:52
  54.4 3.1 %collective-permute-start.15 = (f32[8,128]{1,0:T(8,128)S(1)}, f32[8,128]{1,0:T(8,128)S(1)}, u32[]{:S(2)}, u32[]{:S(2)}) collective-permute-start(f32[8,128]{1,0:T(8,128)S(1)} %get-tuple-element.73.refs_0_), channel_id=1, source_target_pairs={{0,3},{1,2},{2,1},{3,0},{4,7},{5,6},{6,5},{7,4},{8,11},{9,10},{10,... | collective-permute-start | bytes 12296 | tf_op jit(solution)/shard_map/ppermute | solution.py:584
  54.5 3.7 %collective-permute-start.16 = (f32[8,128]{1,0:T(8,128)S(1)}, f32[8,128]{1,0:T(8,128)S(1)}, u32[]{:S(2)}, u32[]{:S(2)}) collective-permute-start(f32[8,128]{1,0:T(8,128)S(1)} %get-tuple-element.73.refs_0_), channel_id=1, source_target_pairs={{0,2},{1,3},{2,0},{3,1},{4,6},{5,7},{6,4},{7,5},{8,10},{9,11},{10,... | collective-permute-start | bytes 12296 | tf_op jit(solution)/shard_map/ppermute | solution.py:584
  55.5 2.6 %collective-permute-start.17 = (f32[8,128]{1,0:T(8,128)S(1)}, f32[8,128]{1,0:T(8,128)S(1)}, u32[]{:S(2)}, u32[]{:S(2)}) collective-permute-start(f32[8,128]{1,0:T(8,128)S(1)} %get-tuple-element.73.refs_0_), channel_id=1, source_target_pairs={{0,1},{1,0},{2,3},{3,2},{4,5},{5,4},{6,7},{7,6},{8,9},{9,8},{10,11... | collective-permute-start | bytes 12296 | tf_op jit(solution)/shard_map/ppermute | solution.py:584

commit v7 on v6

--- a/solution.py
+++ b/solution.py
@@ -400,7 +400,9 @@
 
 def scale_kernel(head_counts, feature_count, device_count, *refs):
     squares = sum(ref[...] for ref in refs[:device_count])
-    parts, out = refs[device_count:-1], refs[-1]
+    parts = refs[device_count:-3]
+    out_hbm, out, semaphores = refs[-3:]
+    copies = []
     factors = as_columns(lax.rsqrt(squares / feature_count + 1e-06))
     for slot in range(out.shape[0] // BLOCK):
         rows = stretch_rows(slot)
@@ -412,6 +414,10 @@
                     part[rows, head_columns(head)] * factor
                 ).astype(jnp.bfloat16)
             base += head_count
+        copies.append(pltpu.make_async_copy(out.at[rows], out_hbm.at[rows], semaphores.at[slot]))
+        copies[-1].start()
+    for copy in copies:
+        copy.wait()
 
 
 def cost(microseconds):
@@ -586,7 +592,11 @@
         functools.partial(scale_kernel, head_counts, float(HEADS * HEAD_DIM), device_count),
         out_shape=jax.ShapeDtypeStruct((token_rows, width_dev), jnp.bfloat16),
         in_specs=[VMEM] * (device_count + len(finished)),
-        out_specs=VMEM,
+        out_specs=pl.BlockSpec(memory_space=pltpu.HBM),
+        scratch_shapes=[
+            pltpu.VMEM((token_rows, width_dev), jnp.bfloat16),
+            pltpu.SemaphoreType.DMA((pair_count,)),
+        ],
         compiler_params=PARAMS,
         name="scale",
     )(*shares, *finished)

time: 59.5 us -> 59.5 us (level)
  no operation moved by 1% of the time
where the time goes in v7:
time: 59.5 us; the launch traced here: 59.3 us
  Pallas kernels  20.7 us (35%)
  waiting for transfers between devices  19.7 us (33%)
  starting transfers between devices  18.7 us (31%)
    pallas_call x10, Pallas kernels, run(): pl.pallas_call(functools.partial(kernel, head_counts[chunk]), out_shape=o...  15.6 us
    ppermute x8, waiting for transfers between devices, round_trip(): return lax.ppermute(block, ('cp', 'tp'), route)  10.8 us
    ppermute x8, starting transfers between devices, round_trip(): return lax.ppermute(block, ('cp', 'tp'), route)  8.1 us
    ppermute x4, waiting for transfers between devices, passed_up(): return lax.ppermute(block, 'cp', route)  7.02 us
    ppermute x4, starting transfers between devices, passed_up(): return lax.ppermute(block, 'cp', route)  5.03 us
    ppermute x3, starting transfers between devices, exchanged(): return lax.ppermute(block, 'stretch', [(0, 1), (1, 0)])  3.63 us
    pallas_call x1, Pallas kernels, on_device(): pl.pallas_call(functools.partial(pack_kernel, CHUNKS, KEYS_MOVED), out_sh...  2.25 us
    ppermute x3, starting transfers between devices, on_device(): shares.append(lax.ppermute(squares, 'tp', route))  1.92 us
  transfers between devices with their start and end apart: 18, of which 10 were waited for; matrix products, arithmetic and copies ran while one was open for 0% of the time, Pallas kernels for 28%

profile of v7, /device:TPU:0, one launch (start us, length us, event | category | flops | bytes accessed | tf_op | source)
XLA Modules:
  0.0 59.3 jit_solution(13376332979728922621)
XLA Ops:
  0.0 0.1 pad_add_fusion.place_ref
  0.1 0.0 copy-start
  0.1 0.0 copy-start.1
  0.1 2.3 %pack.1 = (bf16[256,1536]{1,0:T(8,128)(2,1)S(1)}, bf16[256,1536]{1,0:T(8,128)(2,1)S(1)}, bf16[256,1536]{1,0:T(8,128)(2,1)S(1)}, bf16[256,1280]{1,0:T(8,128)(2,1)...) custom-call(s32[5]{0:T(128)S(1)} %pad_add_fusion.place_ref, ...), custom_call_target="tpu_custom_call" | custom-call | flops 1000000000 | bytes 1000000 | tf_op jit(solution)/shard_map/pack/pallas_call | solution.py:484
  2.3 3.0 %collective-permute-start.7 = (bf16[256,1280]{1,0:T(8,128)(2,1)S(1)}, bf16[256,1280]{1,0:T(8,128)(2,1)S(1)}, u32[]{:S(2)}, u32[]{:S(2)}) collective-permute-start(bf16[256,1280]{1,0:T(8,128)(2,1)S(1)} %get-tuple-element.50), channel_id=1, source_target_pairs={{0,16},{16,0},{1,17},{17,1},{2,18},{18,2},{3,19},{19,3},{4,20},{20... | collective-permute-start | bytes 1966088 | tf_op jit(solution)/shard_map/ppermute | solution.py:30
  5.4 1.6 %collective-permute-start.3 = (bf16[256,640]{1,0:T(8,128)(2,1)S(1)}, bf16[256,640]{1,0:T(8,128)(2,1)S(1)}, u32[]{:S(2)}, u32[]{:S(2)}) collective-permute-start(bf16[256,640]{1,0:T(8,128)(2,1)S(1)} %get-tuple-element.48), channel_id=1, source_target_pairs={{0,4},{4,8},{8,12},{12,14},{14,10},{10,6},{6,2},{2,0},{1,5},{5,9},... | collective-permute-start | bytes 983048 | tf_op jit(solution)/shard_map/ppermute | solution.py:46
  6.9 0.4 collective-permute-start.5
  7.4 0.0 copy-start.2
  7.4 1.6 %collective-permute-start = (bf16[256,384]{1,0:T(8,128)(2,1)S(1)}, bf16[256,384]{1,0:T(8,128)(2,1)S(1)}, u32[]{:S(2)}, u32[]{:S(2)}) collective-permute-start(bf16[256,384]{1,0:T(8,128)(2,1)S(1)} %get-tuple-element.45), channel_id=1, source_target_pairs={{0,4},{4,8},{8,12},{12,14},{14,10},{10,6},{6,2},{2,0},{1,5},{5,9},... | collective-permute-start | bytes 589832 | tf_op jit(solution)/shard_map/ppermute | solution.py:46
  9.0 0.4 collective-permute-start.1
  9.4 6.6 %collective-permute-done.3.forward_q.rest_0_ = bf16[256,640]{1,0:T(8,128)(2,1)S(1)} collective-permute-done((bf16[256,640]{1,0:T(8,128)(2,1)S(1)}, bf16[256,640]{1,0:T(8,128)(2,1)S(1)}, u32[]{:S(2)}, u32[]{:S(2)}) %collective-permute-start.3) | collective-permute-done | bytes 327712 | tf_op jit(solution)/shard_map/ppermute | solution.py:46
  16.0 1.6 %collective-permute-start.4 = (bf16[256,640]{1,0:T(8,128)(2,1)S(1)}, bf16[256,640]{1,0:T(8,128)(2,1)S(1)}, u32[]{:S(2)}, u32[]{:S(2)}) collective-permute-start(bf16[256,640]{1,0:T(8,128)(2,1)S(1)} %collective-permute-done.3.forward_q.rest_0_), channel_id=1, source_target_pairs={{0,4},{4,8},{8,12},{12,14},{14,10},{10,6},{6,2},{2,0},{1,5},{5,9},... | collective-permute-start | bytes 983048 | tf_op jit(solution)/shard_map/ppermute | solution.py:46
  17.6 0.0 collective-permute-done.5.backward_q.rest_1_
  17.6 0.4 collective-permute-start.6
  18.0 0.0 copy-done
  18.0 0.0 copy-done.1
  18.1 0.0 copy-done.2
  18.1 1.7 %plan.1 = (f32[8,1536]{1,0:T(8,128)S(1)}, s32[64]{0:T(128)S(1)}) custom-call(s32[5]{0:T(128)S(1)} %pad_add_fusion.place_ref, s32[2,4,4,4]{3,2,1,0:T(4,128)S(1)} %copy-done.1, s32[4]{0:T(128)S(1)} %copy-done.2, bf16[16,1536]{1,0:T(8,128)(2,1)S(1)} %copy-done), custom_call_target="tpu_custom_call" | custom-call | flops 600000000 | bytes 600000 | tf_op jit(solution)/shard_map/plan/pallas_call | solution.py:506
  19.7 0.5 collective-permute-done.forward_q.rest_2_
  20.2 0.0 collective-permute-start.2
  20.2 1.6 %collective-permute-done.1.backward_q.rest_3_ = bf16[256,384]{1,0:T(8,128)(2,1)S(1)} collective-permute-done((bf16[256,384]{1,0:T(8,128)(2,1)S(1)}, bf16[256,384]{1,0:T(8,128)(2,1)S(1)}, u32[]{:S(2)}, u32[]{:S(2)}) %collective-permute-start.1) | collective-permute-done | bytes 196640 | tf_op jit(solution)/shard_map/ppermute | solution.py:46
  21.8 1.6 %collective-permute-start.8 = (bf16[256,384]{1,0:T(8,128)(2,1)S(1)}, bf16[256,384]{1,0:T(8,128)(2,1)S(1)}, u32[]{:S(2)}, u32[]{:S(2)}) collective-permute-start(bf16[256,384]{1,0:T(8,128)(2,1)S(1)} %collective-permute-done.forward_q.rest_2_), channel_id=1, source_target_pairs={{0,4},{4,8},{8,12},{12,14},{14,10},{10,6},{6,2},{2,0},{1,5},{5,9},... | collective-permute-start | bytes 589832 | tf_op jit(solution)/shard_map/ppermute | solution.py:46
  23.4 0.0 collective-permute-done.7.prior_kv.next_q
  23.4 0.5 collective-permute-start.9
  23.8 2.8 %near.2 = (f32[256,640]{1,0:T(8,128)S(1)}, f32[16,128]{1,0:T(8,128)S(1)}, f32[256,640]{1,0:T(8,128)S(1)}, f32[16,128]{1,0:T(8,128)S(1)}) custom-call(s32[64]{0:T(128)S(1)} %get-tuple-element.41.flags_ref, bf16[256,1536]{1,0:T(8,128)(2,1)S(1)} %get-tuple-element.42.own_q, bf16[256,1536]{1,0:T(8,128)(2,1)S(1)} %get-tuple-element.43.own_k, ...), custom_call_target="tpu_custom_call" | custom-call | flops 3000000000 | bytes 3000000 | tf_op jit(solution)/shard_map/near/pallas_call | solution.py:469
  26.6 0.6 %collective-permute-done.4.forward_q.rest_4_ = bf16[256,640]{1,0:T(8,128)(2,1)S(1)} collective-permute-done((bf16[256,640]{1,0:T(8,128)(2,1)S(1)}, bf16[256,640]{1,0:T(8,128)(2,1)S(1)}, u32[]{:S(2)}, u32[]{:S(2)}) %collective-permute-start.4) | collective-permute-done | bytes 327712 | tf_op jit(solution)/shard_map/ppermute | solution.py:46
  27.2 1.6 %collective-permute-done.6.backward_q.rest_5_ = bf16[256,640]{1,0:T(8,128)(2,1)S(1)} collective-permute-done((bf16[256,640]{1,0:T(8,128)(2,1)S(1)}, bf16[256,640]{1,0:T(8,128)(2,1)S(1)}, u32[]{:S(2)}, u32[]{:S(2)}) %collective-permute-start.6) | collective-permute-done | bytes 327712 | tf_op jit(solution)/shard_map/ppermute | solution.py:46
  28.8 2.0 %far.2 = (bf16[272,640]{1,0:T(8,128)(2,1)S(1)}, f32[16,128]{1,0:T(8,128)S(1)}) custom-call(s32[64]{0:T(128)S(1)} %get-tuple-element.41.flags_ref, bf16[256,1536]{1,0:T(8,128)(2,1)S(1)} %get-tuple-element.43.own_k, bf16[256,1536]{1,0:T(8,128)(2,1)S(1)} %get-tuple-element.44.own_v, bf16[256,640]{1,0:T(8,128)(2,1)S(1)} %collective-permute-done.4.forward_q.rest_4_, ...), custom_call_target="tpu_custom_call" | custom-call | flops 1500000000 | bytes 1500000 | tf_op jit(solution)/shard_map/far/pallas_call | solution.py:469
  30.8 1.6 %collective-permute-start.11 = (bf16[272,640]{1,0:T(8,128)(2,1)S(1)}, bf16[272,640]{1,0:T(8,128)(2,1)S(1)}, u32[]{:S(2)}, u32[]{:S(2)}) collective-permute-start(bf16[272,640]{1,0:T(8,128)(2,1)S(1)} %get-tuple-element.60), channel_id=1, source_target_pairs={{0,4},{4,8},{8,12},{12,0},{1,5},{5,9},{9,13},{13,1},{2,6},{6,10},{... | collective-permute-start | bytes 1044488 | tf_op jit(solution)/shard_map/ppermute | solution.py:52
  32.4 0.0 collective-permute-done.2.prior_kv
  32.4 2.1 %near.3 = (f32[256,384]{1,0:T(8,128)S(1)}, f32[16,128]{1,0:T(8,128)S(1)}, f32[256,384]{1,0:T(8,128)S(1)}, f32[16,128]{1,0:T(8,128)S(1)}) custom-call(s32[64]{0:T(128)S(1)} %get-tuple-element.41.flags_ref, bf16[256,1536]{1,0:T(8,128)(2,1)S(1)} %get-tuple-element.42.own_q, bf16[256,1536]{1,0:T(8,128)(2,1)S(1)} %get-tuple-element.43.own_k, ...), custom_call_target="tpu_custom_call" | custom-call | flops 1800000000 | bytes 1800000 | tf_op jit(solution)/shard_map/near/pallas_call | solution.py:469
  34.5 0.0 collective-permute-done.8.forward_q.rest_6_
  34.5 0.0 collective-permute-done.9.backward_q.rest_7_
  34.6 1.6 %far.3 = (bf16[272,384]{1,0:T(8,128)(2,1)S(1)}, f32[16,128]{1,0:T(8,128)S(1)}) custom-call(s32[64]{0:T(128)S(1)} %get-tuple-element.41.flags_ref, bf16[256,1536]{1,0:T(8,128)(2,1)S(1)} %get-tuple-element.43.own_k, bf16[256,1536]{1,0:T(8,128)(2,1)S(1)} %get-tuple-element.44.own_v, bf16[256,384]{1,0:T(8,128)(2,1)S(1)} %collective-permute-done.8.forward_q.rest_6_, ...), custom_call_target="tpu_custom_call" | custom-call | flops 900000000 | bytes 900000 | tf_op jit(solution)/shard_map/far/pallas_call | solution.py:469
  36.2 1.6 %collective-permute-start.10 = (bf16[272,384]{1,0:T(8,128)(2,1)S(1)}, bf16[272,384]{1,0:T(8,128)(2,1)S(1)}, u32[]{:S(2)}, u32[]{:S(2)}) collective-permute-start(bf16[272,384]{1,0:T(8,128)(2,1)S(1)} %get-tuple-element.57), channel_id=1, source_target_pairs={{0,4},{4,8},{8,12},{12,0},{1,5},{5,9},{9,13},{13,1},{2,6},{6,10},{... | collective-permute-start | bytes 626696 | tf_op jit(solution)/shard_map/ppermute | solution.py:52
  37.8 3.5 %keys_moved.1 = (f32[256,512]{1,0:T(8,128)S(1)}, f32[16,128]{1,0:T(8,128)S(1)}, bf16[272,512]{1,0:T(8,128)(2,1)S(1)}) custom-call(s32[64]{0:T(128)S(1)} %get-tuple-element.41.flags_ref, bf16[256,1536]{1,0:T(8,128)(2,1)S(1)} %get-tuple-element.42.own_q, bf16[256,1536]{1,0:T(8,128)(2,1)S(1)} %get-tuple-element.43.own_k, ...), custom_call_target="tpu_custom_call" | custom-call | flops 2000000000 | bytes 2000000 | tf_op jit(solution)/shard_map/keys_moved/pallas_call | solution.py:469
  41.3 0.6 collective-permute-start.14
  41.9 1.1 %collective-permute-done.11.payload_in = bf16[272,640]{1,0:T(8,128)(2,1)S(1)} collective-permute-done((bf16[272,640]{1,0:T(8,128)(2,1)S(1)}, bf16[272,640]{1,0:T(8,128)(2,1)S(1)}, u32[]{:S(2)}, u32[]{:S(2)}) %collective-permute-start.11) | collective-permute-done | bytes 348192 | tf_op jit(solution)/shard_map/ppermute | solution.py:52
  43.0 0.7 %relay.2 = (bf16[272,640]{1,0:T(8,128)(2,1)S(1)}, f32[16,128]{1,0:T(8,128)S(1)}) custom-call(s32[5]{0:T(128)S(1)} %pad_add_fusion.place_ref, f32[256,640]{1,0:T(8,128)S(1)} %get-tuple-element.58.local_out, f32[16,128]{1,0:T(8,128)S(1)} %get-tuple-element.59.local_stats, bf16[272,640]{1,0:T(8,128)(2,1)S(1)} %collective-permute-done.11.payload_in, ...), custom_call_target="tpu_custom_call" | custom-call | flops 700000000 | bytes 700000 | tf_op jit(solution)/shard_map/relay/pallas_call | solution.py:469
  43.7 0.5 collective-permute-start.13
  44.2 3.2 %collective-permute-done.10.payload_in = bf16[272,384]{1,0:T(8,128)(2,1)S(1)} collective-permute-done((bf16[272,384]{1,0:T(8,128)(2,1)S(1)}, bf16[272,384]{1,0:T(8,128)(2,1)S(1)}, u32[]{:S(2)}, u32[]{:S(2)}) %collective-permute-start.10) | collective-permute-done | bytes 208928 | tf_op jit(solution)/shard_map/ppermute | solution.py:52
  47.4 0.6 %relay.3 = (bf16[272,384]{1,0:T(8,128)(2,1)S(1)}, f32[16,128]{1,0:T(8,128)S(1)}) custom-call(s32[5]{0:T(128)S(1)} %pad_add_fusion.place_ref, f32[256,384]{1,0:T(8,128)S(1)} %get-tuple-element.55.local_out, f32[16,128]{1,0:T(8,128)S(1)} %get-tuple-element.56.local_stats, bf16[272,384]{1,0:T(8,128)(2,1)S(1)} %collective-permute-done.10.payload_in, ...), custom_call_target="tpu_custom_call" | custom-call | flops 700000000 | bytes 700000 | tf_op jit(solution)/shard_map/relay/pallas_call | solution.py:469
  48.0 1.3 %collective-permute-start.12 = (bf16[272,384]{1,0:T(8,128)(2,1)S(1)}, bf16[272,384]{1,0:T(8,128)(2,1)S(1)}, u32[]{:S(2)}, u32[]{:S(2)}) collective-permute-start(bf16[272,384]{1,0:T(8,128)(2,1)S(1)} %get-tuple-element.64), channel_id=1, source_target_pairs={{0,4},{4,8},{8,12},{1,5},{5,9},{9,13},{2,6},{6,10},{10,14},{3,7},{... | collective-permute-start | bytes 626696 | tf_op jit(solution)/shard_map/ppermute | solution.py:52
  49.3 0.0 collective-permute-done.14.payload_in
  49.3 0.8 %finish.3 = (f32[256,512]{1,0:T(8,128)S(1)}, f32[8,128]{1,0:T(8,128)S(1)}) custom-call(s32[5]{0:T(128)S(1)} %pad_add_fusion.place_ref, f32[256,512]{1,0:T(8,128)S(1)} %get-tuple-element.68.local_out, f32[16,128]{1,0:T(8,128)S(1)} %get-tuple-element.62.rest_0_.local_stats, bf16[272,512]{1,0:T(8,128)(2,1)S(1)} %collective-permute-done.14.payload_in, ...), custom_call_target="tpu_custom_call" | custom-call | flops 800000000 | bytes 800000 | tf_op jit(solution)/shard_map/finish/pallas_call | solution.py:469
  50.1 2.7 %collective-permute-done.13.payload_in = bf16[272,640]{1,0:T(8,128)(2,1)S(1)} collective-permute-done((bf16[272,640]{1,0:T(8,128)(2,1)S(1)}, bf16[272,640]{1,0:T(8,128)(2,1)S(1)}, u32[]{:S(2)}, u32[]{:S(2)}) %collective-permute-start.13) | collective-permute-done | bytes 348192 | tf_op jit(solution)/shard_map/ppermute | solution.py:52
  52.8 0.8 %finish.4 = (f32[256,640]{1,0:T(8,128)S(1)}, f32[8,128]{1,0:T(8,128)S(1)}) custom-call(s32[5]{0:T(128)S(1)} %pad_add_fusion.place_ref, f32[256,640]{1,0:T(8,128)S(1)} %get-tuple-element.66.local_out, f32[16,128]{1,0:T(8,128)S(1)} %get-tuple-element.51.rest_0_.local_stats, bf16[272,640]{1,0:T(8,128)(2,1)S(1)} %collective-permute-done.13.payload_in, ...), custom_call_target="tpu_custom_call" | custom-call | flops 800000000 | bytes 800000 | tf_op jit(solution)/shard_map/finish/pallas_call | solution.py:469
  53.7 0.0 collective-permute-done.12.payload_in
  53.7 0.7 %finish.5 = (f32[256,384]{1,0:T(8,128)S(1)}, f32[8,128]{1,0:T(8,128)S(1)}) custom-call(s32[5]{0:T(128)S(1)} %pad_add_fusion.place_ref, f32[256,384]{1,0:T(8,128)S(1)} %get-tuple-element.53.local_out, f32[16,128]{1,0:T(8,128)S(1)} %get-tuple-element.54.rest_0_.local_stats, bf16[272,384]{1,0:T(8,128)(2,1)S(1)} %collective-permute-done.12.payload_in, ...), custom_call_target="tpu_custom_call" | custom-call | flops 800000000 | bytes 800000 | tf_op jit(solution)/shard_map/finish/pallas_call | solution.py:469
  54.4 0.1 collective-permute-start.15
  54.5 1.0 %collective-permute-start.16 = (f32[8,128]{1,0:T(8,128)S(1)}, f32[8,128]{1,0:T(8,128)S(1)}, u32[]{:S(2)}, u32[]{:S(2)}) collective-permute-start(f32[8,128]{1,0:T(8,128)S(1)} %get-tuple-element.73.refs_0_), channel_id=1, source_target_pairs={{0,2},{1,3},{2,0},{3,1},{4,6},{5,7},{6,4},{7,5},{8,10},{9,11},{10,... | collective-permute-start | bytes 12296 | tf_op jit(solution)/shard_map/ppermute | solution.py:590
  55.5 0.8 %collective-permute-start.17 = (f32[8,128]{1,0:T(8,128)S(1)}, f32[8,128]{1,0:T(8,128)S(1)}, u32[]{:S(2)}, u32[]{:S(2)}) collective-permute-start(f32[8,128]{1,0:T(8,128)S(1)} %get-tuple-element.73.refs_0_), channel_id=1, source_target_pairs={{0,1},{1,0},{2,3},{3,2},{4,5},{5,4},{6,7},{7,6},{8,9},{9,8},{10,11... | collective-permute-start | bytes 12296 | tf_op jit(solution)/shard_map/ppermute | solution.py:590
  56.3 1.2 %collective-permute-done.15.refs_1_ = f32[8,128]{1,0:T(8,128)S(1)} collective-permute-done((f32[8,128]{1,0:T(8,128)S(1)}, f32[8,128]{1,0:T(8,128)S(1)}, u32[]{:S(2)}, u32[]{:S(2)}) %collective-permute-start.15) | collective-permute-done | bytes 4128 | tf_op jit(solution)/shard_map/ppermute | solution.py:590
  57.5 0.7 %collective-permute-done.16.refs_2_ = f32[8,128]{1,0:T(8,128)S(1)} collective-permute-done((f32[8,128]{1,0:T(8,128)S(1)}, f32[8,128]{1,0:T(8,128)S(1)}, u32[]{:S(2)}, u32[]{:S(2)}) %collective-permute-start.16) | collective-permute-done | bytes 4128 | tf_op jit(solution)/shard_map/ppermute | solution.py:590
  58.2 0.0 collective-permute-done.17.refs_3_
  58.2 1.1 %scale.1 = bf16[256,1536]{1,0:T(8,128)(2,1)} custom-call(f32[8,128]{1,0:T(8,128)S(1)} %get-tuple-element.73.refs_0_, f32[8,128]{1,0:T(8,128)S(1)} %collective-permute-done.15.refs_1_, f32[8,128]{1,0:T(8,128)S(1)} %collective-permute-done.16.refs_2_, f32[8,128]{1,0:T(8,128)S(1)} %collective-permute-done.17.refs_3_, f32[256,640]{1,0:T(8,128)S(1)} %get-tuple-element.74.refs_4_, ...), custom_call_target="tpu_custom_call" | custom-call | tf_op jit(solution)/shard_map/scale/pallas_call | solution.py:591
  (2 shorter events, 0.0 us)
Async XLA Ops:
  0.1 18.0 %copy-start = (bf16[16,1536]{1,0:T(8,128)(2,1)S(1)}, bf16[16,1536]{1,0:T(8,128)(2,1)}, u32[]{:S(2)}) copy-start(bf16[16,1536]{1,0:T(8,128)(2,1)} %gate_table.1) | copy-start | bytes 147460
  0.1 18.0 %copy-start.1 = (s32[2,4,4,4]{3,2,1,0:T(4,128)S(1)}, s32[2,4,4,4]{3,2,1,0:T(4,128)}, u32[]{:S(2)}) copy-start(s32[2,4,4,4]{3,2,1,0:T(4,128)} %ranges_ref.1) | copy-start | bytes 1540
  2.3 21.0 %collective-permute-start.7 = (bf16[256,1280]{1,0:T(8,128)(2,1)S(1)}, bf16[256,1280]{1,0:T(8,128)(2,1)S(1)}, u32[]{:S(2)}, u32[]{:S(2)}) collective-permute-start(bf16[256,1280]{1,0:T(8,128)(2,1)S(1)} %get-tuple-element.50), channel_id=1, source_target_pairs={{0,16},{16,0},{1,17},{17,1},{2,18},{18,2},{3,19},{19,3},{4,20},{20... | collective-permute-start | bytes 1966088 | tf_op jit(solution)/shard_map/ppermute | solution.py:30
  5.4 10.6 %collective-permute-start.3 = (bf16[256,640]{1,0:T(8,128)(2,1)S(1)}, bf16[256,640]{1,0:T(8,128)(2,1)S(1)}, u32[]{:S(2)}, u32[]{:S(2)}) collective-permute-start(bf16[256,640]{1,0:T(8,128)(2,1)S(1)} %get-tuple-element.48), channel_id=1, source_target_pairs={{0,4},{4,8},{8,12},{12,14},{14,10},{10,6},{6,2},{2,0},{1,5},{5,9},... | collective-permute-start | bytes 983048 | tf_op jit(solution)/shard_map/ppermute | solution.py:46
  6.9 10.7 %collective-permute-start.5 = (bf16[256,640]{1,0:T(8,128)(2,1)S(1)}, bf16[256,640]{1,0:T(8,128)(2,1)S(1)}, u32[]{:S(2)}, u32[]{:S(2)}) collective-permute-start(bf16[256,640]{1,0:T(8,128)(2,1)S(1)} %get-tuple-element.49), channel_id=1, source_target_pairs={{4,0},{8,4},{12,8},{14,12},{10,14},{6,10},{2,6},{0,2},{5,1},{9,5},... | collective-permute-start | bytes 983048 | tf_op jit(solution)/shard_map/ppermute | solution.py:46
  7.4 10.7 %copy-start.2 = (s32[4]{0:T(128)S(1)}, s32[4]{0:T(128)}, u32[]{:S(2)}) copy-start(s32[4]{0:T(128)} %levels_ref.1) | copy-start | bytes 52
  7.4 12.8 %collective-permute-start = (bf16[256,384]{1,0:T(8,128)(2,1)S(1)}, bf16[256,384]{1,0:T(8,128)(2,1)S(1)}, u32[]{:S(2)}, u32[]{:S(2)}) collective-permute-start(bf16[256,384]{1,0:T(8,128)(2,1)S(1)} %get-tuple-element.45), channel_id=1, source_target_pairs={{0,4},{4,8},{8,12},{12,14},{14,10},{10,6},{6,2},{2,0},{1,5},{5,9},... | collective-permute-start | bytes 589832 | tf_op jit(solution)/shard_map/ppermute | solution.py:46
  9.0 12.8 %collective-permute-start.1 = (bf16[256,384]{1,0:T(8,128)(2,1)S(1)}, bf16[256,384]{1,0:T(8,128)(2,1)S(1)}, u32[]{:S(2)}, u32[]{:S(2)}) collective-permute-start(bf16[256,384]{1,0:T(8,128)(2,1)S(1)} %get-tuple-element.46), channel_id=1, source_target_pairs={{4,0},{8,4},{12,8},{14,12},{10,14},{6,10},{2,6},{0,2},{5,1},{9,5},... | collective-permute-start | bytes 589832 | tf_op jit(solution)/shard_map/ppermute | solution.py:46
  16.0 11.2 %collective-permute-start.4 = (bf16[256,640]{1,0:T(8,128)(2,1)S(1)}, bf16[256,640]{1,0:T(8,128)(2,1)S(1)}, u32[]{:S(2)}, u32[]{:S(2)}) collective-permute-start(bf16[256,640]{1,0:T(8,128)(2,1)S(1)} %collective-permute-done.3.forward_q.rest_0_), channel_id=1, source_target_pairs={{0,4},{4,8},{8,12},{12,14},{14,10},{10,6},{6,2},{2,0},{1,5},{5,9},... | collective-permute-start | bytes 983048 | tf_op jit(solution)/shard_map/ppermute | solution.py:46
  17.6 11.2 %collective-permute-start.6 = (bf16[256,640]{1,0:T(8,128)(2,1)S(1)}, bf16[256,640]{1,0:T(8,128)(2,1)S(1)}, u32[]{:S(2)}, u32[]{:S(2)}) collective-permute-start(bf16[256,640]{1,0:T(8,128)(2,1)S(1)} %collective-permute-done.5.backward_q.rest_1_), channel_id=1, source_target_pairs={{4,0},{8,4},{12,8},{14,12},{10,14},{6,10},{2,6},{0,2},{5,1},{9,5},... | collective-permute-start | bytes 983048 | tf_op jit(solution)/shard_map/ppermute | solution.py:46
  20.2 12.2 %collective-permute-start.2 = (bf16[256,768]{1,0:T(8,128)(2,1)S(1)}, bf16[256,768]{1,0:T(8,128)(2,1)S(1)}, u32[]{:S(2)}, u32[]{:S(2)}) collective-permute-start(bf16[256,768]{1,0:T(8,128)(2,1)S(1)} %get-tuple-element.47), channel_id=1, source_target_pairs={{0,16},{16,0},{1,17},{17,1},{2,18},{18,2},{3,19},{19,3},{4,20},{20... | collective-permute-start | bytes 1179656 | tf_op jit(solution)/shard_map/ppermute | solution.py:30
  21.8 12.7 %collective-permute-start.8 = (bf16[256,384]{1,0:T(8,128)(2,1)S(1)}, bf16[256,384]{1,0:T(8,128)(2,1)S(1)}, u32[]{:S(2)}, u32[]{:S(2)}) collective-permute-start(bf16[256,384]{1,0:T(8,128)(2,1)S(1)} %collective-permute-done.forward_q.rest_2_), channel_id=1, source_target_pairs={{0,4},{4,8},{8,12},{12,14},{14,10},{10,6},{6,2},{2,0},{1,5},{5,9},... | collective-permute-start | bytes 589832 | tf_op jit(solution)/shard_map/ppermute | solution.py:46
  23.4 11.2 %collective-permute-start.9 = (bf16[256,384]{1,0:T(8,128)(2,1)S(1)}, bf16[256,384]{1,0:T(8,128)(2,1)S(1)}, u32[]{:S(2)}, u32[]{:S(2)}) collective-permute-start(bf16[256,384]{1,0:T(8,128)(2,1)S(1)} %collective-permute-done.1.backward_q.rest_3_), channel_id=1, source_target_pairs={{4,0},{8,4},{12,8},{14,12},{10,14},{6,10},{2,6},{0,2},{5,1},{9,5},... | collective-permute-start | bytes 589832 | tf_op jit(solution)/shard_map/ppermute | solution.py:46
  30.8 12.2 %collective-permute-start.11 = (bf16[272,640]{1,0:T(8,128)(2,1)S(1)}, bf16[272,640]{1,0:T(8,128)(2,1)S(1)}, u32[]{:S(2)}, u32[]{:S(2)}) collective-permute-start(bf16[272,640]{1,0:T(8,128)(2,1)S(1)} %get-tuple-element.60), channel_id=1, source_target_pairs={{0,4},{4,8},{8,12},{12,0},{1,5},{5,9},{9,13},{13,1},{2,6},{6,10},{... | collective-permute-start | bytes 1044488 | tf_op jit(solution)/shard_map/ppermute | solution.py:52
  36.2 11.2 %collective-permute-start.10 = (bf16[272,384]{1,0:T(8,128)(2,1)S(1)}, bf16[272,384]{1,0:T(8,128)(2,1)S(1)}, u32[]{:S(2)}, u32[]{:S(2)}) collective-permute-start(bf16[272,384]{1,0:T(8,128)(2,1)S(1)} %get-tuple-element.57), channel_id=1, source_target_pairs={{0,4},{4,8},{8,12},{12,0},{1,5},{5,9},{9,13},{13,1},{2,6},{6,10},{... | collective-permute-start | bytes 626696 | tf_op jit(solution)/shard_map/ppermute | solution.py:52
  41.3 8.0 %collective-permute-start.14 = (bf16[272,512]{1,0:T(8,128)(2,1)S(1)}, bf16[272,512]{1,0:T(8,128)(2,1)S(1)}, u32[]{:S(2)}, u32[]{:S(2)}) collective-permute-start(bf16[272,512]{1,0:T(8,128)(2,1)S(1)} %get-tuple-element.69), channel_id=1, source_target_pairs={{0,16},{16,0},{1,17},{17,1},{2,18},{18,2},{3,19},{19,3},{4,20},{20... | collective-permute-start | bytes 835592 | tf_op jit(solution)/shard_map/ppermute | solution.py:30
  43.7 9.1 %collective-permute-start.13 = (bf16[272,640]{1,0:T(8,128)(2,1)S(1)}, bf16[272,640]{1,0:T(8,128)(2,1)S(1)}, u32[]{:S(2)}, u32[]{:S(2)}) collective-permute-start(bf16[272,640]{1,0:T(8,128)(2,1)S(1)} %get-tuple-element.67), channel_id=1, source_target_pairs={{0,4},{4,8},{8,12},{12,0},{1,5},{5,9},{9,13},{13,1},{2,6},{6,10},{... | collective-permute-start | bytes 1044488 | tf_op jit(solution)/shard_map/ppermute | solution.py:52
  48.0 5.7 %collective-permute-start.12 = (bf16[272,384]{1,0:T(8,128)(2,1)S(1)}, bf16[272,384]{1,0:T(8,128)(2,1)S(1)}, u32[]{:S(2)}, u32[]{:S(2)}) collective-permute-start(bf16[272,384]{1,0:T(8,128)(2,1)S(1)} %get-tuple-element.64), channel_id=1, source_target_pairs={{0,4},{4,8},{8,12},{1,5},{5,9},{9,13},{2,6},{6,10},{10,14},{3,7},{... | collective-permute-start | bytes 626696 | tf_op jit(solution)/shard_map/ppermute | solution.py:52
  54.4 3.1 %collective-permute-start.15 = (f32[8,128]{1,0:T(8,128)S(1)}, f32[8,128]{1,0:T(8,128)S(1)}, u32[]{:S(2)}, u32[]{:S(2)}) collective-permute-start(f32[8,128]{1,0:T(8,128)S(1)} %get-tuple-element.73.refs_0_), channel_id=1, source_target_pairs={{0,3},{1,2},{2,1},{3,0},{4,7},{5,6},{6,5},{7,4},{8,11},{9,10},{10,... | collective-permute-start | bytes 12296 | tf_op jit(solution)/shard_map/ppermute | solution.py:590
  54.5 3.7 %collective-permute-start.16 = (f32[8,128]{1,0:T(8,128)S(1)}, f32[8,128]{1,0:T(8,128)S(1)}, u32[]{:S(2)}, u32[]{:S(2)}) collective-permute-start(f32[8,128]{1,0:T(8,128)S(1)} %get-tuple-element.73.refs_0_), channel_id=1, source_target_pairs={{0,2},{1,3},{2,0},{3,1},{4,6},{5,7},{6,4},{7,5},{8,10},{9,11},{10,... | collective-permute-start | bytes 12296 | tf_op jit(solution)/shard_map/ppermute | solution.py:590
  55.5 2.6 %collective-permute-start.17 = (f32[8,128]{1,0:T(8,128)S(1)}, f32[8,128]{1,0:T(8,128)S(1)}, u32[]{:S(2)}, u32[]{:S(2)}) collective-permute-start(f32[8,128]{1,0:T(8,128)S(1)} %get-tuple-element.73.refs_0_), channel_id=1, source_target_pairs={{0,1},{1,0},{2,3},{3,2},{4,5},{5,4},{6,7},{7,6},{8,9},{9,8},{10,11... | collective-permute-start | bytes 12296 | tf_op jit(solution)/shard_map/ppermute | solution.py:590
